TPU v7x, 32 devices: a whole 2x2x4 slice. The times are simulated.
32 devices in a mesh: section: 2 (over x), row: 8 (over z, core), col: 2 (over y).
Axes of the slice: x: 2, y: 2, z: 4, core: 2. Of those that a mesh axis runs over, the one named last changes fastest.
Arguments:
- inputs: bfloat16 [2, 4096, 768], P(None, ('row', 'col')), may hold values from -6 to 6
- cotangent: bfloat16 [2, 4096, 768], P(None, ('row', 'col')), may hold values from -6 to 6
- segments: int32 [2, 4096], P(None, ('row', 'col')), may hold values from 0 to 63, never falling along the last dimension, each value on 1 to 256 neighbouring positions
- routes: int32 [2, 2, 4096, 2], P('section', None, ('row', 'col')), may hold values from 0 to 31, all different within a row
- order: int32 [2, 2, 16, 256], P('section', None, ('row', 'col')), may hold values from 0 to 255, each once within a row
- attn_gain: bfloat16 [2, 768], P('section', ('row', 'col')), may hold values from 0.25 to 1.75
- qkv_weight: bfloat16 [2, 768, 2304], P('section', ('row', 'col')), may hold values from -0.21875 to 0.21875
- position_bias: bfloat16 [2, 384], P('section', ('row', 'col')), may hold values from -4 to 4
- out_weight: bfloat16 [2, 768, 768], P('section', ('row', 'col')), may hold values from -0.875 to 0.875
- moe_gain: bfloat16 [2, 768], P('section', ('row', 'col')), may hold values from 0.25 to 1.75
- router_weight: bfloat16 [2, 768, 32], P('section', ('row', 'col')), may hold values from -0.15625 to 0.15625
- expert_in: bfloat16 [2, 32, 768, 3072], P('section', 'row', None, 'col'), may hold values from -0.21875 to 0.21875
- expert_out: bfloat16 [2, 32, 3072, 768], P('section', 'row', 'col'), may hold values from -0.109375 to 0.109375
Outputs:
- layer_out: bfloat16 [2, 2, 4096, 768], P('section', None, ('row', 'col'))
- layer_in_grad: float32 [2, 2, 4096, 768], P('section', None, ('row', 'col'))
- attn_gain_grad: float32 [2, 768], P('section', ('row', 'col'))
- qkv_grad: float32 [2, 768, 2304], P('section', ('row', 'col'))
- bias_grad: float32 [2, 384], P('section', ('row', 'col'))
- out_grad: float32 [2, 768, 768], P('section', ('row', 'col'))
- moe_gain_grad: float32 [2, 768], P('section', ('row', 'col'))
- router_grad: float32 [2, 768, 32], P('section', ('row', 'col'))
- expert_in_grad: float32 [2, 32, 768, 3072], P('section', 'row', None, 'col')
- expert_out_grad: float32 [2, 32, 3072, 768], P('section', 'row', 'col')
Inputs may be any that keep to these rules, and one draw needn't show every extreme that they name: `segments`: numbers never fall along a micro-batch; a document has at most 256 tokens. `routes`: A token names 2 different experts. `order`: each aligned block of 256 entries holds every value once.
All inputs are finite; a program needn't handle non-finite values.
Results may differ from a plain program's by a relative error of at most 0.024.
Values may be sent and summed in bfloat16 or wider, within the bound.
A program may use at most 320 MiB of HBM per device.

v0:
```python
from functools import partial
import math

import jax
import jax.numpy as jnp
from jax import lax
from jax.sharding import PartitionSpec as P

TOP = 2
DISTANCE_BUCKETS = 32
MAX_DIST = 128


EPS = 1e-06
FULL_PRECISION = lax.Precision.HIGHEST


def shifted(value, axis, steps):
    count = lax.axis_size(axis)
    first, last = (max(0, -steps), min(count, count - steps))
    return lax.ppermute(value, axis, [(source, source + steps) for source in range(first, last)])


def thresholds():
    half_count = DISTANCE_BUCKETS // 2
    limits = []
    for level_index in range(1, DISTANCE_BUCKETS):
        if level_index < half_count:
            limits.append(level_index)
        else:
            ratio = (level_index - half_count) / half_count
            limits.append(int(math.ceil(half_count * (MAX_DIST / half_count) ** ratio)))
    return limits


def bucket_onehot(length):
    positions = jnp.arange(length, dtype=jnp.int32)
    distance = positions[:, None] - positions[None, :]
    bucket = jnp.zeros((length, length), jnp.int32)
    for threshold in thresholds():
        bucket = bucket + (distance >= threshold).astype(jnp.int32)
    levels = jnp.arange(DISTANCE_BUCKETS, dtype=jnp.int32)
    return (bucket[None, :, :] == levels[:, None, None]).astype(jnp.float32)


def matmul(left_side, right_side):
    return jnp.dot(left_side, right_side, preferred_element_type=jnp.float32)


def norm_apply(values, gain_vector):
    factor = lax.rsqrt(jnp.mean(values * values, axis=-1, keepdims=True) + EPS)
    return values * factor * gain_vector


def gate_values(logits, routing):
    probabilities = jax.nn.softmax(logits, axis=-1)
    levels = jnp.arange(logits.shape[1], dtype=jnp.int32)
    pick_table = (routing[:, :, None] == levels[None, None, :]).astype(jnp.float32)
    chosen = jnp.sum(probabilities[:, None, :] * pick_table, axis=2)
    return chosen / jnp.sum(chosen, axis=1, keepdims=True)


def place_pairs(routing, priority, capacity, experts_all):
    length = routing.shape[0]
    pick_rank = jnp.arange(TOP, dtype=jnp.int32)
    pair_keys = (pick_rank[None, :] * length + priority[:, None]).reshape(-1)
    pair_experts = routing.reshape(-1)
    earlier = (pair_experts[:, None] == pair_experts[None, :]) & (
        pair_keys[None, :] < pair_keys[:, None]
    )
    slot_rank = jnp.sum(earlier.astype(jnp.int32), axis=1)
    return jnp.where(
        slot_rank < capacity, pair_experts * capacity + slot_rank, experts_all * capacity
    )


def attention_mask(segment):
    positions = jnp.arange(segment.shape[0], dtype=jnp.int32)
    return (positions[None, :] <= positions[:, None]) & (segment[None, :] == segment[:, None])


def score_block(queries, key_rows, relative_position_bias, allowed):
    scale = 1.0 / math.sqrt(queries.shape[2])
    raw_scores = (
        jnp.einsum("qhd,khd->hqk", queries, key_rows, preferred_element_type=jnp.float32) * scale
        + relative_position_bias
    )
    return jnp.where(allowed[None], raw_scores, -1e30)


def split_heads(qkv_rows, head_count):
    length = qkv_rows.shape[0]
    model_width = qkv_rows.shape[1] // 3
    size_head = model_width // head_count
    queries = qkv_rows[:, :model_width].reshape(length, head_count, size_head)
    key_rows = qkv_rows[:, model_width : 2 * model_width].reshape(length, head_count, size_head)
    value_rows = qkv_rows[:, 2 * model_width :].reshape(length, head_count, size_head)
    return (queries, key_rows, value_rows)


def layer_forward(stream, segment, routing, priority, params, capacity, experts_all):
    gain_one, qkv_w, relative_position_bias, out_w, gain_two, router_w, w_in, w_out = params
    length, model_width = stream.shape
    head_count = relative_position_bias.shape[0]
    row_count = lax.axis_size("row")
    local_experts = w_in.shape[0]
    normed_one = norm_apply(stream, gain_one).astype(jnp.bfloat16)
    qkv_rows = matmul(normed_one, qkv_w).astype(jnp.bfloat16)
    queries, key_rows, value_rows = split_heads(qkv_rows, head_count)
    allowed = attention_mask(segment)
    scores = score_block(queries, key_rows, relative_position_bias, allowed)
    top_score = jnp.max(scores, axis=-1, keepdims=True)
    exponent = jnp.exp(scores - top_score)
    row_total = jnp.sum(exponent, axis=-1, keepdims=True)
    attention = (exponent / row_total).astype(jnp.bfloat16)
    log_total = top_score + jnp.log(row_total)
    context = jnp.einsum("hqk,khd->qhd", attention, value_rows, preferred_element_type=jnp.float32)
    context = context.reshape(length, model_width).astype(jnp.bfloat16)
    residual = stream + matmul(context, out_w)
    moe_in = norm_apply(residual, gain_two).astype(jnp.bfloat16)
    logits = matmul(moe_in, router_w)
    gate_share = gate_values(logits, routing)
    slot_index = place_pairs(routing, priority, capacity, experts_all)
    slot_rows = (
        jnp.zeros((experts_all * capacity + 1, model_width), jnp.bfloat16)
        .at[slot_index]
        .set(jnp.repeat(moe_in, TOP, axis=0))
    )
    blocks = slot_rows[: experts_all * capacity].reshape(
        row_count, local_experts, capacity, model_width
    )
    arrived = lax.all_to_all(blocks, "row", split_axis=0, concat_axis=2, tiled=True).reshape(
        local_experts, row_count * capacity, model_width
    )
    owner_rows = lax.all_gather(arrived, "col", axis=1, tiled=True)
    hidden_pre = jnp.einsum("erd,edf->erf", owner_rows, w_in, preferred_element_type=jnp.float32)
    hidden = jax.nn.gelu(hidden_pre, approximate=False).astype(jnp.bfloat16)
    produced = jnp.einsum("erf,efd->erd", hidden, w_out, preferred_element_type=jnp.float32)
    returned = lax.psum_scatter(produced, "col", scatter_dimension=1, tiled=True).astype(
        jnp.bfloat16
    )
    home_rows = lax.all_to_all(
        returned.reshape(1, local_experts, row_count * capacity, model_width),
        "row",
        split_axis=2,
        concat_axis=0,
        tiled=True,
    )
    flat_rows = jnp.concatenate(
        [
            home_rows.reshape(experts_all * capacity, model_width),
            jnp.zeros((1, model_width), jnp.bfloat16),
        ],
        axis=0,
    )
    picked = flat_rows[slot_index].reshape(length, TOP, model_width).astype(jnp.float32)
    result = residual + jnp.sum(gate_share[:, :, None] * picked, axis=1)
    stored_tick = (
        stream,
        normed_one,
        qkv_rows,
        allowed,
        log_total,
        context,
        residual,
        moe_in,
        logits,
        gate_share,
        slot_index,
        picked,
        owner_rows,
        hidden_pre,
        hidden,
        routing,
    )
    return (result, stored_tick)


def layer_backward(incoming, stored_tick, params, capacity, experts_all):
    gain_one, qkv_w, relative_position_bias, out_w, gain_two, router_w, w_in, w_out = params
    (
        stream,
        normed_one,
        qkv_rows,
        allowed,
        log_total,
        context,
        residual,
        moe_in,
        logits,
        gate_share,
        slot_index,
        picked,
        owner_rows,
        hidden_pre,
        hidden,
        routing,
    ) = stored_tick
    length, model_width = stream.shape
    head_count = relative_position_bias.shape[0]
    row_count = lax.axis_size("row")
    local_experts = w_in.shape[0]
    gate_grad = jnp.sum(picked * incoming[:, None, :], axis=2)
    spread = (gate_share[:, :, None] * incoming[:, None, :]).reshape(length * TOP, model_width)
    slot_grad = (
        jnp.zeros((experts_all * capacity + 1, model_width), jnp.float32).at[slot_index].add(spread)
    )
    slot_grad = (
        slot_grad[: experts_all * capacity]
        .astype(jnp.bfloat16)
        .reshape(row_count, local_experts, capacity, model_width)
    )
    owner_grad = lax.all_to_all(slot_grad, "row", split_axis=0, concat_axis=2, tiled=True).reshape(
        local_experts, row_count * capacity, model_width
    )
    seen_grad = lax.all_gather(owner_grad, "col", axis=1, tiled=True)
    w_out_grad = jnp.einsum("erf,erd->efd", hidden, seen_grad, preferred_element_type=jnp.float32)
    hidden_grad = jnp.einsum("erd,efd->erf", seen_grad, w_out, preferred_element_type=jnp.float32)
    gelu_value, gelu_pull = jax.vjp(partial(jax.nn.gelu, approximate=False), hidden_pre)
    pre_grad = gelu_pull(hidden_grad)[0].astype(jnp.bfloat16)
    w_in_grad = jnp.einsum("erd,erf->edf", owner_rows, pre_grad, preferred_element_type=jnp.float32)
    row_grad = jnp.einsum("erf,edf->erd", pre_grad, w_in, preferred_element_type=jnp.float32)
    sent_grad = lax.psum_scatter(
        row_grad.astype(jnp.bfloat16), "col", scatter_dimension=1, tiled=True
    )
    home_grad = lax.all_to_all(
        sent_grad.reshape(1, local_experts, row_count * capacity, model_width),
        "row",
        split_axis=2,
        concat_axis=0,
        tiled=True,
    )
    flat_grad = jnp.concatenate(
        [
            home_grad.reshape(experts_all * capacity, model_width),
            jnp.zeros((1, model_width), jnp.bfloat16),
        ],
        axis=0,
    )
    moe_grad = jnp.sum(
        flat_grad[slot_index].reshape(length, TOP, model_width).astype(jnp.float32), axis=1
    )

    def gate_of_logits(raw_logits):
        return gate_values(raw_logits, routing)

    gate_value, gate_pull = jax.vjp(gate_of_logits, logits)
    logit_grad = gate_pull(gate_grad)[0].astype(jnp.bfloat16)
    router_grad = matmul(moe_in.T, logit_grad)
    moe_grad = moe_grad + matmul(logit_grad, router_w.T)
    norm_value, norm_pull = jax.vjp(norm_apply, residual, gain_two)
    residual_part, gain_two_grad = norm_pull(moe_grad)
    residual_grad = incoming + residual_part
    branch_grad = residual_grad.astype(jnp.bfloat16)
    out_grad = matmul(context.T, branch_grad)
    size_head = model_width // head_count
    context_grad = (
        matmul(branch_grad, out_w.T).astype(jnp.bfloat16).reshape(length, head_count, size_head)
    )
    queries, key_rows, value_rows = split_heads(qkv_rows, head_count)
    scores = score_block(queries, key_rows, relative_position_bias, allowed)
    softmax_rows = jnp.exp(scores - log_total)
    attention = softmax_rows.astype(jnp.bfloat16)
    value_grad = jnp.einsum(
        "hqk,qhd->khd", attention, context_grad, preferred_element_type=jnp.float32
    )
    prob_grad = jnp.einsum(
        "qhd,khd->hqk", context_grad, value_rows, preferred_element_type=jnp.float32
    )
    row_shift = jnp.sum(softmax_rows * prob_grad, axis=-1, keepdims=True)
    score_grad = (softmax_rows * (prob_grad - row_shift)).astype(jnp.bfloat16)
    scale = 1.0 / math.sqrt(size_head)
    query_grad = (
        jnp.einsum("hqk,khd->qhd", score_grad, key_rows, preferred_element_type=jnp.float32) * scale
    )
    key_grad = (
        jnp.einsum("hqk,qhd->khd", score_grad, queries, preferred_element_type=jnp.float32) * scale
    )
    qkv_grad_rows = jnp.concatenate(
        [
            query_grad.reshape(length, model_width),
            key_grad.reshape(length, model_width),
            value_grad.reshape(length, model_width),
        ],
        axis=1,
    ).astype(jnp.bfloat16)
    qkv_w_grad = matmul(normed_one.T, qkv_grad_rows)
    normed_grad = matmul(qkv_grad_rows, qkv_w.T)
    first_norm, first_pull = jax.vjp(norm_apply, stream, gain_one)
    stream_part, gain_one_grad = first_pull(normed_grad)
    stream_grad = residual_grad + stream_part
    grads = (
        gain_one_grad,
        qkv_w_grad,
        score_grad.astype(jnp.float32),
        out_grad,
        gain_two_grad,
        router_grad,
        w_in_grad,
        w_out_grad,
    )
    return (stream_grad, grads)


def on_device(
    inputs,
    cotangent,
    segments,
    routes,
    order,
    attn_gain,
    qkv_weight,
    position_bias,
    out_weight,
    moe_gain,
    router_weight,
    expert_in,
    expert_out,
):
    micro_count = inputs.shape[0]
    length = inputs.shape[1]
    model_width = inputs.shape[2]
    local_experts = expert_in.shape[1]
    experts_all = local_experts * lax.axis_size("row")
    capacity = max(2, (5 * length * TOP + 4 * experts_all - 1) // (4 * experts_all))
    first_section = lax.axis_index("section") == 0
    gathered = (
        lax.all_gather(attn_gain, ("row", "col"), axis=1, tiled=True),
        lax.all_gather(qkv_weight, ("row", "col"), axis=1, tiled=True),
        lax.all_gather(position_bias, ("row", "col"), axis=1, tiled=True),
        lax.all_gather(out_weight, ("row", "col"), axis=1, tiled=True),
        lax.all_gather(moe_gain, ("row", "col"), axis=1, tiled=True),
        lax.all_gather(router_weight, ("row", "col"), axis=1, tiled=True),
    )
    gain_one = gathered[0][0].astype(jnp.float32)
    qkv_w = gathered[1][0]
    relative_bias_matrix = gathered[2][0].astype(jnp.float32).reshape(DISTANCE_BUCKETS, -1)
    out_w = gathered[3][0]
    gain_two = gathered[4][0].astype(jnp.float32)
    router_w = gathered[5][0]
    bucket_indicator = bucket_onehot(length)
    relative_position_bias = jnp.einsum(
        "rgx,rn->ngx", bucket_indicator, relative_bias_matrix, precision=FULL_PRECISION
    )
    w_in = expert_in[0]
    w_out = expert_out[0]
    params = (gain_one, qkv_w, relative_position_bias, out_w, gain_two, router_w, w_in, w_out)
    received = jnp.zeros((length, model_width), jnp.float32)
    stored = []
    outputs = []
    for tick_index in range(micro_count + 1):
        own_micro = min(tick_index, micro_count - 1)
        later_micro = max(tick_index - 1, 0)
        stream = jnp.where(first_section, inputs[own_micro].astype(jnp.float32), received)
        micro_index = jnp.where(first_section, own_micro, later_micro).astype(jnp.int32)
        segment = lax.dynamic_index_in_dim(segments, micro_index, 0, False)
        routing = lax.dynamic_index_in_dim(routes[0], micro_index, 0, False)
        priority = lax.dynamic_index_in_dim(order[0], micro_index, 0, False)[0]
        result, stored_tick = layer_forward(
            stream, segment, routing, priority, params, capacity, experts_all
        )
        stored.append(stored_tick)
        outputs.append(result)
        if tick_index < micro_count:
            received = shifted(result.astype(jnp.bfloat16), "section", 1).astype(jnp.float32)
    bucket_sums = (
        jnp.zeros((model_width,), jnp.float32),
        jnp.zeros(qkv_w.shape, jnp.float32),
        jnp.zeros(relative_position_bias.shape, jnp.float32),
        jnp.zeros(out_w.shape, jnp.float32),
        jnp.zeros((model_width,), jnp.float32),
        jnp.zeros(router_w.shape, jnp.float32),
        jnp.zeros(w_in.shape, jnp.float32),
        jnp.zeros(w_out.shape, jnp.float32),
    )
    sent_back = jnp.zeros((length, model_width), jnp.float32)
    in_grads = []
    for step_index in range(micro_count + 1):
        tick_index = micro_count - step_index
        last_micro = max(micro_count - 1 - step_index, 0)
        active = jnp.where(first_section, step_index >= 1, step_index <= micro_count - 1).astype(
            jnp.float32
        )
        incoming = (
            jnp.where(first_section, sent_back, cotangent[last_micro].astype(jnp.float32)) * active
        )
        stream_grad, grads = layer_backward(
            incoming, stored[tick_index], params, capacity, experts_all
        )
        bucket_sums = jax.tree.map(jnp.add, bucket_sums, grads)
        in_grads.append(stream_grad)
        if step_index < micro_count:
            sent_back = shifted(stream_grad.astype(jnp.bfloat16), "section", -1).astype(jnp.float32)
    layer_out = jnp.stack(
        [
            jnp.where(first_section, outputs[place], outputs[place + 1])
            for place in range(micro_count)
        ]
    ).astype(jnp.bfloat16)
    layer_in_grad = jnp.stack(
        [
            jnp.where(
                first_section, in_grads[micro_count - place], in_grads[micro_count - 1 - place]
            )
            for place in range(micro_count)
        ]
    )
    bias_matrix_gradient = jnp.einsum(
        "mxi,oxi->mo", bucket_indicator, bucket_sums[2], precision=FULL_PRECISION
    ).reshape(-1)
    dense_grads = (
        lax.psum_scatter(bucket_sums[0], ("row", "col"), scatter_dimension=0, tiled=True),
        lax.psum_scatter(bucket_sums[1], ("row", "col"), scatter_dimension=0, tiled=True),
        lax.psum_scatter(bias_matrix_gradient, ("row", "col"), scatter_dimension=0, tiled=True),
        lax.psum_scatter(bucket_sums[3], ("row", "col"), scatter_dimension=0, tiled=True),
        lax.psum_scatter(bucket_sums[4], ("row", "col"), scatter_dimension=0, tiled=True),
        lax.psum_scatter(bucket_sums[5], ("row", "col"), scatter_dimension=0, tiled=True),
    )
    in_weight_grad = bucket_sums[6][None]
    out_weight_grad = bucket_sums[7][None]
    return (
        layer_out[None],
        layer_in_grad[None],
        dense_grads[0][None],
        dense_grads[1][None],
        dense_grads[2][None],
        dense_grads[3][None],
        dense_grads[4][None],
        dense_grads[5][None],
        in_weight_grad,
        out_weight_grad,
    )


def solution(mesh):
    return jax.shard_map(
        on_device,
        mesh=mesh,
        in_specs=(
            P(None, ("row", "col"), None),
            P(None, ("row", "col"), None),
            P(None, ("row", "col")),
            P("section", None, ("row", "col"), None),
            P("section", None, ("row", "col"), None),
            P("section", ("row", "col")),
            P("section", ("row", "col"), None),
            P("section", ("row", "col")),
            P("section", ("row", "col"), None),
            P("section", ("row", "col")),
            P("section", ("row", "col"), None),
            P("section", "row", None, "col"),
            P("section", "row", "col", None),
        ),
        out_specs=(
            P("section", None, ("row", "col"), None),
            P("section", None, ("row", "col"), None),
            P("section", ("row", "col")),
            P("section", ("row", "col"), None),
            P("section", ("row", "col")),
            P("section", ("row", "col"), None),
            P("section", ("row", "col")),
            P("section", ("row", "col"), None),
            P("section", "row", None, "col"),
            P("section", "row", "col", None),
        ),
        check_vma=False,
    )
```

profile of v0, /device:TPU:0, one launch (start us, length us, event | category | flops | bytes accessed | tf_op | source)
XLA Modules:
  0.0 1455.4 jit_solution(17369587039206394839)
XLA Ops:
  14.3 36.2 %all-reduce.13 = (bf16[768]{0:T(1024)(128)(2,1)S(1)}, bf16[384]{0:T(512)(128)(2,1)S(1)}, bf16[768]{0:T(1024)(128)(2,1)S(1)}) all-reduce(bf16[768]{0:T(1024)(128)(2,1)S(1)} %dynamic-update-slice, bf16[384]{0:T(512)(128)(2,1)S(1)} %dynamic-update-slice.1, ...), channel_id=1, replica_groups=mesh['section'=2,'row'=8,'col'=2] {'row','col'}, use_global_device_ids=true, to_apply=%add.6 | all-reduce | flops 1920 | bytes 7680
  51.8 11.6 copy.352
  110.9 28.5 %all_to_all.180 = bf16[8,4,20,768]{3,1,2,0:T(4,128)(2,1)S(1)} all-to-all(bf16[8,4,20,768]{3,1,2,0:T(4,128)(2,1)S(1)} %copy.360), channel_id=1, replica_groups=mesh['section'=2,'row'=8,'col'=2] {'row'}, dimensions={0} | all-to-all | bytes 1966080 | tf_op jit(solution)/shard_map/all_to_all | solution.py:132
  140.5 29.7 %all-gather.13.cloned.1.call-done = bf16[4,320,768]{2,1,0:T(8,128)(2,1)} async-done(((bf16[4,160,768]{2,1,0:T(8,128)(2,1)}), bf16[4,320,768]{2,1,0:T(8,128)(2,1)}) %all-gather.13.cloned.1.call-update) | async-done | bytes 1966096 | tf_op jit(solution)/shard_map/all_gather | solution.py:135
  179.2 18.5 %multiply_convert_fusion.2 = (bf16[4,320,1536]{2,1,0:T(8,128)(2,1)S(1)}, f32[4,320,1536]{2,1,0:T(8,128)}) fusion(f32[4,320,1536]{2,1,0:T(8,128)S(1)} %get-tuple-element.92, u8[320,1536]{1,0:T(8,128)(4,1)S(1)} %get-tuple-element.15, u8[320,1536]{1,0:T(8,128)(4,1)S(1)} %get-tuple-element.14), kind=kLoop, calls=%fused_computation.87 | loop fusion | flops 137625600 | bytes 20643840 | tf_op jit(solution)/shard_map/convert_element_type | solution.py:137
  204.8 52.1 %reduce-scatter.12.cloned.1.call-done = f32[4,160,768]{2,1,0:T(8,128)} async-done(((f32[4,320,768]{2,1,0:T(8,128)}), f32[4,160,768]{2,1,0:T(8,128)}) %reduce-scatter.12.cloned.1.call-update) | async-done | bytes 1966096 | tf_op jit(solution)/shard_map/reduce_scatter | solution.py:139
  265.0 45.7 %all_gather.41 = bf16[1,768,32]{2,0,1:T(2,128)(2,1)S(1)} all-gather(bf16[1,48,32]{2,0,1:T(2,128)(2,1)S(1)} %copy.355), channel_id=1, replica_groups=mesh['section'=2,'row'=8,'col'=2] {'row','col'}, dimensions={1}, use_global_device_ids=true | all-gather | bytes 52224 | tf_op jit(solution)/shard_map/all_gather | solution.py:333
  357.4 29.9 %all_to_all.181 = bf16[8,4,20,768]{3,1,2,0:T(4,128)(2,1)S(1)} all-to-all(bf16[8,4,20,768]{3,1,2,0:T(4,128)(2,1)S(1)} %copy.372), channel_id=1, replica_groups=mesh['section'=2,'row'=8,'col'=2] {'row'}, dimensions={0} | all-to-all | bytes 1966080 | tf_op jit(solution)/shard_map/all_to_all | solution.py:132
  388.4 30.7 %all-gather.15.cloned.1.call-done = bf16[4,320,768]{2,1,0:T(8,128)(2,1)} async-done(((bf16[4,160,768]{2,1,0:T(8,128)(2,1)}), bf16[4,320,768]{2,1,0:T(8,128)(2,1)}) %all-gather.15.cloned.1.call-update) | async-done | bytes 1966096 | tf_op jit(solution)/shard_map/all_gather | solution.py:135
  427.9 18.5 %multiply_convert_fusion.1 = (bf16[4,320,1536]{2,1,0:T(8,128)(2,1)S(1)}, f32[4,320,1536]{2,1,0:T(8,128)}) fusion(f32[4,320,1536]{2,1,0:T(8,128)S(1)} %get-tuple-element.99, u8[320,1536]{1,0:T(8,128)(4,1)S(1)} %get-tuple-element.13, u8[320,1536]{1,0:T(8,128)(4,1)S(1)} %get-tuple-element.12), kind=kLoop, calls=%fused_computation.74 | loop fusion | flops 137625600 | bytes 20643840 | tf_op jit(solution)/shard_map/convert_element_type | solution.py:137
  453.5 52.1 %reduce-scatter.14.cloned.1.call-done = f32[4,160,768]{2,1,0:T(8,128)} async-done(((f32[4,320,768]{2,1,0:T(8,128)}), f32[4,160,768]{2,1,0:T(8,128)}) %reduce-scatter.14.cloned.1.call-update) | async-done | bytes 1966096 | tf_op jit(solution)/shard_map/reduce_scatter | solution.py:139
  516.0 22.9 %all-to-all-done.3 = bf16[1,4,160,768]{3,1,0,2:T(4,128)(2,1)S(1)} async-done(((bf16[1,4,160,768]{3,1,0,2:T(4,128)(2,1)}), bf16[1,4,160,768]{3,1,0,2:T(4,128)(2,1)S(1)}, u32[]{:S(2)}, u32[]{:S(2)}) %all-to-all-start.3) | async-done | bytes 983072 | tf_op jit(solution)/shard_map/all_to_all | solution.py:142
  601.4 16.6 %all-to-all-done.4 = bf16[8,4,20,768]{3,1,2,0:T(4,128)(2,1)} async-done(((bf16[8,4,20,768]{3,1,2,0:T(4,128)(2,1)}), bf16[8,4,20,768]{3,1,2,0:T(4,128)(2,1)}, u32[]{:S(2)}, u32[]{:S(2)}) %all-to-all-start.4) | async-done | bytes 983072 | tf_op jit(solution)/shard_map/all_to_all | solution.py:132
  634.2 27.6 %all_to_all.182 = bf16[8,4,20,768]{3,1,2,0:T(4,128)(2,1)S(1)} all-to-all(bf16[8,4,20,768]{3,1,2,0:T(4,128)(2,1)S(1)} %copy.389), channel_id=1, replica_groups=mesh['section'=2,'row'=8,'col'=2] {'row'}, dimensions={0} | all-to-all | bytes 1966080 | tf_op jit(solution)/shard_map/all_to_all | solution.py:213
  675.1 18.8 %multiply_convert_fusion = (bf16[4,320,1536]{2,1,0:T(8,128)(2,1)}, f32[4,320,1536]{2,1,0:T(8,128)}) fusion(f32[4,320,1536]{2,1,0:T(8,128)S(1)} %get-tuple-element.106, u8[320,1536]{1,0:T(8,128)(4,1)S(1)} %get-tuple-element.11, u8[320,1536]{1,0:T(8,128)(4,1)S(1)} %get-tuple-element.10), kind=kLoop, calls=%fused_computation.61 | loop fusion | flops 137625600 | bytes 20643840 | tf_op jit(solution)/shard_map/convert_element_type | solution.py:137
  693.8 11.2 add_convert_fusion.2
  728.1 20.3 %reduce-scatter.18.cloned.1.call-done = bf16[4,160,768]{2,1,0:T(8,128)(2,1)} async-done(((bf16[4,320,768]{2,1,0:T(8,128)(2,1)}), bf16[4,160,768]{2,1,0:T(8,128)(2,1)}) %reduce-scatter.18.cloned.1.call-update) | async-done | bytes 983056 | tf_op jit(solution)/shard_map/reduce_scatter | solution.py:223
  756.3 46.3 %reduce-scatter.16.cloned.1.call-done = f32[4,160,768]{2,1,0:T(8,128)} async-done(((f32[4,320,768]{2,1,0:T(8,128)}), f32[4,160,768]{2,1,0:T(8,128)}) %reduce-scatter.16.cloned.1.call-update) | async-done | bytes 1966096 | tf_op jit(solution)/shard_map/reduce_scatter | solution.py:139
  897.4 28.1 %all_to_all.183 = bf16[8,4,20,768]{3,1,2,0:T(4,128)(2,1)S(1)} all-to-all(bf16[8,4,20,768]{3,1,2,0:T(4,128)(2,1)S(1)} %copy.400), channel_id=1, replica_groups=mesh['section'=2,'row'=8,'col'=2] {'row'}, dimensions={0} | all-to-all | bytes 1966080 | tf_op jit(solution)/shard_map/all_to_all | solution.py:213
  926.6 28.8 %all-gather.21.cloned.1.call-done = bf16[4,320,768]{2,1,0:T(8,128)(2,1)} async-done(((bf16[4,160,768]{2,1,0:T(8,128)(2,1)}), bf16[4,320,768]{2,1,0:T(8,128)(2,1)}) %all-gather.21.cloned.1.call-update) | async-done | bytes 1966096 | tf_op jit(solution)/shard_map/all_gather | solution.py:216
  955.4 11.2 add_convert_fusion.1
  979.7 30.5 %reduce-scatter.20.cloned.1.call-done = bf16[4,160,768]{2,1,0:T(8,128)(2,1)} async-done(((bf16[4,320,768]{2,1,0:T(8,128)(2,1)}), bf16[4,160,768]{2,1,0:T(8,128)(2,1)}) %reduce-scatter.20.cloned.1.call-update) | async-done | bytes 983056 | tf_op jit(solution)/shard_map/reduce_scatter | solution.py:223
  1019.6 23.3 %all-to-all-done.9 = bf16[1,4,160,768]{3,1,0,2:T(4,128)(2,1)S(1)} async-done(((bf16[1,4,160,768]{3,1,0,2:T(4,128)(2,1)}), bf16[1,4,160,768]{3,1,0,2:T(4,128)(2,1)S(1)}, u32[]{:S(2)}, u32[]{:S(2)}) %all-to-all-start.9) | async-done | bytes 983072 | tf_op jit(solution)/shard_map/all_to_all | solution.py:226
  1091.6 28.0 %all_to_all.184 = bf16[8,4,20,768]{3,1,2,0:T(4,128)(2,1)S(1)} all-to-all(bf16[8,4,20,768]{3,1,2,0:T(4,128)(2,1)S(1)} %copy.411), channel_id=1, replica_groups=mesh['section'=2,'row'=8,'col'=2] {'row'}, dimensions={0} | all-to-all | bytes 1966080 | tf_op jit(solution)/shard_map/all_to_all | solution.py:213
  1120.7 28.8 %all-gather.23.cloned.1.call-done = bf16[4,320,768]{2,1,0:T(8,128)(2,1)} async-done(((bf16[4,160,768]{2,1,0:T(8,128)(2,1)}), bf16[4,320,768]{2,1,0:T(8,128)(2,1)}) %all-gather.23.cloned.1.call-update) | async-done | bytes 1966096 | tf_op jit(solution)/shard_map/all_gather | solution.py:216
  1162.6 11.2 fusion.77
  1177.5 26.8 %reduce-scatter.22.cloned.1.call-done = bf16[4,160,768]{2,1,0:T(8,128)(2,1)} async-done(((bf16[4,320,768]{2,1,0:T(8,128)(2,1)}), bf16[4,160,768]{2,1,0:T(8,128)(2,1)}) %reduce-scatter.22.cloned.1.call-update) | async-done | bytes 983056 | tf_op jit(solution)/shard_map/reduce_scatter | solution.py:223
  1217.9 19.3 %all-to-all-done.11 = bf16[1,4,160,768]{3,1,0,2:T(4,128)(2,1)} async-done(((bf16[1,4,160,768]{3,1,0,2:T(4,128)(2,1)}), bf16[1,4,160,768]{3,1,0,2:T(4,128)(2,1)}, u32[]{:S(2)}, u32[]{:S(2)}) %all-to-all-start.11) | async-done | bytes 983072 | tf_op jit(solution)/shard_map/all_to_all | solution.py:226
  1278.6 12.2 fusion.256
  1322.5 22.2 %add_bitcast_fusion.1 = f32[1,4,768,1536]{3,2,1,0:T(8,128)} fusion(f32[4,768,1536]{2,1,0:T(8,128)} %fusion.256, f32[4,768,1536]{2,1,0:T(8,128)} %fusion.257, bf16[4,320,768]{2,1,0:T(8,128)(2,1)S(1)} %copy-done.93, bf16[4,320,1536]{2,1,0:T(8,128)(2,1)} %copy-done.65), kind=kOutput, calls=%fused_computation.13 | convolution fusion | flops 3029336064 | bytes 62521344 | tf_op jit(solution)/shard_map/erd,erf->edf/dot_general | solution.py:221
  1344.7 25.8 %add_bitcast_fusion = f32[1,4,1536,768]{3,2,1,0:T(8,128)} fusion(f32[4,1536,768]{2,1,0:T(8,128)} %fusion.258, f32[4,1536,768]{2,1,0:T(8,128)} %fusion.259, bf16[4,320,1536]{2,1,0:T(8,128)(2,1)} %copy-done.22, bf16[4,320,768]{2,1,0:T(8,128)(2,1)} %all-gather.23.cloned.1.call-done), kind=kOutput, calls=%fused_computation.12 | convolution fusion | flops 3029336064 | bytes 62521344 | tf_op jit(solution)/shard_map/erf,erd->efd/dot_general | solution.py:217
  1383.6 60.5 %all-reduce.12 = (f32[768]{0:T(1024)S(1)}, f32[384]{0:T(512)S(1)}, f32[768]{0:T(1024)S(1)}) all-reduce(f32[768]{0:T(1024)S(1)} %add_add_fusion.9, f32[384]{0:T(512)} %reshape.1138, f32[768]{0:T(1024)S(1)} %add_add_fusion.8), channel_id=8, replica_groups=mesh['section'=2,'row'=8,'col'=2] {'row','col'}, use_global_device_ids=true, to_apply=%region_69.70.clone | all-reduce | flops 1920 | bytes 15360
  (845 shorter events, 561.0 us)
Async XLA Ops:
  7.2 69.4 %all-gather.9.cloned.1.call-start = ((), (), s32[]{:S(2)}) async-start(), calls=%async_computation.21 | async-start | bytes 3760128 | tf_op jit(solution)/shard_map/all_gather | solution.py:329
  7.9 92.2 %all-gather.11.cloned.1.call-start = ((), (), s32[]{:S(2)}) async-start(), calls=%async_computation.22 | async-start | bytes 1253376 | tf_op jit(solution)/shard_map/all_gather | solution.py:331
  8.7 161.5 %all-gather.13.cloned.1.call-start = ((), (), s32[]{:S(2)}) async-start(), calls=%async_computation.23 | async-start | bytes 2949120 | tf_op jit(solution)/shard_map/all_gather | solution.py:135
  74.3 238.9 %copy-start.165 = (s32[256,2]{0,1:T(2,128)}, s32[256,2]{0,1:T(2,128)S(1)}, u32[]{:S(2)}) copy-start(s32[256,2]{0,1:T(2,128)S(1)} %get-tuple-element.70) | copy-start | bytes 6148
  103.0 209.2 %copy-start.57 = (bf16[256,768]{1,0:T(8,128)(2,1)}, bf16[256,768]{1,0:T(8,128)(2,1)S(1)}, u32[]{:S(2)}) copy-start(bf16[256,768]{1,0:T(8,128)(2,1)S(1)} %multiply_convert_fusion.11) | copy-start | bytes 1179652
  140.5 116.4 %reduce-scatter.12.cloned.1.call-start = ((), (), s32[]{:S(2)}) async-start(), calls=%async_computation.24 | async-start | bytes 5898240 | tf_op jit(solution)/shard_map/reduce_scatter | solution.py:139
  260.3 53.1 %all-to-all-start.1 = ((bf16[1,4,160,768]{3,1,0,2:T(4,128)(2,1)}), bf16[1,4,160,768]{3,1,0,2:T(4,128)(2,1)S(1)}, u32[]{:S(2)}, u32[]{:S(2)}) async-start(bf16[1,4,160,768]{3,1,0,2:T(4,128)(2,1)} %copy.362), calls=%async_computation.2 | async-start | bytes 1966080 | tf_op jit(solution)/shard_map/all_to_all | solution.py:142
  264.9 154.2 %all-gather.15.cloned.1.call-start = ((), (), s32[]{:S(2)}) async-start(), calls=%async_computation.25 | async-start | bytes 2949120 | tf_op jit(solution)/shard_map/all_gather | solution.py:135
  325.2 9.9 collective-permute-start
  328.6 185.9 %copy-start.211 = (s32[512,1]{0,1:T(1,128)}, s32[512,1]{0,1:T(1,128)S(1)}, u32[]{:S(2)}) copy-start(s32[512,1]{0,1:T(1,128)S(1)} %compare_select_fusion.1) | copy-start | bytes 6148
  349.2 165.7 %copy-start.58 = (bf16[256,768]{1,0:T(8,128)(2,1)}, bf16[256,768]{1,0:T(8,128)(2,1)S(1)}, u32[]{:S(2)}) copy-start(bf16[256,768]{1,0:T(8,128)(2,1)S(1)} %multiply_convert_fusion.9) | copy-start | bytes 1179652
  388.4 117.2 %reduce-scatter.14.cloned.1.call-start = ((), (), s32[]{:S(2)}) async-start(), calls=%async_computation.26 | async-start | bytes 5898240 | tf_op jit(solution)/shard_map/reduce_scatter | solution.py:139
  508.9 29.9 %all-to-all-start.3 = ((bf16[1,4,160,768]{3,1,0,2:T(4,128)(2,1)}), bf16[1,4,160,768]{3,1,0,2:T(4,128)(2,1)S(1)}, u32[]{:S(2)}, u32[]{:S(2)}) async-start(bf16[1,4,160,768]{3,1,0,2:T(4,128)(2,1)} %copy.374), calls=%async_computation.5 | async-start | bytes 1966080 | tf_op jit(solution)/shard_map/all_to_all | solution.py:142
  552.3 10.5 collective-permute-start.1
  588.6 29.4 %all-to-all-start.4 = ((bf16[8,4,20,768]{3,1,2,0:T(4,128)(2,1)}), bf16[8,4,20,768]{3,1,2,0:T(4,128)(2,1)}, u32[]{:S(2)}, u32[]{:S(2)}) async-start(bf16[8,4,20,768]{3,1,2,0:T(4,128)(2,1)} %copy.384), calls=%async_computation.6 | async-start | bytes 1966080 | tf_op jit(solution)/shard_map/all_to_all | solution.py:132
  592.8 70.2 %all-gather.17.cloned.1.call-start = ((), (), s32[]{:S(2)}) async-start(), calls=%async_computation.27 | async-start | bytes 2949120 | tf_op jit(solution)/shard_map/all_gather | solution.py:135
  620.4 73.4 %all-gather.19.cloned.1.call-start = ((), (), s32[]{:S(2)}) async-start(), calls=%async_computation.29 | async-start | bytes 2949120 | tf_op jit(solution)/shard_map/all_gather | solution.py:216
  662.9 85.5 %reduce-scatter.18.cloned.1.call-start = ((), (), s32[]{:S(2)}) async-start(), calls=%async_computation.30 | async-start | bytes 2949120 | tf_op jit(solution)/shard_map/reduce_scatter | solution.py:223
  718.1 84.6 %reduce-scatter.16.cloned.1.call-start = ((), (), s32[]{:S(2)}) async-start(), calls=%async_computation.28 | async-start | bytes 5898240 | tf_op jit(solution)/shard_map/reduce_scatter | solution.py:139
  751.4 54.6 %all-to-all-start.7 = ((bf16[1,4,160,768]{3,1,0,2:T(4,128)(2,1)}), bf16[1,4,160,768]{3,1,0,2:T(4,128)(2,1)}, u32[]{:S(2)}, u32[]{:S(2)}) async-start(bf16[1,4,160,768]{3,1,0,2:T(4,128)(2,1)} %copy.391), calls=%async_computation.11 | async-start | bytes 1966080 | tf_op jit(solution)/shard_map/all_to_all | solution.py:226
  806.0 29.9 %all-to-all-start.5 = ((bf16[1,4,160,768]{3,1,0,2:T(4,128)(2,1)}), bf16[1,4,160,768]{3,1,0,2:T(4,128)(2,1)}, u32[]{:S(2)}, u32[]{:S(2)}) async-start(bf16[1,4,160,768]{3,1,0,2:T(4,128)(2,1)} %copy.386), calls=%async_computation.8 | async-start | bytes 1966080 | tf_op jit(solution)/shard_map/all_to_all | solution.py:142
  810.6 144.8 %all-gather.21.cloned.1.call-start = ((), (), s32[]{:S(2)}) async-start(), calls=%async_computation.31 | async-start | bytes 2949120 | tf_op jit(solution)/shard_map/all_gather | solution.py:216
  872.9 12.6 collective-permute-start.2
  926.6 83.7 %reduce-scatter.20.cloned.1.call-start = ((), (), s32[]{:S(2)}) async-start(), calls=%async_computation.32 | async-start | bytes 2949120 | tf_op jit(solution)/shard_map/reduce_scatter | solution.py:223
  1013.2 29.8 %all-to-all-start.9 = ((bf16[1,4,160,768]{3,1,0,2:T(4,128)(2,1)}), bf16[1,4,160,768]{3,1,0,2:T(4,128)(2,1)S(1)}, u32[]{:S(2)}, u32[]{:S(2)}) async-start(bf16[1,4,160,768]{3,1,0,2:T(4,128)(2,1)} %copy.402), calls=%async_computation.14 | async-start | bytes 1966080 | tf_op jit(solution)/shard_map/all_to_all | solution.py:226
  1017.8 131.7 %all-gather.23.cloned.1.call-start = ((), (), s32[]{:S(2)}) async-start(), calls=%async_computation.33 | async-start | bytes 2949120 | tf_op jit(solution)/shard_map/all_gather | solution.py:216
  1065.9 12.5 collective-permute-start.3
  1120.6 83.7 %reduce-scatter.22.cloned.1.call-start = ((), (), s32[]{:S(2)}) async-start(), calls=%async_computation.34 | async-start | bytes 2949120 | tf_op jit(solution)/shard_map/reduce_scatter | solution.py:223
  1207.2 29.9 %all-to-all-start.11 = ((bf16[1,4,160,768]{3,1,0,2:T(4,128)(2,1)}), bf16[1,4,160,768]{3,1,0,2:T(4,128)(2,1)}, u32[]{:S(2)}, u32[]{:S(2)}) async-start(bf16[1,4,160,768]{3,1,0,2:T(4,128)(2,1)} %copy.413), calls=%async_computation.17 | async-start | bytes 1966080 | tf_op jit(solution)/shard_map/all_to_all | solution.py:226
  1211.9 109.2 %reduce-scatter.28.cloned.1.call-start = ((), (), s32[]{:S(2)}) async-start(), calls=%async_computation.37 | async-start | bytes 417792
  1217.8 230.9 %reduce-scatter.26.cloned.1.call-start = ((), (), s32[]{:S(2)}) async-start(), calls=%async_computation.36 | async-start | bytes 2506752 | tf_op jit(solution)/shard_map/reduce_scatter | solution.py:415
  1252.9 195.8 %reduce-scatter.24.cloned.1.call-start = ((), (), s32[]{:S(2)}) async-start(), calls=%async_computation.35 | async-start | bytes 7520256 | tf_op jit(solution)/shard_map/reduce_scatter | solution.py:413
  (234 other events, 3007.1 us)
Sparse Core Ops, SparseCore 0:
  10.3 49.7 all-gather.8
  62.4 37.7 all-gather.10
  140.6 29.5 all-gather.12
  204.9 51.9 reduce-scatter.11
  388.5 30.5 all-gather.14
  453.5 51.9 reduce-scatter.13
  620.5 30.5 all-gather.16
  663.0 30.5 all-gather.18
  718.2 30.2 reduce-scatter.17
  750.6 51.9 reduce-scatter.15
  926.7 28.6 all-gather.20
  979.8 30.3 reduce-scatter.19
  1120.8 28.6 all-gather.22
  1173.9 30.3 reduce-scatter.21
  1217.9 56.0 reduce-scatter.27
  1278.6 61.9 reduce-scatter.25
  1345.1 90.0 reduce-scatter.23
where the time goes:
time: 1470 us; the launch traced here: 1460 us
  waiting for transfers between devices  482 us (33%)
  blocking collectives  285 us (19%)
  matrix products  280 us (19%)
  local copies, waits for them, and re-layouts  216 us (15%)
  other arithmetic  131 us (9%)
  starting transfers between devices  41.6 us (3%)
  between operations  20.3 us (1%)
    reduce_scatter x3, waiting for transfers between devices, layer_forward(): lax.psum_scatter(produced, 'col', scatter_dimension=1, tiled=True)  151 us
    unnamed x2, blocking collectives  96.8 us
    all_to_all x3, blocking collectives, layer_backward(): lax.all_to_all(slot_grad, 'row', split_axis=0, concat_axis=2, tiled=True)  83.7 us
    reduce_scatter x3, waiting for transfers between devices, layer_backward(): lax.psum_scatter(row_grad.astype(jnp.bfloat16), 'col', scatter_dimension=...  77.7 us
    all_gather x3, waiting for transfers between devices, layer_forward(): owner_rows = lax.all_gather(arrived, 'col', axis=1, tiled=True)  60.4 us
    all_to_all x2, blocking collectives, layer_forward(): lax.all_to_all(blocks, 'row', split_axis=0, concat_axis=2, tiled=True)  58.5 us
    all_gather x3, waiting for transfers between devices, layer_backward(): seen_grad = lax.all_gather(owner_grad, 'col', axis=1, tiled=True)  57.6 us
    convert_element_type x3, other arithmetic, layer_forward(): hidden = jax.nn.gelu(hidden_pre, approximate=False).astype(jnp.bfloat16)  55.8 us
  transfers between devices with their start and end apart: 28, of which 20 were waited for; matrix products, arithmetic and copies ran while one was open for 20% of the time, Pallas kernels for 0%

commit v1 on v0

v1 whole, which is shorter than its diff:
```python
from functools import partial
import math
from types import SimpleNamespace

import jax
import jax.numpy as jnp
import numpy as np
from jax import lax
from jax.experimental import pallas as pl
from jax.experimental.pallas import tpu as pltpu
from jax.sharding import PartitionSpec as P

TOP = 2
DISTANCE_BUCKETS = 32
MAX_DIST = 128
EPS = 1e-06
MESH = pl.DeviceIdType.MESH
F32 = jnp.float32
BF16 = jnp.bfloat16
MIB = 1 << 20


class Geometry:
    def __init__(self, micro, length, width, heads, experts_all, local_experts, hidden, row_count, col_count):
        self.micro, self.length, self.width, self.heads, self.hidden = micro, length, width, heads, hidden
        self.tall = -(-heads // 8) * 8
        self.capacity = max(2, (5 * length * TOP + 4 * experts_all - 1) // (4 * experts_all))
        self.local_experts = local_experts
        self.experts_all = experts_all
        self.rows, self.cols = row_count, col_count
        self.cores = 2 if row_count % 2 == 0 else 1
        self.chips = row_count // self.cores
        main = self.capacity // 16 * 16
        rest = self.capacity - main
        self.share = main // local_experts if 0 < rest <= main // local_experts else 0
        if rest and not self.share:
            main += 16
        self.main = main
        self.first = 1 if self.share else 0
        self.units = local_experts + self.first
        self.slots = row_count * self.units * main
        self.sources = row_count * col_count
        self.expert_rows = self.sources * (main + self.share)

    def bases(self):
        expert = np.arange(self.experts_all)
        owner, local = expert // self.local_experts, expert % self.local_experts
        main = ((self.first + local) * self.rows + owner) * self.main
        tail = owner * self.main + local * self.share
        both = np.stack([main, tail]).astype(np.float32)
        return np.pad(both, ((0, 0), (0, 128 - self.experts_all)))


def buckets(length):
    distance = np.arange(length)
    bucket = np.zeros(length, np.int64)
    half = DISTANCE_BUCKETS // 2
    for level in range(1, DISTANCE_BUCKETS):
        if level < half:
            limit = level
        else:
            limit = int(math.ceil(half * (MAX_DIST / half) ** ((level - half) / half)))
        bucket += distance >= limit
    return (np.arange(DISTANCE_BUCKETS)[:, None] == bucket[None, :]).astype(np.float32)


def mm(left, right, contract):
    return lax.dot_general(
        left, right, (((contract[0],), (contract[1],)), ((), ())), preferred_element_type=F32
    )


def iota(shape, axis):
    return lax.broadcasted_iota(jnp.int32, shape, axis)


def norm_factor(values):
    return lax.rsqrt(jnp.mean(values * values, axis=-1, keepdims=True) + EPS)


def gelu_pair(x):
    density = jnp.exp(-0.5 * x * x)
    t = 1.0 / (1.0 + (0.3275911 * math.sqrt(0.5)) * jnp.abs(x))
    poly = 0.5 * 1.061405429
    for coefficient in (-1.453152027, 1.421413741, -0.284496736, 0.254829592):
        poly = poly * t + 0.5 * coefficient
    beyond = poly * t * density
    cdf = jnp.where(x >= 0, 1.0 - beyond, beyond)
    return x * cdf, cdf + x * density * (1.0 / math.sqrt(2.0 * math.pi))


def slot_onehots(aux, slots):
    positions = iota((aux.shape[0], slots), 1).astype(F32)
    return [(aux[:, 2 + c : 3 + c] == positions) for c in range(TOP)]


def vmem_grant(scratch, spare):
    held = 0
    for ref in scratch:
        if getattr(ref, "memory_space", None) == pltpu.VMEM:
            held += math.prod(ref.shape) * jnp.dtype(ref.dtype).itemsize
    return -(-held // MIB) + spare


def fits(*scratches):
    return vmem_grant([ref for scratch in scratches for ref in scratch.values()], 11) <= 62


def vmem_spec():
    return pl.BlockSpec(memory_space=pltpu.VMEM)


def hbm_spec():
    return pl.BlockSpec(memory_space=pltpu.HBM)


def in_hbm(array):
    return pltpu.with_memory_space_constraint(array, pltpu.HBM)


def shape(dims, kind):
    return jax.ShapeDtypeStruct(dims, kind)


def launch(body, near=None, held=None, outs=None, kept=None, state=None, scratch=None, spare=10, cost=None, **params):
    near, held, outs, kept, scratch = (dict(part or {}) for part in (near, held, outs, kept, scratch))
    state = {} if state is None else state
    old = [name for name in kept if name in state]
    names_in, names_out = list(near) + list(held), list(outs) + list(kept)

    def kernel(*refs):
        refs = list(refs)
        given, refs = refs[: len(names_in)], refs[len(names_in) + len(old) :]
        body(SimpleNamespace(**dict(zip(names_in + names_out + list(scratch), given + refs))))

    out_shapes = list(outs.values()) + [pltpu.HBM(dims, kind) for dims, kind in kept.values()]
    plain = [isinstance(out, jax.ShapeDtypeStruct) for out in out_shapes]
    estimate = {}
    if cost is not None:
        estimate["cost_estimate"] = pl.CostEstimate(flops=cost[0], bytes_accessed=cost[1], transcendentals=0)
    results = pl.pallas_call(
        kernel,
        out_shape=out_shapes,
        in_specs=[vmem_spec()] * len(near) + [hbm_spec()] * (len(held) + len(old)),
        out_specs=[vmem_spec() if near_by else hbm_spec() for near_by in plain],
        scratch_shapes=list(scratch.values()),
        input_output_aliases={len(names_in) + i: names_out.index(name) for i, name in enumerate(old)},
        compiler_params=pltpu.CompilerParams(
            vmem_limit_bytes=vmem_grant(scratch.values(), spare) * MIB, **params
        ),
        **estimate,
    )(*near.values(), *map(in_hbm, held.values()), *(in_hbm(state[name]) for name in old))
    results = dict(zip(names_out, results))
    for name in kept:
        state[name] = results.pop(name)
    return results


def of_micro(rows, m):
    if isinstance(m, int):
        return rows[m : m + 1]
    row = rows[0:1]
    for i in range(1, rows.shape[0]):
        row = jnp.where(m == i, rows[i : i + 1], row)
    return row


def as_column(row):
    return jnp.broadcast_to(row, (8, row.shape[1])).T[:, 0:1]


class Copies:
    def __init__(self, sems):
        self.sems, self.count, self.open = sems, 0, []

    def load(self, source, target):
        copy = pltpu.make_async_copy(source, target, self.sems.at[self.count])
        self.count += 1
        copy.start()
        return copy

    def save(self, source, target):
        self.open.append(self.load(source, target))

    def wait(self):
        for copy in self.open:
            copy.wait()


def remote(source, target, send, receive, where):
    return pltpu.make_async_remote_copy(
        src_ref=source, dst_ref=target, send_sem=send, recv_sem=receive, device_id=where, device_id_type=MESH
    )


def forward_micro(geo, tick):
    if tick == 0:
        return 0
    return geo.micro - 1 if tick == geo.micro else tick - lax.axis_index("section")


def backward_micro(geo, step):
    if step == 0:
        return geo.micro - 1
    return 0 if step == geo.micro else geo.micro - step - lax.axis_index("section")


class Across:
    def __init__(self, sender, sems, at=0):
        self.section = lax.axis_index("section")
        self.sender, self.other = sender, {"section": 1 - self.section}
        self.send_sem, self.recv_sem = sems.at[at], sems.at[at + 1]

    def greet(self):
        pl.semaphore_signal(pltpu.get_barrier_semaphore(), inc=1, device_id=self.other, device_id_type=MESH)

    def copy(self, source, target):
        return remote(source, target, self.send_sem, self.recv_sem, self.other)

    def send(self, source, target):
        @pl.when(self.section == self.sender)
        def _():
            self.copy(source, target).start()

    def sent(self, source, target):
        @pl.when(self.section == self.sender)
        def _():
            self.copy(source, target).wait_send()

    def take(self, target):
        @pl.when(self.section != self.sender)
        def _():
            self.copy(target, target).wait_recv()


def prepare(experts_all, at):
    heads, length = at.bias.shape[:2]
    rows = at.small[...].astype(F32).T
    at.gains[...] = rows[experts_all : experts_all + 2]
    picked = (at.head_pick[...] * rows[experts_all + 2 : experts_all + 3]).astype(BF16)
    by_distance = mm(picked, at.spread[...], (1, 0))
    for h in range(heads):
        block = by_distance[h : h + 1, :]
        step = 1
        while step < length:
            block = jnp.concatenate([block, pltpu.roll(block, step, 1)], axis=0)
            step *= 2
        at.bias[h] = block.astype(BF16)


def diagonal_sums(block):
    length = block.shape[1]
    size = block.shape[0] // 2
    while size >= 1:
        block = block[:size] + pltpu.roll(block[size:], length - size, 1)
        size //= 2
    return block


def only_section(geo, tick):
    return {0: 0, geo.micro: 1}.get(tick)


def where_active(active, body, at):
    if active is None:
        body(at)
    else:
        pl.when(lax.axis_index("section") == active)(partial(body, at))


def dense_forward_part(geo, tick, at, copies, enter, across, loaded, fused=True):
    length, width, heads = geo.length, geo.width, geo.heads
    size = width // heads
    per = 128 // size
    m = forward_micro(geo, tick)
    packed_qkv = copies.load(at.packed.at[:, pl.ds(0, 3 * width)], at.qkv_w)
    if tick == 0:
        copies.load(at.inputs.at[m], at.stream).wait()
    else:
        first = lax.axis_index("section") == 0
        own = pltpu.make_async_copy(at.inputs.at[m], at.stream, at.stream_sem)
        if tick == 1:
            enter()
            across.send(at.out.at[0] if fused else at.out_before.at[0], at.stream_in)
        else:
            came = pltpu.make_async_copy(at.received, at.stream, at.stream_sem)

        @pl.when(first)
        def _():
            own.start()
            own.wait()

        if tick == 1:
            across.take(at.stream_in)

            @pl.when(jnp.logical_not(first))
            def _():
                at.stream[...] = at.stream_in[...]
        else:

            @pl.when(jnp.logical_not(first))
            def _():
                came.start()
                came.wait()

    packed_rest = copies.load(at.packed.at[:, pl.ds(3 * width, width + 128)], at.rest_w)
    bias_load = copies.load(at.bias, at.bias_here)
    copies.save(at.stream, at.kept_stream.at[m])
    stream = at.stream[...].astype(F32)
    at.normed[...] = (stream * norm_factor(stream) * at.gains[0:1, :]).astype(BF16)
    copies.save(at.normed, at.kept_normed.at[m])
    packed_qkv.wait()
    at.qkv[...] = mm(at.normed[...], at.qkv_w[...], (1, 0)).astype(BF16)
    copies.save(at.qkv, at.kept_qkv.at[m])
    key_at, query_at = iota((length, length), 0), iota((length, length), 1)
    segments = of_micro(at.segments[...], m).astype(F32)
    allowed = (key_at <= query_at) & (as_column(segments) == segments)
    which = iota((length, 128), 1) // size
    head_row = iota((128, length), 0) // size
    scale = 1.0 / math.sqrt(size)
    zero = jnp.zeros((length, 128), BF16)
    bias_load.wait()
    for j in range(width // 128):
        queries = at.qkv[:, 128 * j : 128 * (j + 1)]
        keys = at.qkv[:, width + 128 * j : width + 128 * (j + 1)]
        values = at.qkv[:, 2 * width + 128 * j : 2 * width + 128 * (j + 1)]
        turned_values = values.astype(F32).T
        context = jnp.zeros((128, length), F32)
        for part in range(per):
            h = j * per + part
            own = which == part
            scores = mm(jnp.where(own, keys, zero), queries, (1, 1)) * scale + at.bias_here[h].astype(F32)
            scores = jnp.where(allowed, scores, -1e30)
            exponent = jnp.exp(scores - jnp.max(scores, axis=0, keepdims=True))
            prob = (exponent * (1.0 / jnp.sum(exponent, axis=0, keepdims=True))).astype(BF16)
            at.prob[h] = prob
            own_values = jnp.where(head_row == part, turned_values, 0.0).astype(BF16)
            context = context + mm(own_values, prob, (1, 0))
        at.context[:, 128 * j : 128 * (j + 1)] = context.T.astype(BF16)
        heads_here = pl.ds(j * per, per)
        copies.save(at.prob.at[heads_here], at.kept_prob.at[m, heads_here])
    copies.save(at.context, at.kept_context.at[m])
    packed_rest.wait()
    loaded()
    residual = stream + mm(at.context[...], at.rest_w[:, :width], (1, 0))
    at.residual[...] = residual
    copies.save(at.residual, at.kept_residual.at[m])
    moe_in = (residual * norm_factor(residual) * at.gains[1:2, :]).astype(BF16)
    at.moe_in[...] = moe_in
    copies.save(at.moe_in, at.kept_moe_in.at[m])
    logits = mm(moe_in, at.rest_w[:, width:], (1, 0))
    expert_at = iota(logits.shape, 1)
    picks = [(as_column(at.routes[0, m, c : c + 1, :].astype(F32)) == expert_at.astype(F32)).astype(F32) for c in range(TOP)]
    chosen = [jnp.sum(pick * logits, axis=1, keepdims=True) for pick in picks]
    top = jnp.maximum(chosen[0], chosen[1])
    powers = [jnp.exp(value - top) for value in chosen]
    total = powers[0] + powers[1]
    shares = [power / total for power in powers]
    order = of_micro(at.order[0, :, 0, :], m).astype(F32)
    before = (order < as_column(order)).astype(BF16)
    counts = [mm(before, pick.astype(BF16), (1, 0)) for pick in picks]
    counts[1] = counts[1] + jnp.sum(picks[0], axis=0, keepdims=True)
    slots = []
    for pick, count in zip(picks, counts):
        rank = jnp.sum(pick * count, axis=1, keepdims=True)
        main = jnp.sum(pick * at.bases[0:1, :], axis=1, keepdims=True)
        tail = jnp.sum(pick * at.bases[1:2, :], axis=1, keepdims=True)
        place = jnp.where(rank < geo.main, main + rank, tail + rank - geo.main)
        slots.append(jnp.where(rank < geo.capacity, place, -1.0))
    lane = iota((length, 128), 1)
    aux = jnp.zeros((length, 128), F32)
    for place, value in enumerate(shares + slots):
        aux = jnp.where(lane == place, value, aux)
    at.aux[...] = aux
    copies.save(at.aux, at.kept_aux.at[m])
    first, second = slot_onehots(aux, geo.slots)
    at.slots[...] = mm((first | second).astype(BF16), moe_in, (0, 0)).astype(BF16).reshape(at.slots.shape)


def dense_forward_body(geo, tick, at):
    across = Across(0, at.across_sems) if tick == 1 else None
    if across:
        across.greet()

    def enter():
        pl.semaphore_wait(pltpu.get_barrier_semaphore(), 1)

    copies = Copies(at.sems)
    dense_forward_part(geo, tick, at, copies, enter, across, lambda: None, fused=False)
    copies.save(at.slots, at.slot_rows)
    copies.wait()
    if across:
        across.sent(at.out_before.at[0], at.stream_in)


def dense_forward_scratch(geo, tick):
    length, width, heads = geo.length, geo.width, geo.heads
    scratch = dict(
        stream=pltpu.VMEM((length, width), BF16),
        qkv_w=pltpu.VMEM((width, 3 * width), BF16),
        rest_w=pltpu.VMEM((width, width + 128), BF16),
        bias_here=pltpu.VMEM((heads, length, length), BF16),
        normed=pltpu.VMEM((length, width), BF16),
        qkv=pltpu.VMEM((length, 3 * width), BF16),
        prob=pltpu.VMEM((heads, length, length), BF16),
        context=pltpu.VMEM((length, width), BF16),
        residual=pltpu.VMEM((length, width), F32),
        moe_in=pltpu.VMEM((length, width), BF16),
        aux=pltpu.VMEM((length, 128), F32),
        slots=pltpu.VMEM((geo.units, geo.rows, geo.main, width), BF16),
        sems=pltpu.SemaphoreType.DMA((16 + width // 128,)),
        stream_sem=pltpu.SemaphoreType.DMA,
        across_sems=pltpu.SemaphoreType.DMA((4,)),
    )
    if tick == 1:
        scratch["stream_in"] = pltpu.VMEM((length, width), BF16)
    return scratch


def dense_forward_refs(geo, tick, given, state, received):
    micro, length, width, heads = geo.micro, geo.length, geo.width, geo.heads
    near = {name: given[name] for name in ("segments", "order", "routes", "gains", "bases")}
    held = dict(packed=given["packed"], bias=given["bias"], inputs=given["inputs"])
    if tick > 1:
        held["received"] = received
    kept = dict(
        kept_stream=((micro, length, width), BF16),
        kept_normed=((micro, length, width), BF16),
        kept_qkv=((micro, length, 3 * width), BF16),
        kept_prob=((micro, heads, length, length), BF16),
        kept_context=((micro, length, width), BF16),
        kept_residual=((micro, length, width), F32),
        kept_moe_in=((micro, length, width), BF16),
        kept_aux=((micro, length, 128), F32),
    )
    return near, held, kept


def dense_forward(geo, tick, given, state, received):
    near, held, kept = dense_forward_refs(geo, tick, given, state, received)
    params = {}
    if tick == 1:
        held["out_before"] = state["out"]
        params = dict(collective_id=5 + 2 * geo.micro, has_side_effects=True)
    return launch(
        partial(where_active, only_section(geo, tick), partial(dense_forward_body, geo, tick)),
        near=near,
        held=held,
        outs=dict(slot_rows=pltpu.HBM((geo.units, geo.rows, geo.main, geo.width), BF16)),
        kept=kept,
        state=state,
        scratch=dense_forward_scratch(geo, tick),
        cost=(2_000_000_000, 14_000_000),
        **params,
    )["slot_rows"]


def combine(home, aux, result, picked_ref):
    for c, onehot in enumerate(slot_onehots(aux, home.shape[0])):
        picked = mm(onehot.astype(BF16), home, (1, 0))
        picked_ref[c] = picked.astype(BF16)
        result = result + aux[:, c : c + 1] * picked
    return result


def spread(incoming, aux, picked_ref, slots):
    lane = iota((aux.shape[0], 128), 1)
    gates = jnp.zeros(lane.shape, F32)
    total = 0.0
    for c, onehot in enumerate(slot_onehots(aux, slots)):
        gate = jnp.sum(picked_ref[c].astype(F32) * incoming, axis=1, keepdims=True)
        gates = jnp.where(lane == c, gate, gates)
        total = total + mm(onehot.astype(BF16), (aux[:, c : c + 1] * incoming).astype(BF16), (0, 0))
    return gates, total.astype(BF16)


def expert_picker(geo, e):
    dims = (geo.sources * geo.share, geo.sources * geo.main)
    own, place = iota(dims, 0), iota(dims, 1)
    return (place == own // geo.share * geo.main + e * geo.share + own % geo.share).astype(BF16)


class Exchange:
    def __init__(self, geo, at, x, active=None):
        self.geo, self.x, self.at = geo, x, at
        self.relay = geo.chips // 2 if active is not None and geo.chips > 1 else None
        self.near_rows = geo.cores
        self.ahead = 2 if self.relay else 1
        self.peers = geo.cols - 1
        self.other = {"section": 1 - lax.axis_index("section")}
        self.r, self.c = lax.axis_index("row"), lax.axis_index("col")
        self.z, self.core = self.r // geo.cores, self.r % geo.cores
        self.partner = self.z * geo.cores + (self.core + 1) % geo.cores

    def far(self, direct):
        return [k for k in range(1, self.geo.chips) if direct or k != self.relay]

    def far_rows(self, direct):
        return self.geo.cores * len(self.far(direct))

    def kinds(self):
        first = self.geo.first if self.relay else 0
        return [(pl.ds(at, n), direct) for at, n, direct in ((0, first, True), (first, self.geo.units - first, False)) if n]

    def chip(self, k):
        return (self.z + k + self.geo.chips) % self.geo.chips

    def row(self, k, d):
        return self.partner if k == 0 else self.chip(k) * self.geo.cores + d

    def col(self, j):
        return (self.c + j + self.geo.cols) % self.geo.cols

    def rows(self, k):
        return pl.ds(self.chip(k) * self.geo.cores, self.geo.cores)

    def others(self, k):
        return range(self.geo.cores - 1) if k == 0 else range(self.geo.cores)

    def greet(self):
        barrier = pltpu.get_barrier_semaphore()
        for k in range(self.geo.chips):
            for d in self.others(k):
                pl.semaphore_signal(barrier, inc=1, device_id={"row": self.row(k, d)}, device_id_type=MESH)
        for j in range(1, self.geo.cols):
            pl.semaphore_signal(barrier, inc=1, device_id={"col": self.col(j)}, device_id_type=MESH)
        if self.relay:
            pl.semaphore_signal(barrier, inc=1, device_id=self.other, device_id_type=MESH)

    def await_greetings(self, more):
        more = more + (1 if self.relay else 0)
        pl.semaphore_wait(pltpu.get_barrier_semaphore(), self.geo.rows + self.geo.cols - 2 + more)

    def came(self, block, sem):
        remote(block, block, self.at.done, sem, self.other).wait_recv()

    def left(self, block, sem):
        remote(block, block, sem, self.at.done, self.other).wait_send()


    def own(self, u):
        return pltpu.make_async_copy(
            self.x.at[u, self.r], self.at.inbox.at[u, self.c, self.r], self.at.own_sem.at[u]
        )

    def kind(self, u):
        if not (self.relay and self.geo.first):
            return 0
        return int(u < self.geo.first) if isinstance(u, int) else (u + self.geo.units - 1) // self.geo.units * -1 + 1

    def send(self, u, k):
        for d in self.others(k):
            remote(
                self.x.at[u, self.row(k, d)], self.at.inbox.at[u, self.c, self.r], self.at.in_send.at[self.kind(u)],
                self.at.in_recv.at[u, k], {"row": self.row(k, d)},
            ).start()

    def send_out(self, u):
        if self.relay:
            remote(
                self.x.at[u, self.rows(self.relay)], self.at.via_x.at[u], self.at.via_send,
                self.at.via_x_recv.at[u], self.other,
            ).start()

    def hand_over(self, u, k):
        block = self.at.inbox.at[u, self.c, self.rows(-k)]
        for j in range(1, self.geo.cols):
            remote(block, block, self.at.pass_send.at[u], self.at.pass_recv.at[u], {"col": self.col(j)}).start()

    def each(self, body):
        lax.fori_loop(0, self.geo.units, lambda u, carry: (body(u), carry)[1], 0)

    def open(self):
        for u in range(min(self.ahead, self.geo.units)):
            direct = u < self.geo.first
            for k in self.far(direct):
                self.send(u, k)
            if not direct:
                self.send_out(u)

        def body(u):
            self.own(u).start()
            self.send(u, 0)

        self.each(body)
        for u in range(min(3, self.geo.units)):
            self.pass_on_own(u)

    def pass_on_own(self, u):
        self.own(u).wait()
        if self.geo.cores > 1:
            self.came(self.at.inbox.at[u, self.c, pl.ds(0, 1)], self.at.in_recv.at[u, 0])
        self.hand_over(u, 0)

    def pass_on(self, u, direct=False):
        @pl.when(u + self.ahead < self.geo.units)
        def _():
            self.send_out(u + self.ahead)

        for k in self.far(direct):
            self.came(self.at.inbox.at[u, self.c, self.rows(-k)], self.at.in_recv.at[u, k])

            @pl.when(u + self.ahead < self.geo.units)
            def _():
                if k in self.far(False):
                    self.send(u + self.ahead, k)

            self.hand_over(u, k)

        @pl.when(u + 3 < self.geo.units)
        def _():
            self.pass_on_own(u + 3)

    def collect(self, u, direct=False):
        if self.peers:
            block = self.at.inbox.at[u, pl.ds(0, self.peers), pl.ds(0, self.near_rows + self.far_rows(direct))]
            self.came(block, self.at.pass_recv.at[u])
            self.left(block, self.at.pass_send.at[u])
        if self.relay and not direct:
            self.came(self.at.inbox.at[u, :, pl.ds(0, self.geo.cores)], self.at.into_recv.at[u])


    def send_parts(self, u, far, direct=False):
        if far and self.relay and not direct:
            for j in range(self.geo.cols):
                remote(
                    self.at.inbox.at[u, self.col(j), self.rows(self.relay)], self.at.via_part.at[u, j],
                    self.at.via_part_send, self.at.via_part_recv.at[u], self.other,
                ).start()
        for k in self.far(direct) if far else (0,):
            for j in range(1, self.geo.cols):
                remote(
                    self.at.inbox.at[u, self.col(j), self.rows(k)], self.at.arrived.at[u, j - 1, self.rows(k)],
                    self.at.out_send.at[self.kind(u)], self.at.out_recv.at[u, int(far)], {"col": self.col(j)},
                ).start()

    def send_home(self, u, far, direct=False):
        count = self.far_rows(direct) if far else self.near_rows
        if self.peers and count:
            self.came(self.at.arrived.at[u, :, pl.ds(0, count)], self.at.out_recv.at[u, int(far)])
        for k in self.far(direct) if far else (0,):
            rows = self.rows(k)
            total = self.at.inbox[u, self.c, rows].astype(F32)
            for j in range(1, self.geo.cols):
                total = total + self.at.arrived[u, j - 1, rows].astype(F32)
            self.at.stage[u, rows] = total.astype(BF16)
            for d in self.others(k):
                remote(
                    self.at.stage.at[u, self.row(k, d)], self.at.home.at[u, self.r], self.at.home_send.at[self.kind(u)],
                    self.at.home_recv.at[self.kind(u)], {"row": self.row(k, d)},
                ).start()
            if k == 0:
                self.at.home[u, self.r] = self.at.stage[u, self.r]

    def finish(self):
        at, cores = self.at, self.geo.cores
        for units, direct in self.kinds():
            sent_rows = self.far_rows(direct) + cores - 1
            if sent_rows:
                block = at.home.at[units, pl.ds(0, sent_rows)]
                self.came(block, at.home_recv.at[int(direct)])
                self.left(block, at.home_send.at[int(direct)])
                self.left(block, at.in_send.at[int(direct)])
            if self.peers:
                block = at.arrived.at[units, :, pl.ds(0, self.near_rows + self.far_rows(direct))]
                self.left(block, at.out_send.at[int(direct)])
            if self.relay and not direct:
                self.came(at.home.at[units, pl.ds(0, cores)], at.home_in_recv)
                self.left(at.via_x.at[units], at.via_send)
                self.left(at.via_part.at[units], at.via_part_send)


    def along(self, u, d, source, target, at):
        where = {"row": self.row(self.relay, d)}
        return remote(
            source.at[u, d], target.at[u, self.core], self.at.core_sems.at[at, u, d],
            self.at.core_sems.at[at + 1, u, self.core], where,
        )

    def along_came(self, u, d, target, at):
        self.came(target.at[u, d], self.at.core_sems.at[at + 1, u, d])

    def across(self, u, j):
        return remote(
            self.at.via_z.at[u], self.at.via_y.at[u, j - 1], self.at.via_sems.at[2, u, j], self.at.via_sems.at[3, u, j],
            {"col": self.col(j)},
        )

    def into(self, u, j):
        source = self.at.via_y.at[u, j - 1] if j else self.at.via_z.at[u]
        target = self.at.inbox.at[u, self.col(-j), self.rows(-self.relay)]
        return remote(source, target, self.at.via_sems.at[0, u, j], self.at.into_recv.at[u], self.other)

    def part_across(self, u, j):
        return remote(
            self.at.via_part.at[u, j], self.at.via_sum.at[u, j - 1], self.at.via_sems.at[4, u, j],
            self.at.via_sems.at[5, u, j], {"col": self.col(j)},
        )

    def home_in(self, u):
        return remote(
            self.at.via_home.at[u], self.at.home.at[u, self.rows(-self.relay)], self.at.via_sems.at[1, u, 0],
            self.at.home_in_recv, self.other,
        )

    def carry(self):
        geo, at = self.geo, self.at
        cores, columns = range(geo.cores), range(1, geo.cols)

        def rows_out(u):
            self.came(at.via_x.at[u], at.via_x_recv.at[u])
            for d in cores:
                self.along(u, d, at.via_x, at.via_z, 0).start()

        def rows_on(u):
            for d in cores:
                self.along_came(u, d, at.via_z, 0)
            self.into(u, 0).start()
            for j in columns:
                self.across(u, j).start()

        def rows_in(u):
            for j in columns:
                self.across(u, j).wait_recv()
                self.into(u, j).start()

        def parts_out(u):
            self.came(at.via_part.at[u], at.via_part_recv.at[u])
            for j in columns:
                self.part_across(u, j).start()

        def parts_on(u):
            total = at.via_part[u, 0].astype(F32)
            for j in columns:
                self.part_across(u, j).wait_recv()
                total = total + at.via_sum[u, j - 1].astype(F32)
            at.via_total[u] = total.astype(BF16)
            for d in cores:
                self.along(u, d, at.via_total, at.via_home, 2).start()

        def parts_in(u):
            for d in cores:
                self.along_came(u, d, at.via_home, 2)
            self.home_in(u).start()

        units = list(range(geo.first, geo.units))
        for steps in ((rows_out, rows_on, rows_in), (parts_out, parts_on, parts_in)):
            for t in range(len(units) + 2):
                for lag, work in enumerate(steps):
                    if 0 <= t - lag < len(units):
                        work(units[t - lag])
        for u in units:
            for d in cores:
                self.along(u, d, at.via_x, at.via_z, 0).wait_send()
                self.along(u, d, at.via_total, at.via_home, 2).wait_send()
            for j in range(geo.cols):
                self.into(u, j).wait_send()
            for j in columns:
                self.across(u, j).wait_send()
                self.part_across(u, j).wait_send()
            self.home_in(u).wait_send()


def run_experts(geo, exchange, rows, total, shared, loads, expert, saves):
    first, count = geo.first, geo.sources * geo.main
    inbox = exchange.at.inbox
    width = inbox.shape[-1]
    exchange.open()
    if first:
        exchange.pass_on(0, True)
    exchange.pass_on(first)
    if first:
        exchange.collect(0, True)
        shared[...] = jnp.zeros(shared.shape, F32)

    def step(e, carry):
        u = e + first
        slot = e % 2

        @pl.when(e + 1 < geo.local_experts)
        def _():
            exchange.pass_on(u + 1)

        exchange.collect(u)

        @pl.when(e >= 2)
        def _():
            for copy in saves(e - 2, slot):
                copy.wait()

        rows[slot, :count] = inbox[u].reshape(count, width)
        if first:
            picker = expert_picker(geo, e)
            tail = inbox[0].reshape(count, width)
            rows[slot, count:] = mm(picker, tail, (1, 0)).astype(BF16)
        for copy in loads(e):
            copy.wait()
        expert(e, slot)
        for copy in saves(e, slot):
            copy.start()
        inbox[u] = total[:count].astype(BF16).reshape(inbox.shape[1:])
        exchange.send_parts(u, True)
        if first:
            shared[...] += mm(picker, total[count:].astype(BF16), (0, 0))

        @pl.when(e >= 1)
        def _():
            exchange.send_home(u - 1, True)
            if exchange.relay:
                exchange.send_parts(u - 1, False)

        return carry

    lax.fori_loop(0, geo.local_experts, step, 0)
    if first:
        inbox[0] = shared[...].astype(BF16).reshape(inbox.shape[1:])
        exchange.send_parts(0, True, True)
    for u in range(geo.units):
        if not exchange.relay or u < first or u == geo.units - 1:
            exchange.send_parts(u, False)
    exchange.send_home(geo.units - 1, True)
    if first:
        exchange.send_home(0, True, True)
    exchange.each(lambda u: exchange.send_home(u, False))
    for e in range(max(0, geo.local_experts - 2), geo.local_experts):
        for copy in saves(e, e % 2):
            copy.wait()
    exchange.finish()


def share_work(exchange, active, work):
    if not exchange.relay:
        work()
        return
    section = lax.axis_index("section")
    pl.when(section == active)(work)

    @pl.when(section != active)
    def _():
        exchange.await_greetings(0)
        exchange.carry()


def start_loads(geo, loads):
    for e in range(geo.local_experts):
        for copy in loads(e):
            copy.start()


def forward_body(geo, tick, tile, fused, at):
    m = forward_micro(geo, tick)
    take, send = fused and tick == 1, 1 <= tick < geo.micro
    active = only_section(geo, tick)
    exchange = Exchange(geo, at, at.slots if fused else at.slot_rows, active)
    exchange.greet()
    across_in, across_out = Across(0, at.across_sems, 2), Across(0, at.across_sems)
    if take or send:
        across_out.greet()
    w_in, w_out = at.w_in_here, at.w_out_here

    def loads(e):
        return (
            pltpu.make_async_copy(at.w_in.at[e], w_in.at[e], at.load_sem.at[e, 0]),
            pltpu.make_async_copy(at.w_out.at[e], w_out.at[e], at.load_sem.at[e, 1]),
        )

    def saves(e, slot):
        return (
            pltpu.make_async_copy(at.rows.at[slot], at.kept_rows.at[m, e], at.save_sem.at[slot, 0]),
            pltpu.make_async_copy(at.wide.at[slot], at.kept_hidden.at[m, e], at.save_sem.at[slot, 1]),
            pltpu.make_async_copy(at.slope.at[slot], at.kept_slope.at[m, e], at.save_sem.at[slot, 2]),
        )

    def expert(e, slot):
        for f in range(0, geo.hidden, tile):
            value, derivative = gelu_pair(mm(at.rows[slot], w_in[e, :, f : f + tile], (1, 0)))
            value = value.astype(BF16)
            at.wide[slot, :, f : f + tile] = value
            at.slope[slot, :, f : f + tile] = derivative.astype(BF16)
            product = mm(value, w_out[e, f : f + tile, :], (1, 0))
            at.total[...] = product if f == 0 else at.total[...] + product

    def enter():
        exchange.await_greetings(int(take or send))

    def work():
        copies = Copies(at.sems)
        if fused:
            dense_forward_part(geo, tick, at, copies, enter, across_in, lambda: start_loads(geo, loads))
            if not take:
                enter()
        else:
            start_loads(geo, loads)
            aux_load = copies.load(at.kept_aux.at[m], at.aux)
            residual_load = copies.load(at.kept_residual.at[m], at.residual)
            enter()
        run_experts(geo, exchange, at.rows, at.total, at.shared, loads, expert, saves)
        if not fused:
            aux_load.wait()
            residual_load.wait()
        home = at.home[...].reshape(geo.slots, geo.width)
        at.result[...] = combine(home, at.aux[...], at.residual[...], at.picked).astype(BF16)
        if send:
            across_out.send(at.result, at.received_out)
        copies.save(at.result, at.out.at[m])
        copies.save(at.picked, at.kept_picked.at[m])
        copies.wait()
        if take:
            across_in.sent(at.out.at[0], at.stream_in)
        if send:
            across_out.take(at.received_out)
            across_out.sent(at.result, at.received_out)

    share_work(exchange, active, work)


def backward_body(geo, step, tile, fused, at):
    m = backward_micro(geo, step)
    take, send = step == 1, fused and 1 <= step < geo.micro
    active = only_section(geo, geo.micro - step)
    exchange = Exchange(geo, at, at.slot_grad, active)
    exchange.greet()
    first = lax.axis_index("section") == 0
    across, across_out = Across(1, at.across_sems), Across(1, at.across_sems, 2)
    if take or send:
        across.greet()
    w_in, w_out = at.w_in_here, at.w_out_here

    def loads(e):
        return (
            pltpu.make_async_copy(at.w_out.at[e], w_out.at[e], at.load_sem.at[e, 1]),
            pltpu.make_async_copy(at.kept_slope.at[m, e], at.slope.at[e], at.load_sem.at[e, 2]),
            pltpu.make_async_copy(at.w_in.at[e], w_in.at[e], at.load_sem.at[e, 0]),
        )

    def saves(e, slot):
        return (
            pltpu.make_async_copy(at.rows.at[slot], at.kept_seen.at[m, e], at.save_sem.at[slot, 0]),
            pltpu.make_async_copy(at.wide.at[slot], at.kept_pre.at[m, e], at.save_sem.at[slot, 1]),
        )

    def expert(e, slot):
        for f in range(0, geo.hidden, tile):
            grad = mm(at.rows[slot], w_out[e, f : f + tile, :], (1, 1))
            value = (grad * at.slope[e, :, f : f + tile].astype(F32)).astype(BF16)
            at.wide[slot, :, f : f + tile] = value
            product = mm(value, w_in[e, :, f : f + tile], (1, 1))
            at.total[...] = product if f == 0 else at.total[...] + product

    def incoming_load():
        own = pltpu.make_async_copy(at.cotangent.at[m], at.incoming_here, at.incoming_sem)
        if step == 0:
            return [own], [own]
        if step == 1:
            return [], [own]
        return [pltpu.make_async_copy(at.received, at.incoming_here, at.incoming_sem)], [own]

    def of_sections(action):
        early, late = incoming_load()

        @pl.when(first)
        def _():
            for copy in early:
                getattr(copy, action)()

        @pl.when(jnp.logical_not(first))
        def _():
            for copy in late:
                getattr(copy, action)()

    def work():
        copies = Copies(at.sems)
        picked_load = copies.load(at.kept_picked.at[m], at.picked)
        aux_load = copies.load(at.kept_aux.at[m], at.aux)
        of_sections("start")
        start_loads(geo, loads)
        dense_loads = dense_backward_loads(geo, m, at, copies) if fused else None
        exchange.await_greetings(int(take or send))
        if take:
            across.send(at.sent, at.incoming_far)
            across.take(at.incoming_far)

            @pl.when(first)
            def _():
                at.incoming_here[...] = at.incoming_far[...]

        of_sections("wait")
        picked_load.wait()
        aux_load.wait()
        at.incoming[...] = at.incoming_here[...]
        gates, slot_grad = spread(at.incoming_here[...].astype(F32), at.aux[...], at.picked, geo.slots)
        at.gates[...] = gates
        at.slot_grad[...] = slot_grad.reshape(at.slot_grad.shape)
        run_experts(geo, exchange, at.rows, at.total, at.shared, loads, expert, saves)
        first_slots, second_slots = slot_onehots(at.aux[...], geo.slots)
        home = at.home[...].reshape(geo.slots, geo.width)
        at.moe_grad[...] = mm((first_slots | second_slots).astype(BF16), home, (1, 0))
        if fused:
            dense_backward_part(geo, step, at, copies, dense_loads, lambda: None, across_out if send else None)
        if take:
            across.sent(at.sent, at.incoming_far)

    share_work(exchange, active, work)


def tile_of(hidden, limit):
    return limit if hidden % limit == 0 else hidden


def experts_scratch(geo, slope_slots):
    rows, local, width, hidden = geo.expert_rows, geo.local_experts, geo.width, geo.hidden
    steps = max(1, geo.cols - 1)
    one = pltpu.SemaphoreType.DMA
    two = pltpu.SemaphoreType.DMA((2,))
    unit = pltpu.SemaphoreType.DMA((geo.units,))
    return dict(
        inbox=pltpu.VMEM((geo.units, geo.cols, geo.rows, geo.main, width), BF16),
        arrived=pltpu.VMEM((geo.units, steps, geo.rows, geo.main, width), BF16),
        stage=pltpu.VMEM((geo.units, geo.rows, geo.main, width), BF16),
        home=pltpu.VMEM((geo.units, geo.rows, geo.main, width), BF16),
        picked=pltpu.VMEM((TOP, geo.length, width), BF16),
        aux=pltpu.VMEM((geo.length, 128), F32),
        rows=pltpu.VMEM((2, rows, width), BF16),
        wide=pltpu.VMEM((2, rows, hidden), BF16),
        slope=pltpu.VMEM((slope_slots, rows, hidden), BF16),
        w_in_here=pltpu.VMEM((local, width, hidden), BF16),
        w_out_here=pltpu.VMEM((local, hidden, width), BF16),
        total=pltpu.VMEM((rows, width), F32),
        shared=pltpu.VMEM((geo.sources * geo.main if geo.share else 16, width), F32),
        via_x=pltpu.VMEM((geo.units, geo.cores, geo.main, width), BF16),
        via_z=pltpu.VMEM((geo.units, geo.cores, geo.main, width), BF16),
        via_y=pltpu.VMEM((geo.units, steps, geo.cores, geo.main, width), BF16),
        via_part=pltpu.VMEM((geo.units, geo.cols, geo.cores, geo.main, width), BF16),
        via_sum=pltpu.VMEM((geo.units, steps, geo.cores, geo.main, width), BF16),
        via_total=pltpu.VMEM((geo.units, geo.cores, geo.main, width), BF16),
        via_home=pltpu.VMEM((geo.units, geo.cores, geo.main, width), BF16),
        via_sems=pltpu.SemaphoreType.DMA((6, geo.units, geo.cols)),
        core_sems=pltpu.SemaphoreType.DMA((4, geo.units, geo.cores)),
        own_sem=unit, pass_send=unit, pass_recv=unit, into_recv=unit, via_x_recv=unit, via_part_recv=unit,
        in_send=two, out_send=two, home_send=two, home_recv=two, home_in_recv=one, via_send=one, via_part_send=one,
        done=one,
        in_recv=pltpu.SemaphoreType.DMA((geo.units, geo.chips)),
        out_recv=pltpu.SemaphoreType.DMA((geo.units, 2)),
        load_sem=pltpu.SemaphoreType.DMA((local, 3)),
        save_sem=pltpu.SemaphoreType.DMA((2, 3)),
        sems=pltpu.SemaphoreType.DMA((6,)),
        across_sems=pltpu.SemaphoreType.DMA((4,)),
    )


def experts_cost(geo):
    weights = geo.local_experts * geo.hidden * geo.width
    return (4 * geo.expert_rows * weights, 4 * weights)


def forward_scratch(geo):
    scratch = experts_scratch(geo, 2)
    scratch["residual"] = pltpu.VMEM((geo.length, geo.width), F32)
    scratch["result"] = pltpu.VMEM((geo.length, geo.width), BF16)
    return scratch


def forward_tick(geo, tick, given, state, received):
    micro, length, width = geo.micro, geo.length, geo.width
    rows, local, hidden = geo.expert_rows, geo.local_experts, geo.hidden
    dense, scratch = dense_forward_scratch(geo, tick), forward_scratch(geo)
    fused = fits(dense, scratch)
    near, kept = {}, {}
    held = dict(w_in=given["w_in"], w_out=given["w_out"])
    if fused:
        near, dense_held, kept = dense_forward_refs(geo, tick, given, state, received)
        held.update(dense_held)
        scratch.update(dense)
    else:
        held["slot_rows"] = dense_forward(geo, tick, given, state, received)
        held.update(kept_aux=state["kept_aux"], kept_residual=state["kept_residual"])
    kept.update(
        out=((micro, length, width), BF16),
        kept_picked=((micro, TOP, length, width), BF16),
        kept_rows=((micro, local, rows, width), BF16),
        kept_hidden=((micro, local, rows, hidden), BF16),
        kept_slope=((micro, local, rows, hidden), BF16),
    )
    results = launch(
        partial(forward_body, geo, tick, tile_of(hidden, 512), fused),
        near=near,
        held=held,
        outs=dict(received_out=pltpu.HBM((length, width), BF16)) if 1 <= tick < micro else {},
        kept=kept,
        state=state,
        scratch=scratch,
        cost=experts_cost(geo),
        collective_id=3 + tick,
        has_side_effects=True,
    )
    return results.get("received_out")


def backward_step(geo, step, given, state, sent, received):
    micro, length, width = geo.micro, geo.length, geo.width
    rows, local, hidden = geo.expert_rows, geo.local_experts, geo.hidden
    scratch = experts_scratch(geo, local)
    scratch["slot_grad"] = pltpu.VMEM((geo.units, geo.rows, geo.main, width), BF16)
    scratch["incoming_here"] = pltpu.VMEM((length, width), BF16)
    scratch["incoming_sem"] = pltpu.SemaphoreType.DMA
    held = dict(
        cotangent=given["cotangent"], w_in=given["w_in"], w_out=given["w_out"], kept_aux=state["kept_aux"],
        kept_picked=state["kept_picked"], kept_slope=state["kept_slope"],
    )
    if step == 1:
        held["sent"] = sent
        scratch["incoming_far"] = pltpu.VMEM((length, width), BF16)
    elif step:
        held["received"] = received
    between = dict(
        moe_grad=shape((length, width), F32), gates=shape((length, 128), F32), incoming=shape((length, width), BF16)
    )
    dense = dense_backward_scratch(geo)
    near, outs, kept = {}, between, {}
    between_scratch = {name: pltpu.VMEM(one.shape, one.dtype) for name, one in between.items()}
    fused = fits(scratch, dense, between_scratch)
    if fused:
        near, dense_held, outs, kept = dense_backward_refs(geo, step, given, state)
        held.update(dense_held)
        scratch.update(dense)
        scratch.update(between_scratch)
    kept.update(
        kept_seen=((micro, local, rows, width), BF16),
        kept_pre=((micro, local, rows, hidden), BF16),
    )
    results = launch(
        partial(backward_body, geo, step, tile_of(hidden, 512), fused),
        near=near,
        held=held,
        outs=outs,
        kept=kept,
        state=state,
        scratch=scratch,
        cost=experts_cost(geo),
        collective_id=4 + micro + step,
        has_side_effects=True,
    )
    return results if fused else dense_backward(geo, step, results, given, state)


class Shards:
    def __init__(self, geo):
        self.cores, self.chips, self.cols = geo.cores, geo.chips, geo.cols
        r, self.c = lax.axis_index("row"), lax.axis_index("col")
        self.z, self.core = r // self.cores, r % self.cores

    def chip(self, k):
        return (self.z + k + self.chips) % self.chips

    def col(self, j):
        return (self.c + j + self.cols) % self.cols

    def row(self, z, other=0):
        return z * self.cores + (self.core + other) % self.cores

    def greet(self):
        barrier = pltpu.get_barrier_semaphore()
        targets = [{"row": self.row(self.chip(k))} for k in range(1, self.chips)]
        targets += [{"col": self.col(j)} for j in range(1, self.cols)]
        targets += [{"row": self.row(self.z, 1)}] * (self.cores - 1)
        for target in targets:
            pl.semaphore_signal(barrier, inc=1, device_id=target, device_id_type=MESH)
        self.greeted = len(targets)

    def await_greetings(self):
        pl.semaphore_wait(pltpu.get_barrier_semaphore(), self.greeted)


def gather_kernel(geo, pieces, qkv, out, router, gain_one, gain_two, terms, all_ref, small, own_sems, z_send, z_recv,
                  y_send, y_recv, core_send, core_recv):
    at = Shards(geo)
    at.greet()
    share, total = all_ref.shape[2:]
    narrow, wide = out.shape[1], qkv.shape[1]
    mine = all_ref.at[at.row(at.z), at.c]
    copies = Copies(own_sems)
    copies.save(qkv, mine.at[:, pl.ds(0, wide)])
    copies.save(out, mine.at[:, pl.ds(wide, narrow)])
    experts_all, count = router.shape[1], terms.shape[1]

    def unit(dims, shift=0):
        return (iota(dims, 0) + shift == iota(dims, 1)).astype(BF16)

    columns = mm(router[...], unit((experts_all, 128)), (1, 0))
    long_terms = mm(terms[...], unit((count, share)), (1, 0)).astype(BF16)
    for k, row in enumerate((gain_one[...], gain_two[...], long_terms)):
        columns = columns + mm(row, unit((1, 128), experts_all + k), (0, 0))
    small[...] = columns.astype(BF16)
    copies.save(small, mine.at[:, pl.ds(wide + narrow, 128)])
    copies.wait()
    at.await_greetings()
    step = total // pieces

    def block(k, j, h):
        return all_ref.at[at.row(at.chip(-k)), at.col(-j), :, pl.ds(h * step, step)]

    def pass_z(k, h):
        own = block(0, 0, h)
        remote(own, own, z_send, z_recv.at[h, k - 1], {"row": at.row(at.chip(k))}).start()

    def pass_y(k, h):
        for j in range(1, at.cols):
            one = block(k, 0, h)
            remote(one, one, y_send, y_recv.at[h, k, j - 1], {"col": at.col(j)}).start()

    def pass_core(k, j, h):
        if at.cores > 1:
            one = block(k, j, h)
            remote(one, one, core_send, core_recv, {"row": at.row(at.z, 1)}).start()

    def came(one, sem):
        remote(one, one, core_send, sem, {"row": at.row(at.z, 1)}).wait_recv()

    def left(one, sem):
        remote(one, one, sem, core_recv, {"row": at.row(at.z, 1)}).wait_send()

    def take_y(h):
        for k in range(at.chips):
            for j in range(1, at.cols):
                came(block(k, j, h), y_recv.at[h, k, j - 1])
                pass_core(k, j, h)

    for k in range(1, at.chips):
        pass_z(k, 0)
    for h in range(pieces):
        pass_y(0, h)
    for h in range(pieces):
        pass_core(0, 0, h)
    for h in range(pieces):
        for k in range(1, at.chips):
            came(block(k, 0, h), z_recv.at[h, k - 1])
            if h + 1 < pieces:
                pass_z(k, h + 1)
            pass_y(k, h)
            pass_core(k, 0, h)
        if h:
            take_y(h - 1)
    take_y(pieces - 1)
    if at.cores > 1:
        came(all_ref.at[pl.ds(0, at.chips)], core_recv)
        left(all_ref.at[pl.ds(0, at.chips)], core_send)
    if at.chips > 1:
        left(all_ref.at[pl.ds(0, at.chips - 1), 0], z_send)
    if at.cols > 1:
        left(all_ref.at[pl.ds(0, at.chips), pl.ds(0, at.cols - 1)], y_send)


def shard_sems(geo):
    chips = geo.chips
    z = pltpu.SemaphoreType.DMA((max(1, chips - 1),))
    y = pltpu.SemaphoreType.DMA((chips, max(1, geo.cols - 1)))
    core = pltpu.SemaphoreType.DMA((chips, geo.cols))
    return chips, z, y, core


def gather_shards(geo, qkv, out, router, gain_one, gain_two, terms):
    share, total = qkv.shape[0], qkv.shape[1] + out.shape[1] + 128
    pieces = 5 if total % 640 == 0 else 1
    one = pltpu.SemaphoreType.DMA
    return pl.pallas_call(
        partial(gather_kernel, geo, pieces),
        out_shape=pltpu.HBM((geo.rows, geo.cols, share, total), BF16),
        in_specs=[hbm_spec()] * 2 + [vmem_spec()] * 4,
        out_specs=hbm_spec(),
        scratch_shapes=[
            pltpu.VMEM((share, 128), BF16),
            pltpu.SemaphoreType.DMA((3,)),
            one, pltpu.SemaphoreType.DMA((pieces, max(1, geo.chips - 1))),
            one, pltpu.SemaphoreType.DMA((pieces, geo.chips, max(1, geo.cols - 1))),
            one, one,
        ],
        compiler_params=pltpu.CompilerParams(collective_id=1, has_side_effects=True),
    )(in_hbm(qkv), in_hbm(out), router, gain_one, gain_two, terms)


def reduce_kernel(geo, part_ref, out_ref, from_core, from_col, from_chip, pair, column, core_send, core_recv,
                  y_send, y_recv, z_send, z_recv):
    at = Shards(geo)
    at.greet()
    at.await_greetings()
    order = list(range(1, at.chips)) + [0]
    started = []

    def start(copy):
        copy.start()
        started.append(copy)

    def to_core(k):
        return remote(
            part_ref.at[at.row(at.chip(k), 1)], from_core.at[k], core_send.at[k, 0], core_recv.at[k, 0],
            {"row": at.row(at.z, 1)},
        )

    def to_col(k, j):
        return remote(
            pair.at[k, at.col(j)], from_col.at[k, j - 1], y_send.at[k, j - 1], y_recv.at[k, j - 1],
            {"col": at.col(j)},
        )

    def to_chip(k):
        return remote(
            column.at[k - 1], from_chip.at[k - 1], z_send.at[k - 1], z_recv.at[k - 1],
            {"row": at.row(at.chip(k))},
        )

    if at.cores > 1:
        for k in order:
            start(to_core(k))

    def sum_cores(k):
        total = part_ref[at.row(at.chip(k))].astype(F32)
        if at.cores > 1:
            to_core(k).wait_recv()
            total = total + from_core[k].astype(F32)
        pair[k] = total.astype(BF16)
        for j in range(1, at.cols):
            start(to_col(k, j))

    def sum_cols(k):
        total = pair[k, at.c].astype(F32)
        for j in range(1, at.cols):
            to_col(k, j).wait_recv()
            total = total + from_col[k, j - 1].astype(F32)
        if k:
            column[k - 1] = total.astype(BF16)
            start(to_chip(k))
        else:
            out_ref[...] = total

    for step, k in enumerate(order):
        sum_cores(k)
        if step:
            sum_cols(order[step - 1])
    sum_cols(order[-1])
    for k in range(1, at.chips):
        to_chip(k).wait_recv()
        out_ref[...] += from_chip[k - 1].astype(F32)
    for copy in started:
        copy.wait_send()


def reduce_shards(geo, parts):
    chips, z, y, core = shard_sems(geo)
    rows, cols, share, width = parts.shape
    steps = max(1, cols - 1)
    return pl.pallas_call(
        partial(reduce_kernel, geo),
        out_shape=shape((share, width), F32),
        in_specs=[vmem_spec()],
        out_specs=vmem_spec(),
        scratch_shapes=[
            pltpu.VMEM((chips, cols, share, width), BF16),
            pltpu.VMEM((chips, steps, share, width), BF16),
            pltpu.VMEM((max(1, chips - 1), share, width), BF16),
            pltpu.VMEM((chips, cols, share, width), BF16),
            pltpu.VMEM((max(1, chips - 1), share, width), BF16),
            core, core, y, y, z, z,
        ],
        compiler_params=pltpu.CompilerParams(
            vmem_limit_bytes=32 * MIB, collective_id=2, has_side_effects=True
        ),
    )(parts)


def expert_weights_kernel(experts_all, rows, pre, hidden, seen, packed, in_grad, out_grad, qkv, out, router, one, two,
                          terms):
    def product(left, right):
        left, right = (ref[:, 0].reshape(-1, ref.shape[-1]) for ref in (left, right))
        return mm(left, right, (0, 0))

    in_grad[0, 0] = product(rows, pre)
    out_grad[0, 0] = product(hidden, seen)

    @pl.when((pl.program_id(0) == 0) & (pl.program_id(1) == 0))
    def _():
        wide, narrow = qkv.shape[2], out.shape[2]
        qkv[0] = packed[:, :wide]
        out[0] = packed[:, wide : wide + narrow]
        small = packed[:, wide + narrow :]
        router[0] = small[:, :experts_all]
        pick = (iota((8, 128), 0) + experts_all == iota((8, 128), 1)).astype(F32)
        lines = lax.dot_general(
            pick, small, (((1,), (1,)), ((), ())), precision=lax.Precision.HIGHEST, preferred_element_type=F32
        )
        one[...] = lines[0:1]
        two[...] = lines[1:2]
        terms[...] = lines[2:3, : terms.shape[1]]


def expert_weights(geo, state, packed, terms):
    micro, local, count, width, hidden = geo.micro, geo.local_experts, geo.expert_rows, geo.width, geo.hidden
    tile = tile_of(hidden, 768)
    narrow = pl.BlockSpec((micro, 1, count, width), lambda e, f: (0, e, 0, 0))
    wide = pl.BlockSpec((micro, 1, count, tile), lambda e, f: (0, e, 0, f))
    flops = 4 * micro * local * count * width * hidden
    share = packed.shape[0]
    small = [(1, share, 3 * width), (1, share, width), (1, share, geo.experts_all), (1, share), (1, share), (1, terms)]

    def whole(dims):
        return pl.BlockSpec(dims, lambda e, f: (0,) * len(dims))

    return pl.pallas_call(
        partial(expert_weights_kernel, geo.experts_all),
        out_shape=[shape((1, local, width, hidden), F32), shape((1, local, hidden, width), F32)]
        + [shape(dims, F32) for dims in small],
        grid=(local, hidden // tile),
        in_specs=[narrow, wide, wide, narrow, whole(packed.shape)],
        out_specs=[
            pl.BlockSpec((1, 1, width, tile), lambda e, f: (0, e, 0, f)),
            pl.BlockSpec((1, 1, tile, width), lambda e, f: (0, e, f, 0)),
        ]
        + [whole(dims) for dims in small],
        compiler_params=pltpu.CompilerParams(vmem_limit_bytes=48 * MIB),
        cost_estimate=pl.CostEstimate(
            flops=flops, bytes_accessed=8 * local * hidden * width, transcendentals=0
        ),
    )(*(in_hbm(state[name]) for name in ("kept_rows", "kept_pre", "kept_hidden", "kept_seen")), packed)


def norm_backward(values, gain, grad):
    factor = norm_factor(values)
    unit = values * factor
    weighted = grad * gain
    inner = jnp.mean(weighted * unit, axis=-1, keepdims=True)
    return factor * (weighted - unit * inner), jnp.sum(grad * unit, axis=0, keepdims=True)


def dense_backward_loads(geo, m, at, copies):
    width = geo.width
    return dict(
        rest=copies.load(at.packed.at[:, pl.ds(3 * width, width + 128)], at.rest_w),
        residual=copies.load(at.kept_residual.at[m], at.residual),
        qkv=copies.load(at.kept_qkv.at[m], at.qkv),
        prob=copies.load(at.kept_prob.at[m], at.prob),
        stream=copies.load(at.kept_stream.at[m], at.stream),
        qkv_w=copies.load(at.packed.at[:, pl.ds(0, 3 * width)], at.qkv_w),
    )


def dense_backward_part(geo, step, at, copies, loads, enter, across):
    length, width, heads = geo.length, geo.width, geo.heads
    size = width // heads
    per = 128 // size
    m = backward_micro(geo, step)
    send = across is not None
    aux = at.aux[...]
    slope = aux[:, 0:1] * aux[:, 1:2] * (at.gates[:, 0:1] - at.gates[:, 1:2])
    expert_at = iota((length, 128), 1).astype(F32)
    logit_grad = (
        jnp.where(as_column(at.routes[0, m, 0:1, :].astype(F32)) == expert_at, slope, 0.0)
        - jnp.where(as_column(at.routes[0, m, 1:2, :].astype(F32)) == expert_at, slope, 0.0)
    ).astype(BF16)
    at.logit[...] = logit_grad
    copies.save(at.logit, at.kept_logit.at[m])
    loads["rest"].wait()
    moe_grad = at.moe_grad[...] + mm(logit_grad, at.rest_w[:, width:], (1, 1))
    loads["residual"].wait()
    part, gain_two = norm_backward(at.residual[...], at.gains[1:2, :], moe_grad)
    residual_grad = at.incoming[...].astype(F32) + part
    at.branch[...] = residual_grad.astype(BF16)
    copies.save(at.branch, at.kept_branch.at[m])
    at.context_grad[...] = mm(at.branch[...], at.rest_w[:, :width], (1, 1)).astype(BF16)
    which = iota((length, 128), 1) // size
    head_row = iota((128, length), 0) // size
    scale = 1.0 / math.sqrt(size)
    zero = jnp.zeros((length, 128), BF16)
    loads["qkv"].wait()
    loads["prob"].wait()
    at.sums[...] = jnp.zeros(at.sums.shape, F32)
    for j in range(width // 128):
        places = [slice(base * width + 128 * j, base * width + 128 * (j + 1)) for base in range(3)]
        queries, keys, values = (at.qkv[:, place] for place in places)
        grad = at.context_grad[:, places[0]]
        turned_keys = keys.astype(F32).T
        totals = [jnp.zeros(dims, F32) for dims in ((128, length), (length, 128), (length, 128))]
        for part_at in range(per):
            h = j * per + part_at
            own = which == part_at
            own_grad = jnp.where(own, grad, zero)
            prob = at.prob[h]
            prob_grad = mm(values, own_grad, (1, 1))
            weighted = prob.astype(F32)
            shift = jnp.sum(weighted * prob_grad, axis=0, keepdims=True)
            score_grad = (weighted * (prob_grad - shift)).astype(BF16)
            at.sums[h : h + 1, :] = diagonal_sums(score_grad.astype(F32))
            own_keys = jnp.where(head_row == part_at, turned_keys, 0.0).astype(BF16)
            totals[0] = totals[0] + mm(own_keys, score_grad, (1, 0))
            totals[1] = totals[1] + mm(score_grad, jnp.where(own, queries, zero), (1, 0))
            totals[2] = totals[2] + mm(prob, own_grad, (1, 0))
        at.qkv_grad[:, places[0]] = (totals[0].T * scale).astype(BF16)
        at.qkv_grad[:, places[1]] = (totals[1] * scale).astype(BF16)
        at.qkv_grad[:, places[2]] = totals[2].astype(BF16)
    copies.save(at.qkv_grad, at.kept_qkv_grad.at[m])
    copies.save(at.sums, at.kept_sums.at[m])
    loads["qkv_w"].wait()
    normed_grad = mm(at.qkv_grad[...], at.qkv_w[...], (1, 1))
    loads["stream"].wait()
    part, gain_one = norm_backward(at.stream[...].astype(F32), at.gains[0:1, :], normed_grad)
    at.gain_parts[...] = jnp.zeros(at.gain_parts.shape, F32)
    at.gain_parts[0:1, :] = gain_one
    at.gain_parts[1:2, :] = gain_two
    copies.save(at.gain_parts, at.kept_gains.at[m])
    in_grad = residual_grad + part
    at.in_grad_here[...] = in_grad
    copies.save(at.in_grad_here, at.in_grad.at[m])
    if step < geo.micro:
        at.sent_here[...] = in_grad.astype(BF16)
    if send:
        enter()
        across.send(at.sent_here, at.received_out)
    elif step < geo.micro:
        copies.save(at.sent_here, at.sent_out)
    copies.wait()
    if send:
        across.take(at.received_out)
        across.sent(at.sent_here, at.received_out)


def dense_backward_body(geo, step, at):
    send = 1 <= step < geo.micro
    across = Across(1, at.across_sems) if send else None
    if send:
        across.greet()

    def enter():
        pl.semaphore_wait(pltpu.get_barrier_semaphore(), 1)

    m = backward_micro(geo, step)
    copies = Copies(at.sems)
    aux_load = copies.load(at.kept_aux.at[m], at.aux)
    loads = dense_backward_loads(geo, m, at, copies)
    aux_load.wait()
    dense_backward_part(geo, step, at, copies, loads, enter, across)


def dense_backward_scratch(geo):
    length, width, heads = geo.length, geo.width, geo.heads
    return dict(
        aux=pltpu.VMEM((length, 128), F32),
        rest_w=pltpu.VMEM((width, width + 128), BF16),
        qkv_w=pltpu.VMEM((width, 3 * width), BF16),
        residual=pltpu.VMEM((length, width), F32),
        qkv=pltpu.VMEM((length, 3 * width), BF16),
        prob=pltpu.VMEM((heads, length, length), BF16),
        stream=pltpu.VMEM((length, width), BF16),
        logit=pltpu.VMEM((length, 128), BF16),
        branch=pltpu.VMEM((length, width), BF16),
        context_grad=pltpu.VMEM((length, width), BF16),
        qkv_grad=pltpu.VMEM((length, 3 * width), BF16),
        sums=pltpu.VMEM((geo.tall, length), F32),
        gain_parts=pltpu.VMEM((8, width), F32),
        in_grad_here=pltpu.VMEM((length, width), F32),
        sent_here=pltpu.VMEM((length, width), BF16),
        sems=pltpu.SemaphoreType.DMA((20,)),
        across_sems=pltpu.SemaphoreType.DMA((4,)),
    )


def dense_backward_refs(geo, step, given, state):
    micro, length, width = geo.micro, geo.length, geo.width
    outs = {}
    if 1 <= step < micro:
        outs["received_out"] = pltpu.HBM((length, width), BF16)
    elif step < micro:
        outs["sent_out"] = pltpu.HBM((length, width), BF16)
    names = ("kept_aux", "kept_residual", "kept_qkv", "kept_prob", "kept_stream")
    held = dict({name: state[name] for name in names}, packed=given["packed"])
    kept = dict(
        in_grad=((micro, length, width), F32),
        kept_branch=((micro, length, width), BF16),
        kept_qkv_grad=((micro, length, 3 * width), BF16),
        kept_logit=((micro, length, 128), BF16),
        kept_gains=((micro, 8, width), F32),
        kept_sums=((micro, geo.tall, length), F32),
    )
    return dict(routes=given["routes"], gains=given["gains"]), held, outs, kept


def dense_backward(geo, step, near, given, state):
    more, held, outs, kept = dense_backward_refs(geo, step, given, state)
    params = {}
    if 1 <= step < geo.micro:
        params = dict(collective_id=5 + 2 * geo.micro + step, has_side_effects=True)
    return launch(
        partial(where_active, only_section(geo, geo.micro - step), partial(dense_backward_body, geo, step)),
        near=dict(near, **more),
        held=held,
        outs=outs,
        kept=kept,
        state=state,
        scratch=dense_backward_scratch(geo),
        cost=(3_000_000_000, 14_000_000),
        **params,
    )


DENSE_GRADS = ("normed", "qkv_grad", "context", "branch", "moe_in", "logit")


def dense_weights_body(geo, at):
    width = geo.width
    copies = Copies(at.sems)
    loads = {}
    for name in DENSE_GRADS + ("gains", "sums"):
        loads[name] = copies.load(getattr(at, "kept_" + name), getattr(at, name))

    def product(left, right):
        left, right = (ref[...].reshape(-1, ref.shape[-1]) for ref in (left, right))
        return mm(left, right, (0, 0))

    def ready(*names):
        for name in names:
            loads[name].wait()

    ready("normed", "qkv_grad")
    normed = at.normed[...].reshape(-1, width)
    for j in range(0, 3 * width, width):
        grad = at.qkv_grad[:, :, j : j + width].reshape(-1, width)
        at.part[:, j : j + width] = mm(normed, grad, (0, 0)).astype(BF16)
    ready("context", "branch")
    at.part[:, 3 * width : 4 * width] = product(at.context, at.branch).astype(BF16)
    ready("moe_in", "logit", "gains", "sums")
    small = product(at.moe_in, at.logit)
    by_term = lax.dot_general(
        jnp.sum(at.sums[...], axis=0), at.spread[...].astype(F32), (((1,), (1,)), ((), ())),
        precision=lax.Precision.HIGHEST, preferred_element_type=F32,
    )
    bias_row = jnp.sum(by_term[: geo.heads] * at.head_pick[...], axis=0, keepdims=True)
    gain_rows = jnp.sum(at.gains[...], axis=0)
    place = iota((128, width), 0)
    rows = jnp.zeros((128, width), F32)
    for k, row in enumerate((gain_rows[0:1], gain_rows[1:2], bias_row)):
        rows = jnp.where(place == geo.experts_all + k, row, rows)
    at.part[:, 4 * width :] = (small + rows.T).astype(BF16)


def dense_weights(geo, head_pick, spread_table, state):
    held = {"kept_" + name: state["kept_" + name] for name in DENSE_GRADS}
    scratch = {name: pltpu.VMEM(held["kept_" + name].shape, BF16) for name in DENSE_GRADS}
    return launch(
        partial(dense_weights_body, geo),
        near=dict(head_pick=head_pick, spread=spread_table),
        held=dict(held, kept_gains=state["kept_gains"], kept_sums=state["kept_sums"]),
        outs=dict(part=shape((geo.width, 4 * geo.width + 128), BF16)),
        scratch=dict(
            scratch, sems=pltpu.SemaphoreType.DMA((len(DENSE_GRADS) + 2,)),
            gains=pltpu.VMEM(state["kept_gains"].shape, F32), sums=pltpu.VMEM(state["kept_sums"].shape, F32),
        ),
        spare=24,
        cost=(3_000_000_000, 10_000_000),
    )["part"]


def on_device(
    inputs, cotangent, segments, routes, order, attn_gain, qkv_weight, position_bias, out_weight, moe_gain,
    router_weight, expert_in, expert_out,
):
    micro, length, width = inputs.shape
    local_experts, hidden = expert_in.shape[1], expert_in.shape[3]
    experts_all = router_weight.shape[2]
    row_count, col_count = lax.axis_size("row"), lax.axis_size("col")
    devices = row_count * col_count
    share = width // devices
    terms = position_bias.shape[1]
    heads = terms * devices // DISTANCE_BUCKETS
    geo = Geometry(micro, length, width, heads, experts_all, local_experts, hidden, row_count, col_count)
    packed = gather_shards(
        geo, qkv_weight[0], out_weight[0], router_weight[0], attn_gain, moe_gain, position_bias
    ).reshape(width, -1)
    indicator = buckets(length)
    row_at = np.arange(width)
    term_at = np.where(row_at % share < terms, row_at // share * terms + row_at % share, -1)
    head_pick = jnp.asarray((term_at % heads == np.arange(heads)[:, None]) & (term_at >= 0), F32)
    spread_table = jnp.asarray(indicator[np.maximum(term_at, 0) // heads], BF16)
    prepared = launch(
        partial(prepare, experts_all),
        near=dict(small=packed[:, 4 * width :], head_pick=head_pick, spread=spread_table),
        outs=dict(gains=shape((2, width), F32), bias=shape((heads, length, length), BF16)),
        cost=(50_000_000, 6_000_000),
    )
    given = dict(
        prepared, packed=packed, inputs=inputs, cotangent=cotangent, w_in=expert_in[0], w_out=expert_out[0],
        segments=segments, order=order, routes=jnp.swapaxes(routes, 2, 3),
        bases=jnp.asarray(geo.bases()),
    )
    state = {}
    received = None
    for tick in range(micro + 1):
        received = forward_tick(geo, tick, given, state, received)
    sent = received = None
    for step in range(micro + 1):
        passed = backward_step(geo, step, given, state, sent, received)
        sent, received = passed.get("sent_out"), passed.get("received_out")
    part = dense_weights(geo, head_pick, spread_table, state)
    packed = reduce_shards(geo, part.reshape(row_count, col_count, share, -1))
    expert_in_grad, expert_out_grad, qkv, out, router, gain_one, gain_two, bias = expert_weights(
        geo, state, packed, terms
    )
    return (
        state["out"][None], state["in_grad"][None], gain_one, qkv, bias, out, gain_two, router, expert_in_grad,
        expert_out_grad,
    )


def solution(mesh):
    tokens = ("row", "col")
    return jax.shard_map(
        on_device,
        mesh=mesh,
        in_specs=(
            P(None, tokens, None),
            P(None, tokens, None),
            P(None, tokens),
            P("section", None, tokens, None),
            P("section", None, tokens, None),
            P("section", tokens),
            P("section", tokens, None),
            P("section", tokens),
            P("section", tokens, None),
            P("section", tokens),
            P("section", tokens, None),
            P("section", "row", None, "col"),
            P("section", "row", "col", None),
        ),
        out_specs=(
            P("section", None, tokens, None),
            P("section", None, tokens, None),
            P("section", tokens),
            P("section", tokens, None),
            P("section", tokens),
            P("section", tokens, None),
            P("section", tokens),
            P("section", tokens, None),
            P("section", "row", None, "col"),
            P("section", "row", "col", None),
        ),
        check_vma=False,
    )
```

time: 1470 us -> 544 us (0.37)
  Pallas kernels: 0 us -> 527 us
  waiting for transfers between devices: 482 us -> 0 us
  blocking collectives: 285 us -> 0 us
  matrix products: 280 us -> 0 us
  local copies, waits for them, and re-layouts: 216 us -> 6.82 us
  other arithmetic: 131 us -> 0 us
  starting transfers between devices: 41.6 us -> 0 us
  between operations: 20.3 us -> 1.29 us
    pallas_call x0 -> x11, Pallas kernels: none -> 527 us  [the longest x8 409 us: launch(): pl.pallas_call(kernel, out_shape=out_shapes, in_specs=[vmem_spec()] * len...]
    dot_general x65 -> x0, matrix products: 280 us -> none  [the longest x27 49.2 us: matmul(): return jnp.dot(left_side, right_side, preferred_element_type=jnp.float32)]
    reduce_scatter x8 -> x0, waiting for transfers between devices: 228 us -> none  [the longest x3 151 us: layer_forward(): lax.psum_scatter(produced, 'col', scatter_dimension=1, tiled=True)]
    all_to_all x5 -> x0, blocking collectives: 142 us -> none  [the longest x3 83.7 us: layer_backward(): lax.all_to_all(slot_grad, 'row', split_axis=0, concat_axis=2, tiled=True)]
    all_gather x8 -> x0, waiting for transfers between devices: 129 us -> none  [the longest x3 60.4 us: layer_forward(): owner_rows = lax.all_gather(arrived, 'col', axis=1, tiled=True)]
    unnamed x2 -> x0, blocking collectives: 96.8 us -> none
    all_to_all x7 -> x0, waiting for transfers between devices: 88.3 us -> none  [the longest x3 42.6 us: layer_backward(): lax.all_to_all(sent_grad.reshape(1, local_experts, row_count * capacity,...]
    convert_element_type x13 -> x0, other arithmetic: 60.1 us -> none  [the longest x3 55.8 us: layer_forward(): hidden = jax.nn.gelu(hidden_pre, approximate=False).astype(jnp.bfloat16)]
  transfers between devices with their start and end apart: 28 -> 0, of which waited for: 20 -> 0; matrix products, arithmetic and copies ran while one was open for 20% -> 0% of each run, Pallas kernels for 0% -> 0%
where the time goes in v1:
time: 544 us; the launch traced here: 535 us
  Pallas kernels  527 us (97%)
  local copies, waits for them, and re-layouts  6.82 us (1%)
    pallas_call x8, Pallas kernels, launch(): pl.pallas_call(kernel, out_shape=out_shapes, in_specs=[vmem_spec()] * len...  409 us
    pallas_call x1, Pallas kernels, gather_shards(): pl.pallas_call(partial(gather_kernel, geo, pieces), out_shape=pltpu.HBM((...  48.7 us
    pallas_call x1, Pallas kernels, reduce_shards(): pl.pallas_call(partial(reduce_kernel, geo), out_shape=shape((share, width...  39.5 us
    pallas_call x1, Pallas kernels, expert_weights(): pl.pallas_call(partial(expert_weights_kernel, geo.experts_all), out_shape...  29.8 us

profile of v1, /device:TPU:0, one launch (start us, length us, event | category | flops | bytes accessed | tf_op | source)
XLA Modules:
  0.0 535.3 jit_solution(18122774083049445105)
XLA Ops:
  0.6 0.0 copy-start.1
  0.7 0.0 copy-start.3
  0.7 1.4 copy.68
  2.1 48.7 %shard_map.231 = bf16[8,2,48,3200]{3,2,1,0:T(8,128)(2,1)} custom-call(bf16[48,2304]{1,0:T(8,128)(2,1)} %bitcast.32, bf16[48,768]{1,0:T(8,128)(2,1)} %bitcast.39, bf16[48,32]{1,0:T(8,128)(2,1)} %bitcast.40, bf16[1,48]{1,0:T(2,128)(2,1)} %gain_one.1, bf16[1,48]{1,0:T(2,128)(2,1)} %gain_two.1, bf16[1,24]{1,0:T(2,128)(2,1)} %terms.1), custom_call_target="tpu_custom_call" | custom-call | tf_op jit(solution)/shard_map/pallas_call | solution.py:1265
  50.8 0.9 slice.4.refs_0_
  51.8 0.0 copy-done.1
  51.8 0.0 copy-done.3
  51.8 0.8 shard_map.232
  52.7 0.0 copy-start
  52.7 1.1 copy-done
  53.8 0.0 copy-start.2
  53.8 0.6 copy-done.2
  54.4 58.8 %shard_map.233 = (bf16[2,256,768]{2,1,0:T(8,128)(2,1)}, bf16[2,256,768]{2,1,0:T(8,128)(2,1)}, bf16[2,256,2304]{2,1,0:T(8,128)(2,1)}, bf16[2,12,256,256]{3,2,1,0:...) custom-call(s32[2,256]{1,0:T(2,128)} %refs_0_.6, ...), custom_call_target="tpu_custom_call" | custom-call | flops 6039797760 | bytes 18874368 | tf_op jit(solution)/shard_map/pallas_call | solution.py:141
  113.2 72.7 %shard_map.234 = (bf16[256,768]{1,0:T(8,128)(2,1)}, bf16[2,256,768]{2,1,0:T(8,128)(2,1)}, bf16[2,256,768]{2,1,0:T(8,128)(2,1)}, bf16[2,256,2304]{2,1,0:T(8,128)(...) custom-call(s32[2,256]{1,0:T(2,128)} %refs_0_.6, ...), custom_call_target="tpu_custom_call", output_to_operand_aliasing={{1}: (10, {}), {2}: (11, {}), {3}: (12, {}), {4}: (13, {}),... | custom-call | flops 6039797760 | bytes 18874368 | tf_op jit(solution)/shard_map/pallas_call | solution.py:141
  185.9 57.2 %shard_map.235 = (bf16[2,256,768]{2,1,0:T(8,128)(2,1)}, bf16[2,256,768]{2,1,0:T(8,128)(2,1)}, bf16[2,256,2304]{2,1,0:T(8,128)(2,1)}, bf16[2,12,256,256]{3,2,1,0:...) custom-call(s32[2,256]{1,0:T(2,128)} %refs_0_.6, ...), custom_call_target="tpu_custom_call", output_to_operand_aliasing={{0}: (11, {}), {1}: (12, {}), {2}: (13, {}), {3}: (14, {}),... | custom-call | flops 6039797760 | bytes 18874368 | tf_op jit(solution)/shard_map/pallas_call | solution.py:141
  243.1 59.2 %shard_map.236 = (bf16[256,768]{1,0:T(8,128)(2,1)}, f32[2,256,768]{2,1,0:T(8,128)}, bf16[2,256,768]{2,1,0:T(8,128)(2,1)}, bf16[2,256,2304]{2,1,0:T(8,128)(2,1)},...) custom-call(s32[1,2,2,256]{3,2,1,0:T(2,128)} %bitcast.36, ...), custom_call_target="tpu_custom_call" | custom-call | flops 6039797760 | bytes 18874368 | tf_op jit(solution)/shard_map/pallas_call | solution.py:141
  302.3 89.0 %shard_map.237 = (bf16[256,768]{1,0:T(8,128)(2,1)}, f32[2,256,768]{2,1,0:T(8,128)}, bf16[2,256,768]{2,1,0:T(8,128)(2,1)}, bf16[2,256,2304]{2,1,0:T(8,128)(2,1)},...) custom-call(s32[1,2,2,256]{3,2,1,0:T(2,128)} %bitcast.37, ...), custom_call_target="tpu_custom_call", output_to_operand_aliasing={{1}: (14, {}), {2}: (15, {}), {3}: (16, {}), {4}: (17, {}),... | custom-call | flops 6039797760 | bytes 18874368 | tf_op jit(solution)/shard_map/pallas_call | solution.py:141
  391.4 65.1 %shard_map.238 = (f32[2,256,768]{2,1,0:T(8,128)}, bf16[2,256,768]{2,1,0:T(8,128)(2,1)}, bf16[2,256,2304]{2,1,0:T(8,128)(2,1)}, bf16[2,256,128]{2,1,0:T(8,128)(2,...) custom-call(s32[1,2,2,256]{3,2,1,0:T(2,128)} %bitcast.38, ...), custom_call_target="tpu_custom_call", output_to_operand_aliasing={{0}: (14, {}), {1}: (15, {}), {2}: (16, {}), {3}: (17, {}),... | custom-call | flops 6039797760 | bytes 18874368 | tf_op jit(solution)/shard_map/pallas_call | solution.py:141
  456.5 6.3 %shard_map.239 = bf16[768,3200]{1,0:T(8,128)(2,1)S(1)} custom-call(f32[12,768]{1,0:T(8,128)S(1)} %copy-done.3, bf16[768,256]{1,0:T(8,128)(2,1)S(1)} %copy-done.1, bf16[2,256,768]{2,1,0:T(8,128)(2,1)} %get-tuple-element.146.refs_2_, bf16[2,256,2304]{2,1,0:T(8,128)(2,1)} %get-tuple-element.147.refs_3_, bf16[2,256,768]{2,1,0:T(8,128)(2,1)} %get-tuple-element.148.refs_4_, ...), custom_call_target="tpu_custom_call" | custom-call | flops 3000000000 | bytes 10000000 | tf_op jit(solution)/shard_map/pallas_call | solution.py:141
  462.8 39.5 %shard_map.240.packed = f32[48,3200]{1,0:T(8,128)S(1)} custom-call(bf16[8,2,48,3200]{3,2,1,0:T(8,128)(2,1)S(1)} %bitcast.10), custom_call_target="tpu_custom_call" | custom-call | tf_op jit(solution)/shard_map/pallas_call | solution.py:1351
  502.3 0.0 copy-start.5
  502.3 0.0 copy-start.4
  502.3 29.8 %shard_map.241 = (f32[1,4,768,1536]{3,2,1,0:T(8,128)}, f32[1,4,1536,768]{3,2,1,0:T(8,128)}, f32[1,48,2304]{2,1,0:T(8,128)}, f32[1,48,768]{2,1,0:T(8,128)}, f32[1...) custom-call(bf16[2,4,320,768]{3,2,1,0:T(8,128)(2,1)} %get-tuple-element.142.rows, ...), custom_call_target="tpu_custom_call" | custom-call | flops 12079595520 | bytes 37748736 | tf_op jit(solution)/shard_map/pallas_call | solution.py:1407
  532.1 0.7 copy.69
  532.8 0.0 copy-done.5
  532.8 0.9 copy.114
  533.7 0.0 copy-done.4
  533.7 1.1 copy.115
Async XLA Ops:
  0.6 51.1 %copy-start.1 = (bf16[768,256]{1,0:T(8,128)(2,1)S(1)}, bf16[768,256]{1,0:T(8,128)(2,1)}, u32[]{:S(2)}) copy-start(bf16[768,256]{1,0:T(8,128)(2,1)} %constant.7.clone.refs_2_.refs_1_) | copy-start | bytes 1179652
  0.7 51.1 %copy-start.3 = (f32[12,768]{1,0:T(8,128)S(1)}, f32[12,768]{1,0:T(8,128)}, u32[]{:S(2)}) copy-start(f32[12,768]{1,0:T(8,128)} %constant.6.clone.refs_1_.refs_0_) | copy-start | bytes 110596
  52.7 1.1 copy-start
  53.8 0.6 copy-start.2
  502.3 30.5 %copy-start.5 = (bf16[2,256,768]{2,1,0:T(8,128)(2,1)S(1)}, bf16[2,256,768]{2,1,0:T(8,128)(2,1)}, u32[]{:S(2)}) copy-start(bf16[2,256,768]{2,1,0:T(8,128)(2,1)} %get-tuple-element.115) | copy-start | bytes 2359300
  502.3 31.4 %copy-start.4 = (f32[2,256,768]{2,1,0:T(8,128)S(1)}, f32[2,256,768]{2,1,0:T(8,128)}, u32[]{:S(2)}) copy-start(f32[2,256,768]{2,1,0:T(8,128)} %get-tuple-element.141) | copy-start | bytes 4718596

commit v2 on v1

--- a/solution.py
+++ b/solution.py
@@ -234,9 +234,13 @@
 
 
 def prepare(experts_all, at):
-    heads, length = at.bias.shape[:2]
+    heads, length = at.bias_here.shape[:2]
+    width = at.small.shape[0]
+    copies = Copies(at.sems)
+    copies.load(at.packed.at[:, pl.ds(4 * width, 128)], at.small).wait()
     rows = at.small[...].astype(F32).T
-    at.gains[...] = rows[experts_all : experts_all + 2]
+    at.gains_here[0:2, :] = rows[experts_all : experts_all + 2]
+    copies.save(at.gains_here, at.gains)
     picked = (at.head_pick[...] * rows[experts_all + 2 : experts_all + 3]).astype(BF16)
     by_distance = mm(picked, at.spread[...], (1, 0))
     for h in range(heads):
@@ -245,7 +249,9 @@
         while step < length:
             block = jnp.concatenate([block, pltpu.roll(block, step, 1)], axis=0)
             step *= 2
-        at.bias[h] = block.astype(BF16)
+        at.bias_here[h] = block.astype(BF16)
+    copies.save(at.bias_here, at.bias)
+    copies.wait()
 
 
 def diagonal_sums(block):
@@ -273,7 +279,9 @@
     size = width // heads
     per = 128 // size
     m = forward_micro(geo, tick)
-    packed_qkv = copies.load(at.packed.at[:, pl.ds(0, 3 * width)], at.qkv_w)
+    gains_load = copies.load(at.gains, at.gains_here)
+    thirds = [pl.ds(third * width, width) for third in range(3)]
+    packed_qkv = [copies.load(at.packed.at[:, third], at.qkv_w.at[:, third]) for third in thirds]
     if tick == 0:
         copies.load(at.inputs.at[m], at.stream).wait()
     else:
@@ -307,10 +315,12 @@
     bias_load = copies.load(at.bias, at.bias_here)
     copies.save(at.stream, at.kept_stream.at[m])
     stream = at.stream[...].astype(F32)
-    at.normed[...] = (stream * norm_factor(stream) * at.gains[0:1, :]).astype(BF16)
+    gains_load.wait()
+    at.normed[...] = (stream * norm_factor(stream) * at.gains_here[0:1, :]).astype(BF16)
     copies.save(at.normed, at.kept_normed.at[m])
-    packed_qkv.wait()
-    at.qkv[...] = mm(at.normed[...], at.qkv_w[...], (1, 0)).astype(BF16)
+    for third, load in zip(thirds, packed_qkv):
+        load.wait()
+        at.qkv[:, third] = mm(at.normed[...], at.qkv_w[:, third], (1, 0)).astype(BF16)
     copies.save(at.qkv, at.kept_qkv.at[m])
     key_at, query_at = iota((length, length), 0), iota((length, length), 1)
     segments = of_micro(at.segments[...], m).astype(F32)
@@ -345,7 +355,7 @@
     residual = stream + mm(at.context[...], at.rest_w[:, :width], (1, 0))
     at.residual[...] = residual
     copies.save(at.residual, at.kept_residual.at[m])
-    moe_in = (residual * norm_factor(residual) * at.gains[1:2, :]).astype(BF16)
+    moe_in = (residual * norm_factor(residual) * at.gains_here[1:2, :]).astype(BF16)
     at.moe_in[...] = moe_in
     copies.save(at.moe_in, at.kept_moe_in.at[m])
     logits = mm(moe_in, at.rest_w[:, width:], (1, 0))
@@ -408,7 +418,8 @@
         moe_in=pltpu.VMEM((length, width), BF16),
         aux=pltpu.VMEM((length, 128), F32),
         slots=pltpu.VMEM((geo.units, geo.rows, geo.main, width), BF16),
-        sems=pltpu.SemaphoreType.DMA((16 + width // 128,)),
+        gains_here=pltpu.VMEM((8, width), F32),
+        sems=pltpu.SemaphoreType.DMA((20 + width // 128,)),
         stream_sem=pltpu.SemaphoreType.DMA,
         across_sems=pltpu.SemaphoreType.DMA((4,)),
     )
@@ -419,8 +430,8 @@
 
 def dense_forward_refs(geo, tick, given, state, received):
     micro, length, width, heads = geo.micro, geo.length, geo.width, geo.heads
-    near = {name: given[name] for name in ("segments", "order", "routes", "gains", "bases")}
-    held = dict(packed=given["packed"], bias=given["bias"], inputs=given["inputs"])
+    near = {name: given[name] for name in ("segments", "order", "routes", "bases")}
+    held = {name: given[name] for name in ("packed", "bias", "inputs", "gains")}
     if tick > 1:
         held["received"] = received
     kept = dict(
@@ -463,15 +474,20 @@
     return result
 
 
-def spread(incoming, aux, picked_ref, slots):
-    lane = iota((aux.shape[0], 128), 1)
-    gates = jnp.zeros(lane.shape, F32)
+def spread(incoming, aux, slots):
     total = 0.0
     for c, onehot in enumerate(slot_onehots(aux, slots)):
+        total = total + mm(onehot.astype(BF16), (aux[:, c : c + 1] * incoming).astype(BF16), (0, 0))
+    return total.astype(BF16)
+
+
+def gate_gradients(incoming, picked_ref):
+    lane = iota((incoming.shape[0], 128), 1)
+    gates = jnp.zeros(lane.shape, F32)
+    for c in range(TOP):
         gate = jnp.sum(picked_ref[c].astype(F32) * incoming, axis=1, keepdims=True)
         gates = jnp.where(lane == c, gate, gates)
-        total = total + mm(onehot.astype(BF16), (aux[:, c : c + 1] * incoming).astype(BF16), (0, 0))
-    return gates, total.astype(BF16)
+    return gates
 
 
 def expert_picker(geo, e):
@@ -761,11 +777,12 @@
             self.home_in(u).wait_send()
 
 
-def run_experts(geo, exchange, rows, total, shared, loads, expert, saves):
+def run_experts(geo, exchange, rows, total, shared, loads, expert, saves, opened=lambda: None):
     first, count = geo.first, geo.sources * geo.main
     inbox = exchange.at.inbox
     width = inbox.shape[-1]
     exchange.open()
+    opened()
     if first:
         exchange.pass_on(0, True)
     exchange.pass_on(first)
@@ -985,13 +1002,16 @@
                 at.incoming_here[...] = at.incoming_far[...]
 
         of_sections("wait")
-        picked_load.wait()
         aux_load.wait()
-        at.incoming[...] = at.incoming_here[...]
-        gates, slot_grad = spread(at.incoming_here[...].astype(F32), at.aux[...], at.picked, geo.slots)
-        at.gates[...] = gates
+        slot_grad = spread(at.incoming_here[...].astype(F32), at.aux[...], geo.slots)
         at.slot_grad[...] = slot_grad.reshape(at.slot_grad.shape)
-        run_experts(geo, exchange, at.rows, at.total, at.shared, loads, expert, saves)
+
+        def opened():
+            picked_load.wait()
+            at.incoming[...] = at.incoming_here[...]
+            at.gates[...] = gate_gradients(at.incoming_here[...].astype(F32), at.picked)
+
+        run_experts(geo, exchange, at.rows, at.total, at.shared, loads, expert, saves, opened)
         first_slots, second_slots = slot_onehots(at.aux[...], geo.slots)
         home = at.home[...].reshape(geo.slots, geo.width)
         at.moe_grad[...] = mm((first_slots | second_slots).astype(BF16), home, (1, 0))
@@ -1082,7 +1102,7 @@
         kept_slope=((micro, local, rows, hidden), BF16),
     )
     results = launch(
-        partial(forward_body, geo, tick, tile_of(hidden, 512), fused),
+        partial(forward_body, geo, tick, tile_of(hidden, 768), fused),
         near=near,
         held=held,
         outs=dict(received_out=pltpu.HBM((length, width), BF16)) if 1 <= tick < micro else {},
@@ -1129,7 +1149,7 @@
         kept_pre=((micro, local, rows, hidden), BF16),
     )
     results = launch(
-        partial(backward_body, geo, step, tile_of(hidden, 512), fused),
+        partial(backward_body, geo, step, tile_of(hidden, 768), fused),
         near=near,
         held=held,
         outs=outs,
@@ -1181,12 +1201,12 @@
     copies = Copies(own_sems)
     copies.save(qkv, mine.at[:, pl.ds(0, wide)])
     copies.save(out, mine.at[:, pl.ds(wide, narrow)])
-    experts_all, count = router.shape[1], terms.shape[1]
+    experts_all, count = router.shape[0], terms.shape[1]
 
     def unit(dims, shift=0):
         return (iota(dims, 0) + shift == iota(dims, 1)).astype(BF16)
 
-    columns = mm(router[...], unit((experts_all, 128)), (1, 0))
+    columns = mm(router[...], unit((experts_all, 128)), (0, 0))
     long_terms = mm(terms[...], unit((count, share)), (1, 0)).astype(BF16)
     for k, row in enumerate((gain_one[...], gain_two[...], long_terms)):
         columns = columns + mm(row, unit((1, 128), experts_all + k), (0, 0))
@@ -1250,14 +1270,6 @@
         left(all_ref.at[pl.ds(0, at.chips), pl.ds(0, at.cols - 1)], y_send)
 
 
-def shard_sems(geo):
-    chips = geo.chips
-    z = pltpu.SemaphoreType.DMA((max(1, chips - 1),))
-    y = pltpu.SemaphoreType.DMA((chips, max(1, geo.cols - 1)))
-    core = pltpu.SemaphoreType.DMA((chips, geo.cols))
-    return chips, z, y, core
-
-
 def gather_shards(geo, qkv, out, router, gain_one, gain_two, terms):
     share, total = qkv.shape[0], qkv.shape[1] + out.shape[1] + 128
     pieces = 5 if total % 640 == 0 else 1
@@ -1278,11 +1290,13 @@
     )(in_hbm(qkv), in_hbm(out), router, gain_one, gain_two, terms)
 
 
-def reduce_kernel(geo, part_ref, out_ref, from_core, from_col, from_chip, pair, column, core_send, core_recv,
-                  y_send, y_recv, z_send, z_recv):
-    at = Shards(geo)
-    at.greet()
-    at.await_greetings()
+def reduce_part(shards, refs):
+    at = shards
+    part_ref, out_ref = refs.part, refs.shard
+    from_core, from_col, from_chip, pair, column = refs.from_core, refs.from_col, refs.from_chip, refs.pair, refs.column
+    core_send, core_recv, y_send, y_recv, z_send, z_recv = (
+        refs.core_send, refs.core_recv, refs.y_send, refs.y_recv, refs.z_send, refs.z_recv
+    )
     order = list(range(1, at.chips)) + [0]
     started = []
 
@@ -1344,27 +1358,19 @@
         copy.wait_send()
 
 
-def reduce_shards(geo, parts):
-    chips, z, y, core = shard_sems(geo)
-    rows, cols, share, width = parts.shape
-    steps = max(1, cols - 1)
-    return pl.pallas_call(
-        partial(reduce_kernel, geo),
-        out_shape=shape((share, width), F32),
-        in_specs=[vmem_spec()],
-        out_specs=vmem_spec(),
-        scratch_shapes=[
-            pltpu.VMEM((chips, cols, share, width), BF16),
-            pltpu.VMEM((chips, steps, share, width), BF16),
-            pltpu.VMEM((max(1, chips - 1), share, width), BF16),
-            pltpu.VMEM((chips, cols, share, width), BF16),
-            pltpu.VMEM((max(1, chips - 1), share, width), BF16),
-            core, core, y, y, z, z,
-        ],
-        compiler_params=pltpu.CompilerParams(
-            vmem_limit_bytes=32 * MIB, collective_id=2, has_side_effects=True
-        ),
-    )(parts)
+def reduce_scratch(geo, share, width):
+    chips, steps, far = geo.chips, max(1, geo.cols - 1), max(1, geo.chips - 1)
+    z = pltpu.SemaphoreType.DMA((far,))
+    y = pltpu.SemaphoreType.DMA((chips, steps))
+    core = pltpu.SemaphoreType.DMA((chips, geo.cols))
+    return dict(
+        from_core=pltpu.VMEM((chips, geo.cols, share, width), BF16),
+        from_col=pltpu.VMEM((chips, steps, share, width), BF16),
+        from_chip=pltpu.VMEM((far, share, width), BF16),
+        pair=pltpu.VMEM((chips, geo.cols, share, width), BF16),
+        column=pltpu.VMEM((far, share, width), BF16),
+        core_send=core, core_recv=core, y_send=y, y_recv=y, z_send=z, z_recv=z,
+    )
 
 
 def expert_weights_kernel(experts_all, rows, pre, hidden, seen, packed, in_grad, out_grad, qkv, out, router, one, two,
@@ -1382,14 +1388,15 @@
         qkv[0] = packed[:, :wide]
         out[0] = packed[:, wide : wide + narrow]
         small = packed[:, wide + narrow :]
-        router[0] = small[:, :experts_all]
-        pick = (iota((8, 128), 0) + experts_all == iota((8, 128), 1)).astype(F32)
+        dims = (experts_all + 8, 128)
+        pick = (iota(dims, 0) == iota(dims, 1)).astype(F32)
         lines = lax.dot_general(
             pick, small, (((1,), (1,)), ((), ())), precision=lax.Precision.HIGHEST, preferred_element_type=F32
         )
-        one[...] = lines[0:1]
-        two[...] = lines[1:2]
-        terms[...] = lines[2:3, : terms.shape[1]]
+        router[0] = lines[:experts_all]
+        one[...] = lines[experts_all : experts_all + 1]
+        two[...] = lines[experts_all + 1 : experts_all + 2]
+        terms[...] = lines[experts_all + 2 : experts_all + 3, : terms.shape[1]]
 
 
 def expert_weights(geo, state, packed, terms):
@@ -1399,7 +1406,7 @@
     wide = pl.BlockSpec((micro, 1, count, tile), lambda e, f: (0, e, 0, f))
     flops = 4 * micro * local * count * width * hidden
     share = packed.shape[0]
-    small = [(1, share, 3 * width), (1, share, width), (1, share, geo.experts_all), (1, share), (1, share), (1, terms)]
+    small = [(1, share, 3 * width), (1, share, width), (1, geo.experts_all, share), (1, share), (1, share), (1, terms)]
 
     def whole(dims):
         return pl.BlockSpec(dims, lambda e, f: (0,) * len(dims))
@@ -1434,6 +1441,7 @@
     width = geo.width
     return dict(
         rest=copies.load(at.packed.at[:, pl.ds(3 * width, width + 128)], at.rest_w),
+        gains=copies.load(at.gains, at.gains_here),
         residual=copies.load(at.kept_residual.at[m], at.residual),
         qkv=copies.load(at.kept_qkv.at[m], at.qkv),
         prob=copies.load(at.kept_prob.at[m], at.prob),
@@ -1460,7 +1468,8 @@
     loads["rest"].wait()
     moe_grad = at.moe_grad[...] + mm(logit_grad, at.rest_w[:, width:], (1, 1))
     loads["residual"].wait()
-    part, gain_two = norm_backward(at.residual[...], at.gains[1:2, :], moe_grad)
+    loads["gains"].wait()
+    part, gain_two = norm_backward(at.residual[...], at.gains_here[1:2, :], moe_grad)
     residual_grad = at.incoming[...].astype(F32) + part
     at.branch[...] = residual_grad.astype(BF16)
     copies.save(at.branch, at.kept_branch.at[m])
@@ -1500,7 +1509,7 @@
     loads["qkv_w"].wait()
     normed_grad = mm(at.qkv_grad[...], at.qkv_w[...], (1, 1))
     loads["stream"].wait()
-    part, gain_one = norm_backward(at.stream[...].astype(F32), at.gains[0:1, :], normed_grad)
+    part, gain_one = norm_backward(at.stream[...].astype(F32), at.gains_here[0:1, :], normed_grad)
     at.gain_parts[...] = jnp.zeros(at.gain_parts.shape, F32)
     at.gain_parts[0:1, :] = gain_one
     at.gain_parts[1:2, :] = gain_two
@@ -1555,6 +1564,7 @@
         sums=pltpu.VMEM((geo.tall, length), F32),
         gain_parts=pltpu.VMEM((8, width), F32),
         in_grad_here=pltpu.VMEM((length, width), F32),
+        gains_here=pltpu.VMEM((8, width), F32),
         sent_here=pltpu.VMEM((length, width), BF16),
         sems=pltpu.SemaphoreType.DMA((20,)),
         across_sems=pltpu.SemaphoreType.DMA((4,)),
@@ -1569,7 +1579,7 @@
     elif step < micro:
         outs["sent_out"] = pltpu.HBM((length, width), BF16)
     names = ("kept_aux", "kept_residual", "kept_qkv", "kept_prob", "kept_stream")
-    held = dict({name: state[name] for name in names}, packed=given["packed"])
+    held = dict({name: state[name] for name in names}, packed=given["packed"], gains=given["gains"])
     kept = dict(
         in_grad=((micro, length, width), F32),
         kept_branch=((micro, length, width), BF16),
@@ -1578,7 +1588,7 @@
         kept_gains=((micro, 8, width), F32),
         kept_sums=((micro, geo.tall, length), F32),
     )
-    return dict(routes=given["routes"], gains=given["gains"]), held, outs, kept
+    return dict(routes=given["routes"]), held, outs, kept
 
 
 def dense_backward(geo, step, near, given, state):
@@ -1617,13 +1627,20 @@
         for name in names:
             loads[name].wait()
 
+    def put(places, block):
+        block = block.astype(BF16)
+        if len(at.part.shape) == 4:
+            at.part[:, :, :, places] = block.reshape(at.part.shape[:3] + block.shape[1:])
+        else:
+            at.part[:, places] = block
+
     ready("normed", "qkv_grad")
     normed = at.normed[...].reshape(-1, width)
     for j in range(0, 3 * width, width):
         grad = at.qkv_grad[:, :, j : j + width].reshape(-1, width)
-        at.part[:, j : j + width] = mm(normed, grad, (0, 0)).astype(BF16)
+        put(slice(j, j + width), mm(normed, grad, (0, 0)))
     ready("context", "branch")
-    at.part[:, 3 * width : 4 * width] = product(at.context, at.branch).astype(BF16)
+    put(slice(3 * width, 4 * width), product(at.context, at.branch))
     ready("moe_in", "logit", "gains", "sums")
     small = product(at.moe_in, at.logit)
     by_term = lax.dot_general(
@@ -1636,24 +1653,59 @@
     rows = jnp.zeros((128, width), F32)
     for k, row in enumerate((gain_rows[0:1], gain_rows[1:2], bias_row)):
         rows = jnp.where(place == geo.experts_all + k, row, rows)
-    at.part[:, 4 * width :] = (small + rows.T).astype(BF16)
+    put(slice(4 * width, None), small + rows.T)
+
+
+def reduce_body(geo, at):
+    shards = Shards(geo)
+    shards.greet()
+    dense_weights_body(geo, at)
+    shards.await_greetings()
+    reduce_part(shards, at)
 
 
 def dense_weights(geo, head_pick, spread_table, state):
-    held = {"kept_" + name: state["kept_" + name] for name in DENSE_GRADS}
+    held = {"kept_" + name: state["kept_" + name] for name in DENSE_GRADS + ("gains", "sums")}
     scratch = {name: pltpu.VMEM(held["kept_" + name].shape, BF16) for name in DENSE_GRADS}
-    return launch(
-        partial(dense_weights_body, geo),
+    scratch.update(
+        sems=pltpu.SemaphoreType.DMA((len(DENSE_GRADS) + 2,)),
+        gains=pltpu.VMEM(state["kept_gains"].shape, F32), sums=pltpu.VMEM(state["kept_sums"].shape, F32),
+    )
+    share, total = geo.width // geo.sources, 4 * geo.width + 128
+    parts = (geo.rows, geo.cols, share, total)
+    fused = share % 16 == 0
+    outs = dict(shard=shape((share, total), F32)) if fused else dict(part=shape((geo.width, total), BF16))
+    params = {}
+    if fused:
+        scratch.update(reduce_scratch(geo, share, total), part=pltpu.VMEM(parts, BF16))
+        params = dict(collective_id=2, has_side_effects=True)
+    results = launch(
+        partial(reduce_body if fused else dense_weights_body, geo),
         near=dict(head_pick=head_pick, spread=spread_table),
-        held=dict(held, kept_gains=state["kept_gains"], kept_sums=state["kept_sums"]),
-        outs=dict(part=shape((geo.width, 4 * geo.width + 128), BF16)),
-        scratch=dict(
-            scratch, sems=pltpu.SemaphoreType.DMA((len(DENSE_GRADS) + 2,)),
-            gains=pltpu.VMEM(state["kept_gains"].shape, F32), sums=pltpu.VMEM(state["kept_sums"].shape, F32),
-        ),
+        held=held,
+        outs=outs,
+        scratch=scratch,
         spare=24,
         cost=(3_000_000_000, 10_000_000),
-    )["part"]
+        **params,
+    )
+    if fused:
+        return results["shard"]
+
+    def body(at):
+        shards = Shards(geo)
+        shards.greet()
+        shards.await_greetings()
+        reduce_part(shards, at)
+
+    return launch(
+        body,
+        near=dict(part=results["part"].reshape(parts)),
+        outs=dict(shard=shape((share, total), F32)),
+        scratch=reduce_scratch(geo, share, total),
+        collective_id=2,
+        has_side_effects=True,
+    )["shard"]
 
 
 def on_device(
@@ -1670,7 +1722,7 @@
     heads = terms * devices // DISTANCE_BUCKETS
     geo = Geometry(micro, length, width, heads, experts_all, local_experts, hidden, row_count, col_count)
     packed = gather_shards(
-        geo, qkv_weight[0], out_weight[0], router_weight[0], attn_gain, moe_gain, position_bias
+        geo, qkv_weight[0], out_weight[0], router_weight[0].T, attn_gain, moe_gain, position_bias
     ).reshape(width, -1)
     indicator = buckets(length)
     row_at = np.arange(width)
@@ -1679,8 +1731,13 @@
     spread_table = jnp.asarray(indicator[np.maximum(term_at, 0) // heads], BF16)
     prepared = launch(
         partial(prepare, experts_all),
-        near=dict(small=packed[:, 4 * width :], head_pick=head_pick, spread=spread_table),
-        outs=dict(gains=shape((2, width), F32), bias=shape((heads, length, length), BF16)),
+        near=dict(head_pick=head_pick, spread=spread_table),
+        held=dict(packed=packed),
+        outs=dict(gains=pltpu.HBM((8, width), F32), bias=pltpu.HBM((heads, length, length), BF16)),
+        scratch=dict(
+            small=pltpu.VMEM((width, 128), BF16), gains_here=pltpu.VMEM((8, width), F32),
+            bias_here=pltpu.VMEM((heads, length, length), BF16), sems=pltpu.SemaphoreType.DMA((3,)),
+        ),
         cost=(50_000_000, 6_000_000),
     )
     given = dict(
@@ -1696,13 +1753,13 @@
     for step in range(micro + 1):
         passed = backward_step(geo, step, given, state, sent, received)
         sent, received = passed.get("sent_out"), passed.get("received_out")
-    part = dense_weights(geo, head_pick, spread_table, state)
-    packed = reduce_shards(geo, part.reshape(row_count, col_count, share, -1))
+    packed = dense_weights(geo, head_pick, spread_table, state)
     expert_in_grad, expert_out_grad, qkv, out, router, gain_one, gain_two, bias = expert_weights(
         geo, state, packed, terms
     )
     return (
-        state["out"][None], state["in_grad"][None], gain_one, qkv, bias, out, gain_two, router, expert_in_grad,
+        state["out"][None], state["in_grad"][None], gain_one, qkv, bias, out, gain_two,
+        jnp.swapaxes(router, 1, 2), expert_in_grad,
         expert_out_grad,
     )
 

time: 544 us -> 539 us (level)
    pallas_call x1 -> x0, Pallas kernels: 39.5 us -> none  [reduce_shards(): pl.pallas_call(partial(reduce_kernel, geo), out_shape=shape((share, width...]
    pallas_call x8, Pallas kernels: 409 us -> 448 us  [launch(): pl.pallas_call(kernel, out_shape=out_shapes, in_specs=[vmem_spec()] * len...]
where the time goes in v2:
time: 539 us; the launch traced here: 531 us
  Pallas kernels  527 us (98%)
    pallas_call x8, Pallas kernels, launch(): pl.pallas_call(kernel, out_shape=out_shapes, in_specs=[vmem_spec()] * len...  448 us
    pallas_call x1, Pallas kernels, gather_shards(): pl.pallas_call(partial(gather_kernel, geo, pieces), out_shape=pltpu.HBM((...  48.8 us
    pallas_call x1, Pallas kernels, expert_weights(): pl.pallas_call(partial(expert_weights_kernel, geo.experts_all), out_shape...  29.9 us

profile of v2, /device:TPU:0, one launch (start us, length us, event | category | flops | bytes accessed | tf_op | source)
XLA Modules:
  0.0 530.5 jit_solution(1558276780909342366)
XLA Ops:
  0.6 0.0 copy-start
  0.7 0.0 copy-start.1
  0.7 48.8 %shard_map.231 = bf16[8,2,48,3200]{3,2,1,0:T(8,128)(2,1)} custom-call(bf16[48,2304]{1,0:T(8,128)(2,1)} %bitcast.33, bf16[48,768]{1,0:T(8,128)(2,1)} %bitcast.40, bf16[32,48]{1,0:T(8,128)(2,1)} %bitcast.41, bf16[1,48]{1,0:T(2,128)(2,1)} %gain_one.1, bf16[1,48]{1,0:T(2,128)(2,1)} %gain_two.1, bf16[1,24]{1,0:T(2,128)(2,1)} %terms.1), custom_call_target="tpu_custom_call" | custom-call | tf_op jit(solution)/shard_map/pallas_call | solution.py:1277
  49.5 0.0 copy-done
  49.5 0.0 copy-done.1
  49.5 2.9 shard_map.232
  52.4 59.2 %shard_map.233 = (bf16[2,256,768]{2,1,0:T(8,128)(2,1)}, bf16[2,256,768]{2,1,0:T(8,128)(2,1)}, bf16[2,256,2304]{2,1,0:T(8,128)(2,1)}, bf16[2,12,256,256]{3,2,1,0:...) custom-call(s32[2,256]{1,0:T(2,128)} %refs_0_.7, ...), custom_call_target="tpu_custom_call" | custom-call | flops 6039797760 | bytes 18874368 | tf_op jit(solution)/shard_map/pallas_call | solution.py:141
  111.6 71.3 %shard_map.234 = (bf16[256,768]{1,0:T(8,128)(2,1)}, bf16[2,256,768]{2,1,0:T(8,128)(2,1)}, bf16[2,256,768]{2,1,0:T(8,128)(2,1)}, bf16[2,256,2304]{2,1,0:T(8,128)(...) custom-call(s32[2,256]{1,0:T(2,128)} %refs_0_.7, ...), custom_call_target="tpu_custom_call", output_to_operand_aliasing={{1}: (10, {}), {2}: (11, {}), {3}: (12, {}), {4}: (13, {}),... | custom-call | flops 6039797760 | bytes 18874368 | tf_op jit(solution)/shard_map/pallas_call | solution.py:141
  182.9 57.3 %shard_map.235 = (bf16[2,256,768]{2,1,0:T(8,128)(2,1)}, bf16[2,256,768]{2,1,0:T(8,128)(2,1)}, bf16[2,256,2304]{2,1,0:T(8,128)(2,1)}, bf16[2,12,256,256]{3,2,1,0:...) custom-call(s32[2,256]{1,0:T(2,128)} %refs_0_.7, ...), custom_call_target="tpu_custom_call", output_to_operand_aliasing={{0}: (11, {}), {1}: (12, {}), {2}: (13, {}), {3}: (14, {}),... | custom-call | flops 6039797760 | bytes 18874368 | tf_op jit(solution)/shard_map/pallas_call | solution.py:141
  240.3 58.1 %shard_map.236 = (bf16[256,768]{1,0:T(8,128)(2,1)}, f32[2,256,768]{2,1,0:T(8,128)}, bf16[2,256,768]{2,1,0:T(8,128)(2,1)}, bf16[2,256,2304]{2,1,0:T(8,128)(2,1)},...) custom-call(s32[1,2,2,256]{3,2,1,0:T(2,128)} %bitcast.37, ...), custom_call_target="tpu_custom_call" | custom-call | flops 6039797760 | bytes 18874368 | tf_op jit(solution)/shard_map/pallas_call | solution.py:141
  298.4 89.8 %shard_map.237 = (bf16[256,768]{1,0:T(8,128)(2,1)}, f32[2,256,768]{2,1,0:T(8,128)}, bf16[2,256,768]{2,1,0:T(8,128)(2,1)}, bf16[2,256,2304]{2,1,0:T(8,128)(2,1)},...) custom-call(s32[1,2,2,256]{3,2,1,0:T(2,128)} %bitcast.38, ...), custom_call_target="tpu_custom_call", output_to_operand_aliasing={{1}: (14, {}), {2}: (15, {}), {3}: (16, {}), {4}: (17, {}),... | custom-call | flops 6039797760 | bytes 18874368 | tf_op jit(solution)/shard_map/pallas_call | solution.py:141
  388.2 63.9 %shard_map.238 = (f32[2,256,768]{2,1,0:T(8,128)}, bf16[2,256,768]{2,1,0:T(8,128)(2,1)}, bf16[2,256,2304]{2,1,0:T(8,128)(2,1)}, bf16[2,256,128]{2,1,0:T(8,128)(2,...) custom-call(s32[1,2,2,256]{3,2,1,0:T(2,128)} %bitcast.39, ...), custom_call_target="tpu_custom_call", output_to_operand_aliasing={{0}: (14, {}), {1}: (15, {}), {2}: (16, {}), {3}: (17, {}),... | custom-call | flops 6039797760 | bytes 18874368 | tf_op jit(solution)/shard_map/pallas_call | solution.py:141
  452.1 45.9 %shard_map.239.packed = f32[48,3200]{1,0:T(8,128)S(1)} custom-call(f32[12,768]{1,0:T(8,128)S(1)} %copy-done.1, bf16[768,256]{1,0:T(8,128)(2,1)S(1)} %copy-done, bf16[2,256,768]{2,1,0:T(8,128)(2,1)} %get-tuple-element.146.refs_2_, bf16[2,256,2304]{2,1,0:T(8,128)(2,1)} %get-tuple-element.147.refs_3_, bf16[2,256,768]{2,1,0:T(8,128)(2,1)} %get-tuple-element.148.refs_4_, ...), custom_call_target="tpu_custom_call" | custom-call | flops 3000000000 | bytes 10000000 | tf_op jit(solution)/shard_map/pallas_call | solution.py:141
  498.0 0.0 copy-start.3
  498.0 0.0 copy-start.2
  498.0 29.9 %shard_map.240 = (f32[1,4,768,1536]{3,2,1,0:T(8,128)}, f32[1,4,1536,768]{3,2,1,0:T(8,128)}, f32[1,48,2304]{2,1,0:T(8,128)}, f32[1,48,768]{2,1,0:T(8,128)}, f32[1...) custom-call(bf16[2,4,320,768]{3,2,1,0:T(8,128)(2,1)} %get-tuple-element.142.rows, ...), custom_call_target="tpu_custom_call" | custom-call | flops 12079595520 | bytes 37748736 | tf_op jit(solution)/shard_map/pallas_call | solution.py:1414
  528.0 0.0 copy-done.3
  528.0 0.9 copy.112
  528.9 0.0 copy-done.2
  528.9 1.1 copy.113
Async XLA Ops:
  0.6 48.8 %copy-start = (bf16[768,256]{1,0:T(8,128)(2,1)S(1)}, bf16[768,256]{1,0:T(8,128)(2,1)}, u32[]{:S(2)}) copy-start(bf16[768,256]{1,0:T(8,128)(2,1)} %constant.7.clone.refs_1_) | copy-start | bytes 1179652
  0.7 48.8 %copy-start.1 = (f32[12,768]{1,0:T(8,128)S(1)}, f32[12,768]{1,0:T(8,128)}, u32[]{:S(2)}) copy-start(f32[12,768]{1,0:T(8,128)} %constant.6.clone.refs_0_) | copy-start | bytes 110596
  498.0 30.0 %copy-start.3 = (bf16[2,256,768]{2,1,0:T(8,128)(2,1)S(1)}, bf16[2,256,768]{2,1,0:T(8,128)(2,1)}, u32[]{:S(2)}) copy-start(bf16[2,256,768]{2,1,0:T(8,128)(2,1)} %get-tuple-element.115) | copy-start | bytes 2359300
  498.0 30.9 %copy-start.2 = (f32[2,256,768]{2,1,0:T(8,128)S(1)}, f32[2,256,768]{2,1,0:T(8,128)}, u32[]{:S(2)}) copy-start(f32[2,256,768]{2,1,0:T(8,128)} %get-tuple-element.141) | copy-start | bytes 4718596

commit v3 on v2

--- a/solution.py
+++ b/solution.py
@@ -347,8 +347,7 @@
             own_values = jnp.where(head_row == part, turned_values, 0.0).astype(BF16)
             context = context + mm(own_values, prob, (1, 0))
         at.context[:, 128 * j : 128 * (j + 1)] = context.T.astype(BF16)
-        heads_here = pl.ds(j * per, per)
-        copies.save(at.prob.at[heads_here], at.kept_prob.at[m, heads_here])
+    copies.save(at.prob, at.kept_prob.at[m])
     copies.save(at.context, at.kept_context.at[m])
     packed_rest.wait()
     loaded()
@@ -509,7 +508,8 @@
         self.partner = self.z * geo.cores + (self.core + 1) % geo.cores
 
     def far(self, direct):
-        return [k for k in range(1, self.geo.chips) if direct or k != self.relay]
+        chips = sorted(range(1, self.geo.chips), key=lambda k: abs(2 * k - self.geo.chips))
+        return [k for k in chips if direct or k != self.relay]
 
     def far_rows(self, direct):
         return self.geo.cores * len(self.far(direct))
@@ -647,15 +647,14 @@
             for j in range(1, self.geo.cols):
                 remote(
                     self.at.inbox.at[u, self.col(j), self.rows(k)], self.at.arrived.at[u, j - 1, self.rows(k)],
-                    self.at.out_send.at[self.kind(u)], self.at.out_recv.at[u, int(far)], {"col": self.col(j)},
+                    self.at.out_send.at[self.kind(u)], self.at.out_recv.at[u, k], {"col": self.col(j)},
                 ).start()
 
     def send_home(self, u, far, direct=False):
-        count = self.far_rows(direct) if far else self.near_rows
-        if self.peers and count:
-            self.came(self.at.arrived.at[u, :, pl.ds(0, count)], self.at.out_recv.at[u, int(far)])
         for k in self.far(direct) if far else (0,):
             rows = self.rows(k)
+            if self.peers:
+                self.came(self.at.arrived.at[u, :, rows], self.at.out_recv.at[u, k])
             total = self.at.inbox[u, self.c, rows].astype(F32)
             for j in range(1, self.geo.cols):
                 total = total + self.at.arrived[u, j - 1, rows].astype(F32)
@@ -832,12 +831,15 @@
     if first:
         inbox[0] = shared[...].astype(BF16).reshape(inbox.shape[1:])
         exchange.send_parts(0, True, True)
-    for u in range(geo.units):
-        if not exchange.relay or u < first or u == geo.units - 1:
-            exchange.send_parts(u, False)
+    near = [u for u in range(geo.units) if not exchange.relay or u < first or u == geo.units - 1]
+    half = len(near) // 2
     exchange.send_home(geo.units - 1, True)
+    for u in near[half:]:
+        exchange.send_parts(u, False)
     if first:
         exchange.send_home(0, True, True)
+    for u in near[:half]:
+        exchange.send_parts(u, False)
     exchange.each(lambda u: exchange.send_home(u, False))
     for e in range(max(0, geo.local_experts - 2), geo.local_experts):
         for copy in saves(e, e % 2):
@@ -1060,7 +1062,7 @@
         in_send=two, out_send=two, home_send=two, home_recv=two, home_in_recv=one, via_send=one, via_part_send=one,
         done=one,
         in_recv=pltpu.SemaphoreType.DMA((geo.units, geo.chips)),
-        out_recv=pltpu.SemaphoreType.DMA((geo.units, 2)),
+        out_recv=pltpu.SemaphoreType.DMA((geo.units, geo.chips)),
         load_sem=pltpu.SemaphoreType.DMA((local, 3)),
         save_sem=pltpu.SemaphoreType.DMA((2, 3)),
         sems=pltpu.SemaphoreType.DMA((6,)),
@@ -1245,8 +1247,10 @@
                 came(block(k, j, h), y_recv.at[h, k, j - 1])
                 pass_core(k, j, h)
 
-    for k in range(1, at.chips):
-        pass_z(k, 0)
+    ahead = min(2, pieces)
+    for h in range(ahead):
+        for k in range(1, at.chips):
+            pass_z(k, h)
     for h in range(pieces):
         pass_y(0, h)
     for h in range(pieces):
@@ -1254,8 +1258,8 @@
     for h in range(pieces):
         for k in range(1, at.chips):
             came(block(k, 0, h), z_recv.at[h, k - 1])
-            if h + 1 < pieces:
-                pass_z(k, h + 1)
+            if h + ahead < pieces:
+                pass_z(k, h + ahead)
             pass_y(k, h)
             pass_core(k, 0, h)
         if h:

time: 539 us -> 538 us (level)
  no operation moved by 1% of the time
where the time goes in v3:
time: 538 us; the launch traced here: 529 us
  Pallas kernels  526 us (98%)
    pallas_call x8, Pallas kernels, launch(): pl.pallas_call(kernel, out_shape=out_shapes, in_specs=[vmem_spec()] * len...  447 us
    pallas_call x1, Pallas kernels, gather_shards(): pl.pallas_call(partial(gather_kernel, geo, pieces), out_shape=pltpu.HBM((...  48.7 us
    pallas_call x1, Pallas kernels, expert_weights(): pl.pallas_call(partial(expert_weights_kernel, geo.experts_all), out_shape...  29.9 us

profile of v3, /device:TPU:0, one launch (start us, length us, event | category | flops | bytes accessed | tf_op | source)
XLA Modules:
  0.0 529.0 jit_solution(7443970470772708402)
XLA Ops:
  0.6 0.0 copy-start
  0.7 0.0 copy-start.1
  0.7 48.7 %shard_map.231 = bf16[8,2,48,3200]{3,2,1,0:T(8,128)(2,1)} custom-call(bf16[48,2304]{1,0:T(8,128)(2,1)} %bitcast.33, bf16[48,768]{1,0:T(8,128)(2,1)} %bitcast.40, bf16[32,48]{1,0:T(8,128)(2,1)} %bitcast.41, bf16[1,48]{1,0:T(2,128)(2,1)} %gain_one.1, bf16[1,48]{1,0:T(2,128)(2,1)} %gain_two.1, bf16[1,24]{1,0:T(2,128)(2,1)} %terms.1), custom_call_target="tpu_custom_call" | custom-call | tf_op jit(solution)/shard_map/pallas_call | solution.py:1281
  49.4 0.0 copy-done
  49.4 0.0 copy-done.1
  49.4 2.9 shard_map.232
  52.3 57.1 %shard_map.233 = (bf16[2,256,768]{2,1,0:T(8,128)(2,1)}, bf16[2,256,768]{2,1,0:T(8,128)(2,1)}, bf16[2,256,2304]{2,1,0:T(8,128)(2,1)}, bf16[2,12,256,256]{3,2,1,0:...) custom-call(s32[2,256]{1,0:T(2,128)} %refs_0_.7, ...), custom_call_target="tpu_custom_call" | custom-call | flops 6039797760 | bytes 18874368 | tf_op jit(solution)/shard_map/pallas_call | solution.py:141
  109.4 73.2 %shard_map.234 = (bf16[256,768]{1,0:T(8,128)(2,1)}, bf16[2,256,768]{2,1,0:T(8,128)(2,1)}, bf16[2,256,768]{2,1,0:T(8,128)(2,1)}, bf16[2,256,2304]{2,1,0:T(8,128)(...) custom-call(s32[2,256]{1,0:T(2,128)} %refs_0_.7, ...), custom_call_target="tpu_custom_call", output_to_operand_aliasing={{1}: (10, {}), {2}: (11, {}), {3}: (12, {}), {4}: (13, {}),... | custom-call | flops 6039797760 | bytes 18874368 | tf_op jit(solution)/shard_map/pallas_call | solution.py:141
  182.7 56.9 %shard_map.235 = (bf16[2,256,768]{2,1,0:T(8,128)(2,1)}, bf16[2,256,768]{2,1,0:T(8,128)(2,1)}, bf16[2,256,2304]{2,1,0:T(8,128)(2,1)}, bf16[2,12,256,256]{3,2,1,0:...) custom-call(s32[2,256]{1,0:T(2,128)} %refs_0_.7, ...), custom_call_target="tpu_custom_call", output_to_operand_aliasing={{0}: (11, {}), {1}: (12, {}), {2}: (13, {}), {3}: (14, {}),... | custom-call | flops 6039797760 | bytes 18874368 | tf_op jit(solution)/shard_map/pallas_call | solution.py:141
  239.6 57.6 %shard_map.236 = (bf16[256,768]{1,0:T(8,128)(2,1)}, f32[2,256,768]{2,1,0:T(8,128)}, bf16[2,256,768]{2,1,0:T(8,128)(2,1)}, bf16[2,256,2304]{2,1,0:T(8,128)(2,1)},...) custom-call(s32[1,2,2,256]{3,2,1,0:T(2,128)} %bitcast.37, ...), custom_call_target="tpu_custom_call" | custom-call | flops 6039797760 | bytes 18874368 | tf_op jit(solution)/shard_map/pallas_call | solution.py:141
  297.2 89.8 %shard_map.237 = (bf16[256,768]{1,0:T(8,128)(2,1)}, f32[2,256,768]{2,1,0:T(8,128)}, bf16[2,256,768]{2,1,0:T(8,128)(2,1)}, bf16[2,256,2304]{2,1,0:T(8,128)(2,1)},...) custom-call(s32[1,2,2,256]{3,2,1,0:T(2,128)} %bitcast.38, ...), custom_call_target="tpu_custom_call", output_to_operand_aliasing={{1}: (14, {}), {2}: (15, {}), {3}: (16, {}), {4}: (17, {}),... | custom-call | flops 6039797760 | bytes 18874368 | tf_op jit(solution)/shard_map/pallas_call | solution.py:141
  387.0 64.5 %shard_map.238 = (f32[2,256,768]{2,1,0:T(8,128)}, bf16[2,256,768]{2,1,0:T(8,128)(2,1)}, bf16[2,256,2304]{2,1,0:T(8,128)(2,1)}, bf16[2,256,128]{2,1,0:T(8,128)(2,...) custom-call(s32[1,2,2,256]{3,2,1,0:T(2,128)} %bitcast.39, ...), custom_call_target="tpu_custom_call", output_to_operand_aliasing={{0}: (14, {}), {1}: (15, {}), {2}: (16, {}), {3}: (17, {}),... | custom-call | flops 6039797760 | bytes 18874368 | tf_op jit(solution)/shard_map/pallas_call | solution.py:141
  451.4 45.0 %shard_map.239.packed = f32[48,3200]{1,0:T(8,128)S(1)} custom-call(f32[12,768]{1,0:T(8,128)S(1)} %copy-done.1, bf16[768,256]{1,0:T(8,128)(2,1)S(1)} %copy-done, bf16[2,256,768]{2,1,0:T(8,128)(2,1)} %get-tuple-element.146.refs_2_, bf16[2,256,2304]{2,1,0:T(8,128)(2,1)} %get-tuple-element.147.refs_3_, bf16[2,256,768]{2,1,0:T(8,128)(2,1)} %get-tuple-element.148.refs_4_, ...), custom_call_target="tpu_custom_call" | custom-call | flops 3000000000 | bytes 10000000 | tf_op jit(solution)/shard_map/pallas_call | solution.py:141
  496.5 0.0 copy-start.3
  496.5 0.0 copy-start.2
  496.5 29.9 %shard_map.240 = (f32[1,4,768,1536]{3,2,1,0:T(8,128)}, f32[1,4,1536,768]{3,2,1,0:T(8,128)}, f32[1,48,2304]{2,1,0:T(8,128)}, f32[1,48,768]{2,1,0:T(8,128)}, f32[1...) custom-call(bf16[2,4,320,768]{3,2,1,0:T(8,128)(2,1)} %get-tuple-element.142.rows, ...), custom_call_target="tpu_custom_call" | custom-call | flops 12079595520 | bytes 37748736 | tf_op jit(solution)/shard_map/pallas_call | solution.py:1418
  526.5 0.0 copy-done.3
  526.5 0.9 copy.112
  527.4 0.0 copy-done.2
  527.4 1.1 copy.113
Async XLA Ops:
  0.6 48.7 %copy-start = (bf16[768,256]{1,0:T(8,128)(2,1)S(1)}, bf16[768,256]{1,0:T(8,128)(2,1)}, u32[]{:S(2)}) copy-start(bf16[768,256]{1,0:T(8,128)(2,1)} %constant.7.clone.refs_1_) | copy-start | bytes 1179652
  0.7 48.7 %copy-start.1 = (f32[12,768]{1,0:T(8,128)S(1)}, f32[12,768]{1,0:T(8,128)}, u32[]{:S(2)}) copy-start(f32[12,768]{1,0:T(8,128)} %constant.6.clone.refs_0_) | copy-start | bytes 110596
  496.5 30.0 %copy-start.3 = (bf16[2,256,768]{2,1,0:T(8,128)(2,1)S(1)}, bf16[2,256,768]{2,1,0:T(8,128)(2,1)}, u32[]{:S(2)}) copy-start(bf16[2,256,768]{2,1,0:T(8,128)(2,1)} %get-tuple-element.115) | copy-start | bytes 2359300
  496.5 30.9 %copy-start.2 = (f32[2,256,768]{2,1,0:T(8,128)S(1)}, f32[2,256,768]{2,1,0:T(8,128)}, u32[]{:S(2)}) copy-start(f32[2,256,768]{2,1,0:T(8,128)} %get-tuple-element.141) | copy-start | bytes 4718596

commit v4 on v3

--- a/solution.py
+++ b/solution.py
@@ -1377,8 +1377,7 @@
     )
 
 
-def expert_weights_kernel(experts_all, rows, pre, hidden, seen, packed, in_grad, out_grad, qkv, out, router, one, two,
-                          terms):
+def expert_weights_kernel(rows, pre, hidden, seen, in_grad, out_grad):
     def product(left, right):
         left, right = (ref[:, 0].reshape(-1, ref.shape[-1]) for ref in (left, right))
         return mm(left, right, (0, 0))
@@ -1386,51 +1385,27 @@
     in_grad[0, 0] = product(rows, pre)
     out_grad[0, 0] = product(hidden, seen)
 
-    @pl.when((pl.program_id(0) == 0) & (pl.program_id(1) == 0))
-    def _():
-        wide, narrow = qkv.shape[2], out.shape[2]
-        qkv[0] = packed[:, :wide]
-        out[0] = packed[:, wide : wide + narrow]
-        small = packed[:, wide + narrow :]
-        dims = (experts_all + 8, 128)
-        pick = (iota(dims, 0) == iota(dims, 1)).astype(F32)
-        lines = lax.dot_general(
-            pick, small, (((1,), (1,)), ((), ())), precision=lax.Precision.HIGHEST, preferred_element_type=F32
-        )
-        router[0] = lines[:experts_all]
-        one[...] = lines[experts_all : experts_all + 1]
-        two[...] = lines[experts_all + 1 : experts_all + 2]
-        terms[...] = lines[experts_all + 2 : experts_all + 3, : terms.shape[1]]
-
-
-def expert_weights(geo, state, packed, terms):
+
+def expert_weights(geo, state):
     micro, local, count, width, hidden = geo.micro, geo.local_experts, geo.expert_rows, geo.width, geo.hidden
     tile = tile_of(hidden, 768)
     narrow = pl.BlockSpec((micro, 1, count, width), lambda e, f: (0, e, 0, 0))
     wide = pl.BlockSpec((micro, 1, count, tile), lambda e, f: (0, e, 0, f))
     flops = 4 * micro * local * count * width * hidden
-    share = packed.shape[0]
-    small = [(1, share, 3 * width), (1, share, width), (1, geo.experts_all, share), (1, share), (1, share), (1, terms)]
-
-    def whole(dims):
-        return pl.BlockSpec(dims, lambda e, f: (0,) * len(dims))
-
     return pl.pallas_call(
-        partial(expert_weights_kernel, geo.experts_all),
-        out_shape=[shape((1, local, width, hidden), F32), shape((1, local, hidden, width), F32)]
-        + [shape(dims, F32) for dims in small],
+        expert_weights_kernel,
+        out_shape=(shape((1, local, width, hidden), F32), shape((1, local, hidden, width), F32)),
         grid=(local, hidden // tile),
-        in_specs=[narrow, wide, wide, narrow, whole(packed.shape)],
+        in_specs=[narrow, wide, wide, narrow],
         out_specs=[
             pl.BlockSpec((1, 1, width, tile), lambda e, f: (0, e, 0, f)),
             pl.BlockSpec((1, 1, tile, width), lambda e, f: (0, e, f, 0)),
-        ]
-        + [whole(dims) for dims in small],
+        ],
         compiler_params=pltpu.CompilerParams(vmem_limit_bytes=48 * MIB),
         cost_estimate=pl.CostEstimate(
             flops=flops, bytes_accessed=8 * local * hidden * width, transcendentals=0
         ),
-    )(*(in_hbm(state[name]) for name in ("kept_rows", "kept_pre", "kept_hidden", "kept_seen")), packed)
+    )(*(in_hbm(state[name]) for name in ("kept_rows", "kept_pre", "kept_hidden", "kept_seen")))
 
 
 def norm_backward(values, gain, grad):
@@ -1631,20 +1606,27 @@
         for name in names:
             loads[name].wait()
 
+    early = 2 * width
+
     def put(places, block):
-        block = block.astype(BF16)
-        if len(at.part.shape) == 4:
-            at.part[:, :, :, places] = block.reshape(at.part.shape[:3] + block.shape[1:])
-        else:
-            at.part[:, places] = block
+        at.late[:, places] = block.astype(BF16)
 
     ready("normed", "qkv_grad")
     normed = at.normed[...].reshape(-1, width)
-    for j in range(0, 3 * width, width):
+
+    def qkv_product(j):
         grad = at.qkv_grad[:, :, j : j + width].reshape(-1, width)
-        put(slice(j, j + width), mm(normed, grad, (0, 0)))
+        return mm(normed, grad, (0, 0))
+
+    put(slice(0, width), qkv_product(early))
+    for j in range(0, early, width):
+        block = qkv_product(j).astype(BF16)
+        if len(at.part.shape) == 4:
+            at.part[:, :, :, j : j + width] = block.reshape(at.part.shape[:3] + block.shape[1:])
+        else:
+            at.part[:, j : j + width] = block
     ready("context", "branch")
-    put(slice(3 * width, 4 * width), product(at.context, at.branch))
+    put(slice(width, 2 * width), product(at.context, at.branch))
     ready("moe_in", "logit", "gains", "sums")
     small = product(at.moe_in, at.logit)
     by_term = lax.dot_general(
@@ -1657,15 +1639,7 @@
     rows = jnp.zeros((128, width), F32)
     for k, row in enumerate((gain_rows[0:1], gain_rows[1:2], bias_row)):
         rows = jnp.where(place == geo.experts_all + k, row, rows)
-    put(slice(4 * width, None), small + rows.T)
-
-
-def reduce_body(geo, at):
-    shards = Shards(geo)
-    shards.greet()
-    dense_weights_body(geo, at)
-    shards.await_greetings()
-    reduce_part(shards, at)
+    put(slice(2 * width, 2 * width + 128), small + rows.T)
 
 
 def dense_weights(geo, head_pick, spread_table, state):
@@ -1675,36 +1649,34 @@
         sems=pltpu.SemaphoreType.DMA((len(DENSE_GRADS) + 2,)),
         gains=pltpu.VMEM(state["kept_gains"].shape, F32), sums=pltpu.VMEM(state["kept_sums"].shape, F32),
     )
-    share, total = geo.width // geo.sources, 4 * geo.width + 128
-    parts = (geo.rows, geo.cols, share, total)
-    fused = share % 16 == 0
-    outs = dict(shard=shape((share, total), F32)) if fused else dict(part=shape((geo.width, total), BF16))
-    params = {}
-    if fused:
-        scratch.update(reduce_scratch(geo, share, total), part=pltpu.VMEM(parts, BF16))
-        params = dict(collective_id=2, has_side_effects=True)
+    share, width = geo.width // geo.sources, geo.width
+    parts = (geo.rows, geo.cols, share, 2 * width)
     results = launch(
-        partial(reduce_body if fused else dense_weights_body, geo),
+        partial(dense_weights_body, geo),
         near=dict(head_pick=head_pick, spread=spread_table),
         held=held,
-        outs=outs,
+        outs=dict(
+            part=shape(parts if share % 16 == 0 else (width, 2 * width), BF16),
+            late=shape((width, 2 * width + 128), BF16),
+        ),
         scratch=scratch,
         spare=24,
         cost=(3_000_000_000, 10_000_000),
-        **params,
-    )
-    if fused:
-        return results["shard"]
-
+    )
+    return results["part"].reshape(parts), results["late"]
+
+
+def reduce_shards(geo, part):
     def body(at):
         shards = Shards(geo)
         shards.greet()
         shards.await_greetings()
         reduce_part(shards, at)
 
+    share, total = part.shape[2:]
     return launch(
         body,
-        near=dict(part=results["part"].reshape(parts)),
+        near=dict(part=part),
         outs=dict(shard=shape((share, total), F32)),
         scratch=reduce_scratch(geo, share, total),
         collective_id=2,
@@ -1757,14 +1729,17 @@
     for step in range(micro + 1):
         passed = backward_step(geo, step, given, state, sent, received)
         sent, received = passed.get("sent_out"), passed.get("received_out")
-    packed = dense_weights(geo, head_pick, spread_table, state)
-    expert_in_grad, expert_out_grad, qkv, out, router, gain_one, gain_two, bias = expert_weights(
-        geo, state, packed, terms
-    )
+    part, late = dense_weights(geo, head_pick, spread_table, state)
+    late = lax.psum_scatter(late, ("row", "col"), scatter_dimension=0, tiled=True)
+    part = reduce_shards(geo, part)
+    expert_in_grad, expert_out_grad = expert_weights(geo, state)
+    late = late.astype(F32)
+    small = late[:, 2 * width :]
     return (
-        state["out"][None], state["in_grad"][None], gain_one, qkv, bias, out, gain_two,
-        jnp.swapaxes(router, 1, 2), expert_in_grad,
-        expert_out_grad,
+        state["out"][None], state["in_grad"][None], small[:, experts_all][None],
+        jnp.concatenate([part, late[:, :width]], axis=1)[None], small[:terms, experts_all + 2][None],
+        late[None, :, width : 2 * width], small[:, experts_all + 1][None], small[None, :, :experts_all],
+        expert_in_grad, expert_out_grad,
     )
 
 

time: 538 us -> 550 us (1.022)
  Pallas kernels: 526 us -> 508 us
  between operations: 1.28 us -> 14.7 us
  waiting for transfers between devices: 0 us -> 11.7 us
    pallas_call x8 -> x9, Pallas kernels: 447 us -> 431 us  [launch(): pl.pallas_call(kernel, out_shape=out_shapes, in_specs=[vmem_spec()] * len...]
    reduce_scatter x0 -> x1, waiting for transfers between devices: none -> 11.7 us  [on_device(): lax.psum_scatter(late, ('row', 'col'), scatter_dimension=0, tiled=True)]
  transfers between devices with their start and end apart: 0 -> 1, of which waited for: 0 -> 1; matrix products, arithmetic and copies ran while one was open for 0% -> 0% of each run, Pallas kernels for 0% -> 9%
where the time goes in v4:
time: 550 us; the launch traced here: 542 us
  Pallas kernels  508 us (92%)
  between operations  14.7 us (3%)
  waiting for transfers between devices  11.7 us (2%)
  local copies, waits for them, and re-layouts  5.68 us (1%)
    pallas_call x9, Pallas kernels, launch(): pl.pallas_call(kernel, out_shape=out_shapes, in_specs=[vmem_spec()] * len...  431 us
    pallas_call x1, Pallas kernels, gather_shards(): pl.pallas_call(partial(gather_kernel, geo, pieces), out_shape=pltpu.HBM((...  48.7 us
    pallas_call x1, Pallas kernels, expert_weights(): pl.pallas_call(expert_weights_kernel, out_shape=(shape((1, local, width,...  28.1 us
    reduce_scatter x1, waiting for transfers between devices, on_device(): lax.psum_scatter(late, ('row', 'col'), scatter_dimension=0, tiled=True)  11.7 us
  transfers between devices with their start and end apart: 1, of which 1 were waited for; matrix products, arithmetic and copies ran while one was open for 0% of the time, Pallas kernels for 9%

profile of v4, /device:TPU:0, one launch (start us, length us, event | category | flops | bytes accessed | tf_op | source)
XLA Modules:
  0.0 541.6 jit_solution(16445532305794644153)
XLA Ops:
  7.2 0.0 copy-start
  7.2 0.0 copy-start.1
  7.2 0.0 reduce-scatter.2.cloned.1.call-start
  7.2 48.7 %shard_map.231 = bf16[8,2,48,3200]{3,2,1,0:T(8,128)(2,1)} custom-call(bf16[48,2304]{1,0:T(8,128)(2,1)} %bitcast.41, bf16[48,768]{1,0:T(8,128)(2,1)} %bitcast.48, bf16[32,48]{1,0:T(8,128)(2,1)} %bitcast.49, bf16[1,48]{1,0:T(2,128)(2,1)} %gain_one.1, bf16[1,48]{1,0:T(2,128)(2,1)} %gain_two.1, bf16[1,24]{1,0:T(2,128)(2,1)} %terms.1), custom_call_target="tpu_custom_call" | custom-call | tf_op jit(solution)/shard_map/pallas_call | solution.py:1281
  56.0 0.0 copy-done
  56.0 0.0 copy-done.1
  56.0 2.9 shard_map.232
  58.9 57.1 %shard_map.233 = (bf16[2,256,768]{2,1,0:T(8,128)(2,1)}, bf16[2,256,768]{2,1,0:T(8,128)(2,1)}, bf16[2,256,2304]{2,1,0:T(8,128)(2,1)}, bf16[2,12,256,256]{3,2,1,0:...) custom-call(s32[2,256]{1,0:T(2,128)} %refs_0_.7, ...), custom_call_target="tpu_custom_call" | custom-call | flops 6039797760 | bytes 18874368 | tf_op jit(solution)/shard_map/pallas_call | solution.py:141
  116.0 73.2 %shard_map.234 = (bf16[256,768]{1,0:T(8,128)(2,1)}, bf16[2,256,768]{2,1,0:T(8,128)(2,1)}, bf16[2,256,768]{2,1,0:T(8,128)(2,1)}, bf16[2,256,2304]{2,1,0:T(8,128)(...) custom-call(s32[2,256]{1,0:T(2,128)} %refs_0_.7, ...), custom_call_target="tpu_custom_call", output_to_operand_aliasing={{1}: (10, {}), {2}: (11, {}), {3}: (12, {}), {4}: (13, {}),... | custom-call | flops 6039797760 | bytes 18874368 | tf_op jit(solution)/shard_map/pallas_call | solution.py:141
  189.3 56.9 %shard_map.235 = (bf16[2,256,768]{2,1,0:T(8,128)(2,1)}, bf16[2,256,768]{2,1,0:T(8,128)(2,1)}, bf16[2,256,2304]{2,1,0:T(8,128)(2,1)}, bf16[2,12,256,256]{3,2,1,0:...) custom-call(s32[2,256]{1,0:T(2,128)} %refs_0_.7, ...), custom_call_target="tpu_custom_call", output_to_operand_aliasing={{0}: (11, {}), {1}: (12, {}), {2}: (13, {}), {3}: (14, {}),... | custom-call | flops 6039797760 | bytes 18874368 | tf_op jit(solution)/shard_map/pallas_call | solution.py:141
  246.2 57.8 %shard_map.236 = (bf16[256,768]{1,0:T(8,128)(2,1)}, f32[2,256,768]{2,1,0:T(8,128)}, bf16[2,256,768]{2,1,0:T(8,128)(2,1)}, bf16[2,256,2304]{2,1,0:T(8,128)(2,1)},...) custom-call(s32[1,2,2,256]{3,2,1,0:T(2,128)} %bitcast.45, ...), custom_call_target="tpu_custom_call" | custom-call | flops 6039797760 | bytes 18874368 | tf_op jit(solution)/shard_map/pallas_call | solution.py:141
  304.0 88.8 %shard_map.237 = (bf16[256,768]{1,0:T(8,128)(2,1)}, f32[2,256,768]{2,1,0:T(8,128)}, bf16[2,256,768]{2,1,0:T(8,128)(2,1)}, bf16[2,256,2304]{2,1,0:T(8,128)(2,1)},...) custom-call(s32[1,2,2,256]{3,2,1,0:T(2,128)} %bitcast.46, ...), custom_call_target="tpu_custom_call", output_to_operand_aliasing={{1}: (14, {}), {2}: (15, {}), {3}: (16, {}), {4}: (17, {}),... | custom-call | flops 6039797760 | bytes 18874368 | tf_op jit(solution)/shard_map/pallas_call | solution.py:141
  392.9 65.0 %shard_map.238 = (f32[2,256,768]{2,1,0:T(8,128)}, bf16[2,256,768]{2,1,0:T(8,128)(2,1)}, bf16[2,256,2304]{2,1,0:T(8,128)(2,1)}, bf16[2,256,128]{2,1,0:T(8,128)(2,...) custom-call(s32[1,2,2,256]{3,2,1,0:T(2,128)} %bitcast.47, ...), custom_call_target="tpu_custom_call", output_to_operand_aliasing={{0}: (14, {}), {1}: (15, {}), {2}: (16, {}), {3}: (17, {}),... | custom-call | flops 6039797760 | bytes 18874368 | tf_op jit(solution)/shard_map/pallas_call | solution.py:141
  457.9 7.8 %shard_map.239 = (bf16[8,2,48,1536]{3,2,1,0:T(8,128)(2,1)S(1)}, bf16[768,1664]{1,0:T(8,128)(2,1)}) custom-call(f32[12,768]{1,0:T(8,128)S(1)} %copy-done.1, bf16[768,256]{1,0:T(8,128)(2,1)S(1)} %copy-done, bf16[2,256,768]{2,1,0:T(8,128)(2,1)} %get-tuple-element.138.refs_2_, bf16[2,256,2304]{2,1,0:T(8,128)(2,1)} %get-tuple-element.139.refs_3_, ...), custom_call_target="tpu_custom_call" | custom-call | flops 3000000000 | bytes 10000000 | tf_op jit(solution)/shard_map/pallas_call | solution.py:141
  465.7 0.0 reduce-scatter.2.cloned.1.call-update
  465.7 21.4 %shard_map.240 = f32[48,1536]{1,0:T(8,128)S(1)} custom-call(bf16[8,2,48,1536]{3,2,1,0:T(8,128)(2,1)S(1)} %get-tuple-element.147.refs_0_), custom_call_target="tpu_custom_call" | custom-call | tf_op jit(solution)/shard_map/pallas_call | solution.py:141
  487.1 0.0 copy-start.3
  487.1 28.1 %shard_map.241 = (f32[1,4,768,1536]{3,2,1,0:T(8,128)}, f32[1,4,1536,768]{3,2,1,0:T(8,128)}) custom-call(bf16[2,4,320,768]{3,2,1,0:T(8,128)(2,1)} %get-tuple-element.148.rows, bf16[2,4,320,1536]{3,2,1,0:T(8,128)(2,1)} %get-tuple-element.149.pre, bf16[2,4,320,1536]{3,2,1,0:T(8,128)(2,1)} %get-tuple-element.150.hidden, ...), custom_call_target="tpu_custom_call" | custom-call | flops 12079595520 | bytes 37748736 | tf_op jit(solution)/shard_map/pallas_call | solution.py:1395
  515.2 0.0 copy-start.2
  515.2 11.7 %reduce-scatter.2.cloned.1.call-done = bf16[48,1664]{1,0:T(8,128)(2,1)} async-done(((bf16[768,1664]{1,0:T(8,128)(2,1)}), bf16[48,1664]{1,0:T(8,128)(2,1)}) %reduce-scatter.2.cloned.1.call-update) | async-done | bytes 159760 | tf_op jit(solution)/shard_map/reduce_scatter | solution.py:1733
  526.9 0.9 convert_element_type.3
  527.8 0.7 slice_reduce_fusion.2
  528.5 0.7 slice_reduce_fusion
  529.2 0.7 slice_bitcast_fusion
  529.9 0.7 copy.69
  530.5 0.9 slice.30
  531.4 0.8 maximum_bitcast_fusion
  532.2 0.0 copy-done.3
  532.2 0.9 copy.114
  533.1 0.0 copy-done.2
  533.1 1.1 copy.115
  (1 shorter events, 0.0 us)
Async XLA Ops:
  7.2 48.8 %copy-start = (bf16[768,256]{1,0:T(8,128)(2,1)S(1)}, bf16[768,256]{1,0:T(8,128)(2,1)}, u32[]{:S(2)}) copy-start(bf16[768,256]{1,0:T(8,128)(2,1)} %constant.7.clone.refs_1_) | copy-start | bytes 1179652
  7.2 48.8 %copy-start.1 = (f32[12,768]{1,0:T(8,128)S(1)}, f32[12,768]{1,0:T(8,128)}, u32[]{:S(2)}) copy-start(f32[12,768]{1,0:T(8,128)} %constant.6.clone.refs_0_) | copy-start | bytes 110596
  7.2 519.6 %reduce-scatter.2.cloned.1.call-start = ((), (), s32[]{:S(2)}) async-start(), calls=%async_computation.1 | async-start | bytes 2715648 | tf_op jit(solution)/shard_map/reduce_scatter | solution.py:1733
  487.1 45.1 %copy-start.3 = (bf16[2,256,768]{2,1,0:T(8,128)(2,1)S(1)}, bf16[2,256,768]{2,1,0:T(8,128)(2,1)}, u32[]{:S(2)}) copy-start(bf16[2,256,768]{2,1,0:T(8,128)(2,1)} %get-tuple-element.111) | copy-start | bytes 2359300
  515.2 17.9 %copy-start.2 = (f32[2,256,768]{2,1,0:T(8,128)S(1)}, f32[2,256,768]{2,1,0:T(8,128)}, u32[]{:S(2)}) copy-start(f32[2,256,768]{2,1,0:T(8,128)} %get-tuple-element.137) | copy-start | bytes 4718596
Sparse Core Ops, SparseCore 0:
  465.8 60.9 reduce-scatter.1

commit v5 on v3

--- a/solution.py
+++ b/solution.py
@@ -1294,79 +1294,89 @@
     )(in_hbm(qkv), in_hbm(out), router, gain_one, gain_two, terms)
 
 
-def reduce_part(shards, refs):
+def reduce_part(shards, refs, groups):
     at = shards
-    part_ref, out_ref = refs.part, refs.shard
-    from_core, from_col, from_chip, pair, column = refs.from_core, refs.from_col, refs.from_chip, refs.pair, refs.column
-    core_send, core_recv, y_send, y_recv, z_send, z_recv = (
-        refs.core_send, refs.core_recv, refs.y_send, refs.y_recv, refs.z_send, refs.z_recv
-    )
-    order = list(range(1, at.chips)) + [0]
     started = []
 
     def start(copy):
         copy.start()
         started.append(copy)
 
-    def to_core(k):
+    def to_core(g, k):
         return remote(
-            part_ref.at[at.row(at.chip(k), 1)], from_core.at[k], core_send.at[k, 0], core_recv.at[k, 0],
-            {"row": at.row(at.z, 1)},
+            refs.part.at[at.row(at.chip(k), 1), :, :, lanes[g]], refs.from_core.at[k, :, :, lanes[g]],
+            refs.core_send.at[g, k], refs.core_recv.at[g, k], {"row": at.row(at.z, 1)},
         )
 
-    def to_col(k, j):
+    def to_col(g, k, j):
         return remote(
-            pair.at[k, at.col(j)], from_col.at[k, j - 1], y_send.at[k, j - 1], y_recv.at[k, j - 1],
-            {"col": at.col(j)},
+            refs.pair.at[k, at.col(j), :, lanes[g]], refs.from_col.at[k, j - 1, :, lanes[g]],
+            refs.y_send.at[g, k, j - 1], refs.y_recv.at[g, k, j - 1], {"col": at.col(j)},
         )
 
-    def to_chip(k):
+    def to_chip(g, k):
         return remote(
-            column.at[k - 1], from_chip.at[k - 1], z_send.at[k - 1], z_recv.at[k - 1],
-            {"row": at.row(at.chip(k))},
+            refs.column.at[k - 1, :, lanes[g]], refs.from_chip.at[k - 1, :, lanes[g]], refs.z_send.at[g, k - 1],
+            refs.z_recv.at[g, k - 1], {"row": at.row(at.chip(k))},
         )
 
-    if at.cores > 1:
-        for k in order:
-            start(to_core(k))
-
-    def sum_cores(k):
-        total = part_ref[at.row(at.chip(k))].astype(F32)
+    def sum_cores(g, k):
+        total = refs.part[at.row(at.chip(k)), :, :, lanes[g]].astype(F32)
         if at.cores > 1:
-            to_core(k).wait_recv()
-            total = total + from_core[k].astype(F32)
-        pair[k] = total.astype(BF16)
+            to_core(g, k).wait_recv()
+            total = total + refs.from_core[k, :, :, lanes[g]].astype(F32)
+        refs.pair[k, :, :, lanes[g]] = total.astype(BF16)
         for j in range(1, at.cols):
-            start(to_col(k, j))
-
-    def sum_cols(k):
-        total = pair[k, at.c].astype(F32)
+            start(to_col(g, k, j))
+
+    def sum_cols(g, k):
+        total = refs.pair[k, at.c, :, lanes[g]].astype(F32)
         for j in range(1, at.cols):
-            to_col(k, j).wait_recv()
-            total = total + from_col[k, j - 1].astype(F32)
+            to_col(g, k, j).wait_recv()
+            total = total + refs.from_col[k, j - 1, :, lanes[g]].astype(F32)
         if k:
-            column[k - 1] = total.astype(BF16)
-            start(to_chip(k))
+            refs.column[k - 1, :, lanes[g]] = total.astype(BF16)
+            start(to_chip(g, k))
         else:
-            out_ref[...] = total
-
-    for step, k in enumerate(order):
-        sum_cores(k)
-        if step:
-            sum_cols(order[step - 1])
-    sum_cols(order[-1])
-    for k in range(1, at.chips):
-        to_chip(k).wait_recv()
-        out_ref[...] += from_chip[k - 1].astype(F32)
+            refs.shard[:, lanes[g]] = total
+
+    lanes, waiting = [], []
+
+    def advance(g, k):
+        sum_cores(g, k)
+        waiting.append((g, k))
+        if len(waiting) > 2:
+            sum_cols(*waiting.pop(0))
+
+    far = sorted(range(1, at.chips), key=lambda k: abs(2 * k - at.chips))
+    for places in groups:
+        lanes.append(places)
+        g = len(lanes) - 1
+        if at.cores > 1:
+            for k in far + [0]:
+                start(to_core(g, k))
+        if g:
+            for k in far:
+                advance(g - 1, k)
+    for k in far:
+        advance(len(lanes) - 1, k)
+    for g in range(len(lanes)):
+        advance(g, 0)
+    while waiting:
+        sum_cols(*waiting.pop(0))
+    for g in range(len(lanes)):
+        for k in far:
+            to_chip(g, k).wait_recv()
+            refs.shard[:, lanes[g]] += refs.from_chip[k - 1, :, lanes[g]].astype(F32)
     for copy in started:
         copy.wait_send()
 
 
 def reduce_scratch(geo, share, width):
     chips, steps, far = geo.chips, max(1, geo.cols - 1), max(1, geo.chips - 1)
-    z = pltpu.SemaphoreType.DMA((far,))
-    y = pltpu.SemaphoreType.DMA((chips, steps))
-    core = pltpu.SemaphoreType.DMA((chips, geo.cols))
+    z = pltpu.SemaphoreType.DMA((4, far))
+    y = pltpu.SemaphoreType.DMA((4, chips, steps))
+    core = pltpu.SemaphoreType.DMA((4, chips))
     return dict(
         from_core=pltpu.VMEM((chips, geo.cols, share, width), BF16),
         from_col=pltpu.VMEM((chips, steps, share, width), BF16),
@@ -1616,7 +1626,7 @@
 DENSE_GRADS = ("normed", "qkv_grad", "context", "branch", "moe_in", "logit")
 
 
-def dense_weights_body(geo, at):
+def dense_weights_groups(geo, at):
     width = geo.width
     copies = Copies(at.sems)
     loads = {}
@@ -1643,6 +1653,7 @@
     for j in range(0, 3 * width, width):
         grad = at.qkv_grad[:, :, j : j + width].reshape(-1, width)
         put(slice(j, j + width), mm(normed, grad, (0, 0)))
+        yield slice(j, j + width)
     ready("context", "branch")
     put(slice(3 * width, 4 * width), product(at.context, at.branch))
     ready("moe_in", "logit", "gains", "sums")
@@ -1657,15 +1668,26 @@
     rows = jnp.zeros((128, width), F32)
     for k, row in enumerate((gain_rows[0:1], gain_rows[1:2], bias_row)):
         rows = jnp.where(place == geo.experts_all + k, row, rows)
-    put(slice(4 * width, None), small + rows.T)
+    put(slice(4 * width, 4 * width + 128), small + rows.T)
+    yield slice(3 * width, 4 * width + 128)
+
+
+def dense_weights_body(geo, at):
+    for _ in dense_weights_groups(geo, at):
+        pass
 
 
 def reduce_body(geo, at):
     shards = Shards(geo)
     shards.greet()
-    dense_weights_body(geo, at)
-    shards.await_greetings()
-    reduce_part(shards, at)
+
+    def groups():
+        for g, places in enumerate(dense_weights_groups(geo, at)):
+            if g == 0:
+                shards.await_greetings()
+            yield places
+
+    reduce_part(shards, at, groups())
 
 
 def dense_weights(geo, head_pick, spread_table, state):
@@ -1700,7 +1722,7 @@
         shards = Shards(geo)
         shards.greet()
         shards.await_greetings()
-        reduce_part(shards, at)
+        reduce_part(shards, at, [slice(0, total)])
 
     return launch(
         body,

time: 538 us -> 527 us (0.980)
  Pallas kernels: 526 us -> 516 us
    pallas_call x8, Pallas kernels: 447 us -> 438 us  [launch(): pl.pallas_call(kernel, out_shape=out_shapes, in_specs=[vmem_spec()] * len...]
where the time goes in v5:
time: 527 us; the launch traced here: 519 us
  Pallas kernels  516 us (98%)
    pallas_call x8, Pallas kernels, launch(): pl.pallas_call(kernel, out_shape=out_shapes, in_specs=[vmem_spec()] * len...  438 us
    pallas_call x1, Pallas kernels, gather_shards(): pl.pallas_call(partial(gather_kernel, geo, pieces), out_shape=pltpu.HBM((...  48.7 us
    pallas_call x1, Pallas kernels, expert_weights(): pl.pallas_call(partial(expert_weights_kernel, geo.experts_all), out_shape...  29.9 us

profile of v5, /device:TPU:0, one launch (start us, length us, event | category | flops | bytes accessed | tf_op | source)
XLA Modules:
  0.0 519.5 jit_solution(8290439220816905074)
XLA Ops:
  0.6 0.0 copy-start
  0.7 0.0 copy-start.1
  0.7 48.7 %shard_map.231 = bf16[8,2,48,3200]{3,2,1,0:T(8,128)(2,1)} custom-call(bf16[48,2304]{1,0:T(8,128)(2,1)} %bitcast.33, bf16[48,768]{1,0:T(8,128)(2,1)} %bitcast.40, bf16[32,48]{1,0:T(8,128)(2,1)} %bitcast.41, bf16[1,48]{1,0:T(2,128)(2,1)} %gain_one.1, bf16[1,48]{1,0:T(2,128)(2,1)} %gain_two.1, bf16[1,24]{1,0:T(2,128)(2,1)} %terms.1), custom_call_target="tpu_custom_call" | custom-call | tf_op jit(solution)/shard_map/pallas_call | solution.py:1281
  49.4 0.0 copy-done
  49.4 0.0 copy-done.1
  49.4 2.9 shard_map.232
  52.3 57.1 %shard_map.233 = (bf16[2,256,768]{2,1,0:T(8,128)(2,1)}, bf16[2,256,768]{2,1,0:T(8,128)(2,1)}, bf16[2,256,2304]{2,1,0:T(8,128)(2,1)}, bf16[2,12,256,256]{3,2,1,0:...) custom-call(s32[2,256]{1,0:T(2,128)} %refs_0_.7, ...), custom_call_target="tpu_custom_call" | custom-call | flops 6039797760 | bytes 18874368 | tf_op jit(solution)/shard_map/pallas_call | solution.py:141
  109.4 73.2 %shard_map.234 = (bf16[256,768]{1,0:T(8,128)(2,1)}, bf16[2,256,768]{2,1,0:T(8,128)(2,1)}, bf16[2,256,768]{2,1,0:T(8,128)(2,1)}, bf16[2,256,2304]{2,1,0:T(8,128)(...) custom-call(s32[2,256]{1,0:T(2,128)} %refs_0_.7, ...), custom_call_target="tpu_custom_call", output_to_operand_aliasing={{1}: (10, {}), {2}: (11, {}), {3}: (12, {}), {4}: (13, {}),... | custom-call | flops 6039797760 | bytes 18874368 | tf_op jit(solution)/shard_map/pallas_call | solution.py:141
  182.6 57.1 %shard_map.235 = (bf16[2,256,768]{2,1,0:T(8,128)(2,1)}, bf16[2,256,768]{2,1,0:T(8,128)(2,1)}, bf16[2,256,2304]{2,1,0:T(8,128)(2,1)}, bf16[2,12,256,256]{3,2,1,0:...) custom-call(s32[2,256]{1,0:T(2,128)} %refs_0_.7, ...), custom_call_target="tpu_custom_call", output_to_operand_aliasing={{0}: (11, {}), {1}: (12, {}), {2}: (13, {}), {3}: (14, {}),... | custom-call | flops 6039797760 | bytes 18874368 | tf_op jit(solution)/shard_map/pallas_call | solution.py:141
  239.7 57.3 %shard_map.236 = (bf16[256,768]{1,0:T(8,128)(2,1)}, f32[2,256,768]{2,1,0:T(8,128)}, bf16[2,256,768]{2,1,0:T(8,128)(2,1)}, bf16[2,256,2304]{2,1,0:T(8,128)(2,1)},...) custom-call(s32[1,2,2,256]{3,2,1,0:T(2,128)} %bitcast.37, ...), custom_call_target="tpu_custom_call" | custom-call | flops 6039797760 | bytes 18874368 | tf_op jit(solution)/shard_map/pallas_call | solution.py:141
  297.0 90.1 %shard_map.237 = (bf16[256,768]{1,0:T(8,128)(2,1)}, f32[2,256,768]{2,1,0:T(8,128)}, bf16[2,256,768]{2,1,0:T(8,128)(2,1)}, bf16[2,256,2304]{2,1,0:T(8,128)(2,1)},...) custom-call(s32[1,2,2,256]{3,2,1,0:T(2,128)} %bitcast.38, ...), custom_call_target="tpu_custom_call", output_to_operand_aliasing={{1}: (14, {}), {2}: (15, {}), {3}: (16, {}), {4}: (17, {}),... | custom-call | flops 6039797760 | bytes 18874368 | tf_op jit(solution)/shard_map/pallas_call | solution.py:141
  387.2 63.8 %shard_map.238 = (f32[2,256,768]{2,1,0:T(8,128)}, bf16[2,256,768]{2,1,0:T(8,128)(2,1)}, bf16[2,256,2304]{2,1,0:T(8,128)(2,1)}, bf16[2,256,128]{2,1,0:T(8,128)(2,...) custom-call(s32[1,2,2,256]{3,2,1,0:T(2,128)} %bitcast.39, ...), custom_call_target="tpu_custom_call", output_to_operand_aliasing={{0}: (14, {}), {1}: (15, {}), {2}: (16, {}), {3}: (17, {}),... | custom-call | flops 6039797760 | bytes 18874368 | tf_op jit(solution)/shard_map/pallas_call | solution.py:141
  451.0 36.0 %shard_map.239.packed = f32[48,3200]{1,0:T(8,128)S(1)} custom-call(f32[12,768]{1,0:T(8,128)S(1)} %copy-done.1, bf16[768,256]{1,0:T(8,128)(2,1)S(1)} %copy-done, bf16[2,256,768]{2,1,0:T(8,128)(2,1)} %get-tuple-element.146.refs_2_, bf16[2,256,2304]{2,1,0:T(8,128)(2,1)} %get-tuple-element.147.refs_3_, bf16[2,256,768]{2,1,0:T(8,128)(2,1)} %get-tuple-element.148.refs_4_, ...), custom_call_target="tpu_custom_call" | custom-call | flops 3000000000 | bytes 10000000 | tf_op jit(solution)/shard_map/pallas_call | solution.py:141
  487.0 0.0 copy-start.3
  487.0 0.0 copy-start.2
  487.0 29.9 %shard_map.240 = (f32[1,4,768,1536]{3,2,1,0:T(8,128)}, f32[1,4,1536,768]{3,2,1,0:T(8,128)}, f32[1,48,2304]{2,1,0:T(8,128)}, f32[1,48,768]{2,1,0:T(8,128)}, f32[1...) custom-call(bf16[2,4,320,768]{3,2,1,0:T(8,128)(2,1)} %get-tuple-element.142.rows, ...), custom_call_target="tpu_custom_call" | custom-call | flops 12079595520 | bytes 37748736 | tf_op jit(solution)/shard_map/pallas_call | solution.py:1428
  517.0 0.0 copy-done.3
  517.0 0.9 copy.112
  517.9 0.0 copy-done.2
  517.9 1.1 copy.113
Async XLA Ops:
  0.6 48.7 %copy-start = (bf16[768,256]{1,0:T(8,128)(2,1)S(1)}, bf16[768,256]{1,0:T(8,128)(2,1)}, u32[]{:S(2)}) copy-start(bf16[768,256]{1,0:T(8,128)(2,1)} %constant.7.clone.refs_1_) | copy-start | bytes 1179652
  0.7 48.7 %copy-start.1 = (f32[12,768]{1,0:T(8,128)S(1)}, f32[12,768]{1,0:T(8,128)}, u32[]{:S(2)}) copy-start(f32[12,768]{1,0:T(8,128)} %constant.6.clone.refs_0_) | copy-start | bytes 110596
  487.0 30.0 %copy-start.3 = (bf16[2,256,768]{2,1,0:T(8,128)(2,1)S(1)}, bf16[2,256,768]{2,1,0:T(8,128)(2,1)}, u32[]{:S(2)}) copy-start(bf16[2,256,768]{2,1,0:T(8,128)(2,1)} %get-tuple-element.115) | copy-start | bytes 2359300
  487.0 30.9 %copy-start.2 = (f32[2,256,768]{2,1,0:T(8,128)S(1)}, f32[2,256,768]{2,1,0:T(8,128)}, u32[]{:S(2)}) copy-start(f32[2,256,768]{2,1,0:T(8,128)} %get-tuple-element.141) | copy-start | bytes 4718596

commit v6 on v5

--- a/solution.py
+++ b/solution.py
@@ -1247,24 +1247,28 @@
                 came(block(k, j, h), y_recv.at[h, k, j - 1])
                 pass_core(k, j, h)
 
-    ahead = min(2, pieces)
+    ahead, lag = min(3, pieces), 2
+    far = sorted(range(1, at.chips), key=lambda k: abs(2 * k - at.chips))
     for h in range(ahead):
-        for k in range(1, at.chips):
+        for k in far:
             pass_z(k, h)
-    for h in range(pieces):
+    for h in range(min(lag, pieces)):
         pass_y(0, h)
     for h in range(pieces):
         pass_core(0, 0, h)
     for h in range(pieces):
-        for k in range(1, at.chips):
+        if h + lag < pieces:
+            pass_y(0, h + lag)
+        for k in far:
             came(block(k, 0, h), z_recv.at[h, k - 1])
             if h + ahead < pieces:
                 pass_z(k, h + ahead)
             pass_y(k, h)
             pass_core(k, 0, h)
-        if h:
-            take_y(h - 1)
-    take_y(pieces - 1)
+        if h >= lag:
+            take_y(h - lag)
+    for h in range(max(0, pieces - lag), pieces):
+        take_y(h)
     if at.cores > 1:
         came(all_ref.at[pl.ds(0, at.chips)], core_recv)
         left(all_ref.at[pl.ds(0, at.chips)], core_send)

time: 527 us -> 531 us (level)
  no operation moved by 1% of the time
where the time goes in v6:
time: 531 us; the launch traced here: 522 us
  Pallas kernels  519 us (98%)
    pallas_call x8, Pallas kernels, launch(): pl.pallas_call(kernel, out_shape=out_shapes, in_specs=[vmem_spec()] * len...  438 us
    pallas_call x1, Pallas kernels, gather_shards(): pl.pallas_call(partial(gather_kernel, geo, pieces), out_shape=pltpu.HBM((...  51.4 us
    pallas_call x1, Pallas kernels, expert_weights(): pl.pallas_call(partial(expert_weights_kernel, geo.experts_all), out_shape...  29.9 us

profile of v6, /device:TPU:0, one launch (start us, length us, event | category | flops | bytes accessed | tf_op | source)
XLA Modules:
  0.0 522.3 jit_solution(4285750949283443246)
XLA Ops:
  0.6 0.0 copy-start
  0.7 0.0 copy-start.1
  0.7 51.4 %shard_map.231 = bf16[8,2,48,3200]{3,2,1,0:T(8,128)(2,1)} custom-call(bf16[48,2304]{1,0:T(8,128)(2,1)} %bitcast.33, bf16[48,768]{1,0:T(8,128)(2,1)} %bitcast.40, bf16[32,48]{1,0:T(8,128)(2,1)} %bitcast.41, bf16[1,48]{1,0:T(2,128)(2,1)} %gain_one.1, bf16[1,48]{1,0:T(2,128)(2,1)} %gain_two.1, bf16[1,24]{1,0:T(2,128)(2,1)} %terms.1), custom_call_target="tpu_custom_call" | custom-call | tf_op jit(solution)/shard_map/pallas_call | solution.py:1285
  52.0 0.0 copy-done
  52.0 0.0 copy-done.1
  52.1 2.9 shard_map.232
  55.0 58.0 %shard_map.233 = (bf16[2,256,768]{2,1,0:T(8,128)(2,1)}, bf16[2,256,768]{2,1,0:T(8,128)(2,1)}, bf16[2,256,2304]{2,1,0:T(8,128)(2,1)}, bf16[2,12,256,256]{3,2,1,0:...) custom-call(s32[2,256]{1,0:T(2,128)} %refs_0_.7, ...), custom_call_target="tpu_custom_call" | custom-call | flops 6039797760 | bytes 18874368 | tf_op jit(solution)/shard_map/pallas_call | solution.py:141
  113.0 72.4 %shard_map.234 = (bf16[256,768]{1,0:T(8,128)(2,1)}, bf16[2,256,768]{2,1,0:T(8,128)(2,1)}, bf16[2,256,768]{2,1,0:T(8,128)(2,1)}, bf16[2,256,2304]{2,1,0:T(8,128)(...) custom-call(s32[2,256]{1,0:T(2,128)} %refs_0_.7, ...), custom_call_target="tpu_custom_call", output_to_operand_aliasing={{1}: (10, {}), {2}: (11, {}), {3}: (12, {}), {4}: (13, {}),... | custom-call | flops 6039797760 | bytes 18874368 | tf_op jit(solution)/shard_map/pallas_call | solution.py:141
  185.4 58.6 %shard_map.235 = (bf16[2,256,768]{2,1,0:T(8,128)(2,1)}, bf16[2,256,768]{2,1,0:T(8,128)(2,1)}, bf16[2,256,2304]{2,1,0:T(8,128)(2,1)}, bf16[2,12,256,256]{3,2,1,0:...) custom-call(s32[2,256]{1,0:T(2,128)} %refs_0_.7, ...), custom_call_target="tpu_custom_call", output_to_operand_aliasing={{0}: (11, {}), {1}: (12, {}), {2}: (13, {}), {3}: (14, {}),... | custom-call | flops 6039797760 | bytes 18874368 | tf_op jit(solution)/shard_map/pallas_call | solution.py:141
  244.0 58.0 %shard_map.236 = (bf16[256,768]{1,0:T(8,128)(2,1)}, f32[2,256,768]{2,1,0:T(8,128)}, bf16[2,256,768]{2,1,0:T(8,128)(2,1)}, bf16[2,256,2304]{2,1,0:T(8,128)(2,1)},...) custom-call(s32[1,2,2,256]{3,2,1,0:T(2,128)} %bitcast.37, ...), custom_call_target="tpu_custom_call" | custom-call | flops 6039797760 | bytes 18874368 | tf_op jit(solution)/shard_map/pallas_call | solution.py:141
  302.0 87.2 %shard_map.237 = (bf16[256,768]{1,0:T(8,128)(2,1)}, f32[2,256,768]{2,1,0:T(8,128)}, bf16[2,256,768]{2,1,0:T(8,128)(2,1)}, bf16[2,256,2304]{2,1,0:T(8,128)(2,1)},...) custom-call(s32[1,2,2,256]{3,2,1,0:T(2,128)} %bitcast.38, ...), custom_call_target="tpu_custom_call", output_to_operand_aliasing={{1}: (14, {}), {2}: (15, {}), {3}: (16, {}), {4}: (17, {}),... | custom-call | flops 6039797760 | bytes 18874368 | tf_op jit(solution)/shard_map/pallas_call | solution.py:141
  389.3 63.2 %shard_map.238 = (f32[2,256,768]{2,1,0:T(8,128)}, bf16[2,256,768]{2,1,0:T(8,128)(2,1)}, bf16[2,256,2304]{2,1,0:T(8,128)(2,1)}, bf16[2,256,128]{2,1,0:T(8,128)(2,...) custom-call(s32[1,2,2,256]{3,2,1,0:T(2,128)} %bitcast.39, ...), custom_call_target="tpu_custom_call", output_to_operand_aliasing={{0}: (14, {}), {1}: (15, {}), {2}: (16, {}), {3}: (17, {}),... | custom-call | flops 6039797760 | bytes 18874368 | tf_op jit(solution)/shard_map/pallas_call | solution.py:141
  452.5 37.3 %shard_map.239.packed = f32[48,3200]{1,0:T(8,128)S(1)} custom-call(f32[12,768]{1,0:T(8,128)S(1)} %copy-done.1, bf16[768,256]{1,0:T(8,128)(2,1)S(1)} %copy-done, bf16[2,256,768]{2,1,0:T(8,128)(2,1)} %get-tuple-element.146.refs_2_, bf16[2,256,2304]{2,1,0:T(8,128)(2,1)} %get-tuple-element.147.refs_3_, bf16[2,256,768]{2,1,0:T(8,128)(2,1)} %get-tuple-element.148.refs_4_, ...), custom_call_target="tpu_custom_call" | custom-call | flops 3000000000 | bytes 10000000 | tf_op jit(solution)/shard_map/pallas_call | solution.py:141
  489.8 0.0 copy-start.3
  489.9 0.0 copy-start.2
  489.9 29.9 %shard_map.240 = (f32[1,4,768,1536]{3,2,1,0:T(8,128)}, f32[1,4,1536,768]{3,2,1,0:T(8,128)}, f32[1,48,2304]{2,1,0:T(8,128)}, f32[1,48,768]{2,1,0:T(8,128)}, f32[1...) custom-call(bf16[2,4,320,768]{3,2,1,0:T(8,128)(2,1)} %get-tuple-element.142.rows, ...), custom_call_target="tpu_custom_call" | custom-call | flops 12079595520 | bytes 37748736 | tf_op jit(solution)/shard_map/pallas_call | solution.py:1432
  519.8 0.0 copy-done.3
  519.8 0.9 copy.112
  520.7 0.0 copy-done.2
  520.7 1.1 copy.113
Async XLA Ops:
  0.6 51.4 %copy-start = (bf16[768,256]{1,0:T(8,128)(2,1)S(1)}, bf16[768,256]{1,0:T(8,128)(2,1)}, u32[]{:S(2)}) copy-start(bf16[768,256]{1,0:T(8,128)(2,1)} %constant.7.clone.refs_1_) | copy-start | bytes 1179652
  0.7 51.4 %copy-start.1 = (f32[12,768]{1,0:T(8,128)S(1)}, f32[12,768]{1,0:T(8,128)}, u32[]{:S(2)}) copy-start(f32[12,768]{1,0:T(8,128)} %constant.6.clone.refs_0_) | copy-start | bytes 110596
  489.8 30.0 %copy-start.3 = (bf16[2,256,768]{2,1,0:T(8,128)(2,1)S(1)}, bf16[2,256,768]{2,1,0:T(8,128)(2,1)}, u32[]{:S(2)}) copy-start(bf16[2,256,768]{2,1,0:T(8,128)(2,1)} %get-tuple-element.115) | copy-start | bytes 2359300
  489.9 30.9 %copy-start.2 = (f32[2,256,768]{2,1,0:T(8,128)S(1)}, f32[2,256,768]{2,1,0:T(8,128)}, u32[]{:S(2)}) copy-start(f32[2,256,768]{2,1,0:T(8,128)} %get-tuple-element.141) | copy-start | bytes 4718596
